TPU v7x, 32 devices: a whole 2x2x4 slice. The times are simulated.
32 devices in a mesh: rows: 4 (over x, core), neur: 8 (over z, y).
Axes of the slice: x: 2, y: 2, z: 4, core: 2. Of those that a mesh axis runs over, the one named last changes fastest.
Arguments:
- tokens: bfloat16 [512, 12288], P('neur', 'rows'), may hold values from -6 to 6
- teacher_up: bfloat16 [12288, 49152], P('rows', 'neur'), may hold values from -0.0546875 to 0.0546875
- teacher_bias: float32 [49152], P('neur'), may hold values from -3 to 3
- predictor_down: bfloat16 [12288, 1024], P('rows', 'neur'), may hold values from -0.0546875 to 0.0546875
- predictor_up: bfloat16 [1024, 49152], P(None, ('neur', 'rows')), may hold values from -0.375 to 0.375
Outputs:
- teacher_relu: bfloat16 [512, 49152], P(None, ('neur', 'rows'))
- grad_down: float32 [12288, 1024], P('rows', 'neur')
- grad_up: float32 [1024, 49152], P(None, ('neur', 'rows'))
All inputs are finite; a program needn't handle non-finite values.
Results may differ from a plain program's by a relative error of at most 0.0047.
Values may be sent and summed in bfloat16 or wider, within the bound.
No kernel may reach another device: no remote copies, remote signals or barrier semaphores. Data moves between devices by JAX's collectives and lax.ppermute only.
A program may use at most 128 MiB of HBM per device.

v0:
```python
import jax
import jax.numpy as jnp
from jax import lax
from jax.sharding import PartitionSpec as P

loss_weight = 0.03125


def body(tokens, teacher_up, teacher_bias, predictor_down, predictor_up):
    gathered = lax.all_gather(tokens, "neur", axis=0, tiled=True)
    partial_value = jnp.dot(gathered, teacher_up, preferred_element_type=jnp.float32)
    preact = lax.psum_scatter(partial_value, "rows", scatter_dimension=1, tiled=True)
    width = preact.shape[1]
    bias_cols = lax.dynamic_slice_in_dim(teacher_bias, lax.axis_index("rows") * width, width, 0)
    preact = preact + bias_cols[None, :]
    teacher_relu = jnp.maximum(preact, 0.0).astype(jnp.bfloat16)
    target = jax.nn.sigmoid(preact)
    hidden_part = jnp.dot(gathered, predictor_down, preferred_element_type=jnp.float32)
    hidden_sum = lax.psum(hidden_part, "rows")
    hidden = lax.all_gather(hidden_sum.astype(jnp.bfloat16), "neur", axis=1, tiled=True)
    logits = jnp.dot(hidden, predictor_up, preferred_element_type=jnp.float32)
    residue = (loss_weight * (jax.nn.sigmoid(logits) - target)).astype(jnp.bfloat16)
    grad_up = jnp.einsum("tr,tf->rf", hidden, residue, preferred_element_type=jnp.float32)
    back_part = jnp.einsum("tf,rf->tr", residue, predictor_up, preferred_element_type=jnp.float32)
    rank_cols = predictor_down.shape[1]
    back_total = lax.psum(back_part, ("rows", "neur"))
    back_owned = lax.dynamic_slice_in_dim(
        back_total, lax.axis_index("neur") * rank_cols, rank_cols, 1
    )
    back = back_owned.astype(jnp.bfloat16)
    grad_down = jnp.einsum("td,tr->dr", gathered, back, preferred_element_type=jnp.float32)
    return (teacher_relu, grad_down, grad_up)


def solution(mesh):
    in_specs = (
        P("neur", "rows"),
        P("rows", "neur"),
        P("neur"),
        P("rows", "neur"),
        P(None, ("neur", "rows")),
    )
    out_specs = (P(None, ("neur", "rows")), P("rows", "neur"), P(None, ("neur", "rows")))
    return jax.shard_map(body, mesh=mesh, in_specs=in_specs, out_specs=out_specs, check_vma=False)
```

profile of v0, /device:TPU:0, one launch (start us, length us, event | category | flops | bytes accessed | tf_op | source)
XLA Modules:
  0.0 321.8 jit_solution(4014817436667375227)
XLA Ops:
  7.2 0.0 copy-start
  7.2 0.0 all-gather.3.cloned.1.call-start
  7.2 0.7 all-gather.3.cloned.1.call-update
  7.9 0.0 all-gather.5.cloned.1.call-start
  8.0 65.4 %all-gather.3.cloned.1.call-done = bf16[512,3072]{1,0:T(8,128)(2,1)} async-done(((bf16[64,3072]{1,0:T(8,128)(2,1)}), bf16[512,3072]{1,0:T(8,128)(2,1)}) %all-gather.3.cloned.1.call-update) | async-done | bytes 3145744 | tf_op jit(solution)/shard_map/all_gather | solution.py:10
  73.4 3.0 fusion.4
  76.4 13.5 %all-reduce.2 = bf16[512,128]{1,0:T(8,128)(2,1)} all-reduce(f32[512,128]{1,0:T(8,128)S(1)} %fusion.4), channel_id=1, replica_groups=mesh['rows'=4,'neur'=8] {'rows'}, use_global_device_ids=true, to_apply=%region_1.0 | all-reduce | flops 65536 | bytes 393216 | tf_op jit(solution)/shard_map/psum | solution.py:19
  90.0 0.0 all-gather.5.cloned.1.call-update
  90.0 0.0 reduce-scatter.2.cloned.1.call-start
  90.0 27.6 %fusion.3 = f32[512,6144]{1,0:T(8,128)} fusion(bf16[512,3072]{1,0:T(8,128)(2,1)} %all-gather.3.cloned.1.call-done, bf16[3072,6144]{1,0:T(8,128)(2,1)} %param.6), kind=kOutput, calls=%fused_computation.8 | convolution fusion | flops 19327352832 | bytes 53477376 | tf_op jit(solution)/shard_map/dot_general | solution.py:11
  117.6 0.0 reduce-scatter.2.cloned.1.call-update
  117.6 0.8 dynamic_slice.6
  118.4 10.9 %all-gather.5.cloned.1.call-done = bf16[512,1024]{1,0:T(8,128)(2,1)} async-done(((bf16[512,128]{1,0:T(8,128)(2,1)}), bf16[512,1024]{1,0:T(8,128)(2,1)}) %all-gather.5.cloned.1.call-update) | async-done | bytes 1048592 | tf_op jit(solution)/shard_map/all_gather | solution.py:20
  129.3 100.6 %reduce-scatter.2.cloned.1.call-done = f32[512,1536]{1,0:T(8,128)} async-done(((f32[512,6144]{1,0:T(8,128)}), f32[512,1536]{1,0:T(8,128)}) %reduce-scatter.2.cloned.1.call-update) | async-done | bytes 3145744 | tf_op jit(solution)/shard_map/reduce_scatter | solution.py:12
  229.9 0.0 copy-done
  229.9 5.0 %multiply_convert_fusion = bf16[512,1536]{1,0:T(8,128)(2,1)S(1)} fusion(bf16[512,1024]{1,0:T(8,128)(2,1)} %all-gather.5.cloned.1.call-done, bf16[1024,1536]{1,0:T(8,128)(2,1)S(1)} %copy-done, f32[512,1536]{1,0:T(8,128)} %reduce-scatter.2.cloned.1.call-done, f32[1536]{0:T(1024)S(1)} %dynamic_slice.6), kind=kOutput, calls=%fused_computation.4 | convolution fusion | flops 1618477056 | bytes 8919040 | tf_op jit(solution)/shard_map/dot_general | solution.py:21
  234.9 0.0 copy-start.2
  234.9 1.2 copy-done.2
  236.1 3.2 fusion.5
  239.2 61.2 %all-reduce.3 = bf16[512,1024]{1,0:T(8,128)(2,1)} all-reduce(f32[512,1024]{1,0:T(8,128)} %fusion.5), channel_id=1, replica_groups=mesh['rows'=4,'neur'=8] {'rows','neur'}, use_global_device_ids=true, to_apply=%region_2.0 | all-reduce | flops 524288 | bytes 3145728 | tf_op jit(solution)/shard_map/psum | solution.py:26
  300.4 3.7 %convolution_bitcast_fusion = f32[3072,128]{0,1:T(8,128)} fusion(bf16[512,3072]{1,0:T(8,128)(2,1)} %all-gather.3.cloned.1.call-done, bf16[512,1024]{1,0:T(8,128)(2,1)} %all-reduce.3, s32[]{:T(128)S(6)} %select_n.7), kind=kOutput, calls=%fused_computation | convolution fusion | flops 402653184 | bytes 4849668 | tf_op jit(solution)/shard_map/td,tr->dr/dot_general | solution.py:31
  304.1 3.0 copy.8
  307.2 3.5 %maximum_convert_fusion = bf16[512,1536]{1,0:T(8,128)(2,1)} fusion(f32[512,1536]{1,0:T(8,128)} %reduce-scatter.2.cloned.1.call-done, f32[1536]{0:T(1024)S(1)} %dynamic_slice.6), kind=kLoop, calls=%fused_computation.5 | loop fusion | flops 2359296 | bytes 4724736 | tf_op jit(solution)/shard_map/convert_element_type | solution.py:16
  310.7 4.5 %fusion.6 = f32[1024,1536]{1,0:T(8,128)} fusion(bf16[512,1024]{1,0:T(8,128)(2,1)S(1)} %copy-done.1, bf16[512,1536]{1,0:T(8,128)(2,1)S(1)} %copy-done.3), kind=kOutput, calls=%fused_computation.11 | convolution fusion | flops 1610612736 | bytes 8912896 | tf_op jit(solution)/shard_map/tr,tf->rf/dot_general | solution.py:23
  (4 shorter events, 0.0 us)
Async XLA Ops:
  7.2 222.7 %copy-start = (bf16[1024,1536]{1,0:T(8,128)(2,1)S(1)}, bf16[1024,1536]{1,0:T(8,128)(2,1)}, u32[]{:S(2)}) copy-start(bf16[1024,1536]{1,0:T(8,128)(2,1)} %param.9) | copy-start | bytes 9437188
  7.2 66.2 %all-gather.3.cloned.1.call-start = ((), (), s32[]{:S(2)}) async-start(), calls=%async_computation.1 | async-start | bytes 3538944 | tf_op jit(solution)/shard_map/all_gather | solution.py:10
  7.9 121.4 %all-gather.5.cloned.1.call-start = ((), (), s32[]{:S(2)}) async-start(), calls=%async_computation.3 | async-start | bytes 1179648 | tf_op jit(solution)/shard_map/all_gather | solution.py:20
  90.0 139.9 %reduce-scatter.2.cloned.1.call-start = ((), (), s32[]{:S(2)}) async-start(), calls=%async_computation.2 | async-start | bytes 15728640 | tf_op jit(solution)/shard_map/reduce_scatter | solution.py:12
  234.9 1.2 copy-start.2
  307.2 3.5 %copy-start.1 = (bf16[512,1024]{1,0:T(8,128)(2,1)S(1)}, bf16[512,1024]{1,0:T(8,128)(2,1)}, u32[]{:S(2)}) copy-start(bf16[512,1024]{1,0:T(8,128)(2,1)} %all-gather.5.cloned.1.call-done) | copy-start | bytes 3145732
  307.2 3.5 %copy-start.3 = (bf16[512,1536]{1,0:T(8,128)(2,1)S(1)}, bf16[512,1536]{1,0:T(8,128)(2,1)}, u32[]{:S(2)}) copy-start(bf16[512,1536]{1,0:T(8,128)(2,1)} %copy-done.2) | copy-start | bytes 4718596
Sparse Core Ops, SparseCore 0:
  10.2 63.1 all-gather.2
  90.1 39.1 all-gather.4
  131.9 97.9 reduce-scatter.1
where the time goes:
time: 322 us
  waiting for transfers between devices  178 us (55%)
  blocking collectives  74.7 us (23%)
  matrix products  47 us (15%)
  between operations  13.8 us (4%)
  local copies, waits for them, and re-layouts  4.98 us (2%)
  other arithmetic  3.54 us (1%)
    reduce_scatter x1, waiting for transfers between devices, body(): lax.psum_scatter(partial_value, 'rows', scatter_dimension=1, tiled=True)  101 us
    all_gather x1, waiting for transfers between devices, body(): gathered = lax.all_gather(tokens, 'neur', axis=0, tiled=True)  65.4 us
    psum x1, blocking collectives, body(): back_total = lax.psum(back_part, ('rows', 'neur'))  61.2 us
    dot_general x1, matrix products, body(): jnp.dot(gathered, teacher_up, preferred_element_type=jnp.float32)  27.6 us
    psum x1, blocking collectives, body(): hidden_sum = lax.psum(hidden_part, 'rows')  13.5 us
    all_gather x1, waiting for transfers between devices, body(): lax.all_gather(hidden_sum.astype(jnp.bfloat16), 'neur', axis=1, tiled=True)  10.9 us
  transfers between devices with their start and end apart: 3, of which 3 were waited for; matrix products, arithmetic and copies ran while one was open for 9% of the time, Pallas kernels for 0%

commit v1 on v0

v1 whole, which is shorter than its diff:
```python
import jax
import jax.numpy as jnp
from jax import lax
from jax.experimental import pallas as pl
from jax.experimental.pallas import tpu as pltpu
from jax.sharding import PartitionSpec as P

loss_weight = 0.03125
bf16 = jnp.bfloat16
f32 = jnp.float32


def flip(value, axis, size, distance):
    return lax.ppermute(value, axis, [(i, i ^ distance) for i in range(size)])


def block(value, index, width, axis):
    return lax.dynamic_slice_in_dim(value, index * width, width, axis)


def gather_line(own, lines, size, place):
    def pairs(moves):
        return [(a * lines + y, b * lines + y) for a, b in moves for y in range(lines)]

    edge = (place == 0) | (place == 3)
    middle = pairs([(1, 2), (2, 1)])
    outward = pairs([(1, 0), (2, 3)])
    near = flip(own, "neur", size, lines)
    across = lax.ppermute(own, "neur", middle)
    far = lax.ppermute(near, "neur", middle)
    second = jnp.where(edge, lax.ppermute(across, "neur", outward), far)
    third = jnp.where(edge, lax.ppermute(far, "neur", outward), across)
    return [own, near, second, third]


def general_body(n_rows, n_neur):
    lines = 1
    while lines * lines * 4 <= n_neur:
        lines *= 2
    places = n_neur // lines
    pairs_x = n_rows // 2

    def body(tokens, teacher_up, teacher_bias, predictor_down, predictor_up):
        row = lax.axis_index("rows")
        core, x = row % 2, row // 2
        neur = lax.axis_index("neur")
        place, line = neur // lines, neur % lines
        t = tokens.shape[0]
        half_rows = t * n_neur // 2
        width = teacher_up.shape[1] // n_rows
        rank = predictor_down.shape[1]
        ranks = predictor_up.shape[0]

        if places == 4:
            column = gather_line(tokens, lines, n_neur, place)
        else:
            column = [tokens] + [flip(tokens, "neur", n_neur, d * lines) for d in range(1, places)]
        shards = []
        for shard in column:
            shards.append(shard)
            for d in range(1, lines):
                shards.append(flip(shard, "neur", n_neur, d))
        half = n_neur // 2
        within = neur % half
        side = neur // half

        def ordered(parts):
            whole = jnp.zeros((half_rows, tokens.shape[1]), bf16)
            for s, part in enumerate(parts):
                whole = lax.dynamic_update_slice_in_dim(whole, part, (within ^ s) * t, 0)
            return whole

        near_rows = ordered(shards[:half])
        far_rows = ordered(shards[half:])

        def in_order(near, far):
            return jnp.where(side == 0, jnp.concatenate([near, far]), jnp.concatenate([far, near]))

        gathered = in_order(near_rows, far_rows)

        hidden_part = jnp.dot(gathered, predictor_down, preferred_element_type=f32)
        mine = block(hidden_part, core, half_rows, 0)
        mine = mine + flip(block(hidden_part, 1 - core, half_rows, 0), "rows", n_rows, 1)
        step = 2
        while step < n_rows:
            mine = mine + flip(mine, "rows", n_rows, step)
            step *= 2
        mine = mine.astype(bf16)
        column = [mine] + [flip(mine, "neur", n_neur, d * lines) for d in range(1, places)]
        stack = jnp.stack(column)
        stacks = [stack] + [flip(stack, "neur", n_neur, e) for e in range(1, lines)]
        blocks = [stacks[d % lines][d // lines] for d in range(n_neur)]
        hidden_half = jnp.zeros((half_rows, ranks), bf16)
        for d, part in enumerate(blocks):
            hidden_half = lax.dynamic_update_slice_in_dim(hidden_half, part, (neur ^ d) * rank, 1)
        other = flip(hidden_half, "rows", n_rows, 1)
        hidden = jnp.where(
            core == 0,
            jnp.concatenate([hidden_half, other]),
            jnp.concatenate([other, hidden_half]),
        )

        bias_cols = block(teacher_bias, row, width, 0)

        def preactivation(part):
            value = jnp.dot(part, teacher_up, preferred_element_type=f32)
            value = value.reshape(part.shape[0], pairs_x, 2, width)
            keep = lax.dynamic_index_in_dim(value, core, 2, keepdims=False)
            send = lax.dynamic_index_in_dim(value, 1 - core, 2, keepdims=False)
            chip = keep + flip(send.astype(bf16), "rows", n_rows, 1)
            total = lax.dynamic_index_in_dim(chip, x, 1, keepdims=False)
            for d in range(1, pairs_x):
                away = lax.dynamic_index_in_dim(chip, x ^ d, 1, keepdims=False)
                total = total + flip(away.astype(bf16), "rows", n_rows, 2 * d)
            return total + bias_cols[None, :]

        preact = in_order(preactivation(near_rows), preactivation(far_rows))
        teacher_relu = jnp.maximum(preact, 0.0).astype(bf16)
        target = jax.nn.sigmoid(preact)
        logits = jnp.dot(hidden, predictor_up, preferred_element_type=f32)
        residue = (loss_weight * (jax.nn.sigmoid(logits) - target)).astype(bf16)
        grad_up = jnp.einsum("tr,tf->rf", hidden, residue, preferred_element_type=f32)

        back_part = jnp.einsum("tf,rf->tr", residue, predictor_up, preferred_element_type=f32)
        total = block(back_part, core, half_rows, 0)
        total = total + flip(block(back_part, 1 - core, half_rows, 0), "rows", n_rows, 1)
        total = total.reshape(half_rows, places, lines, rank)
        kept = lax.dynamic_index_in_dim(total, line, 2, keepdims=False)
        for e in range(1, lines):
            away = lax.dynamic_index_in_dim(total, line ^ e, 2, keepdims=False)
            kept = kept + flip(away.astype(bf16), "neur", n_neur, e)
        back = lax.dynamic_index_in_dim(kept, place, 1, keepdims=False)
        for d in range(1, places):
            away = lax.dynamic_index_in_dim(kept, place ^ d, 1, keepdims=False)
            back = back + flip(away.astype(bf16), "neur", n_neur, d * lines)
        step = 2
        while step < n_rows:
            back = back + flip(back, "rows", n_rows, step)
            step *= 2
        back = back.astype(bf16)
        other = flip(back, "rows", n_rows, 1)
        back = jnp.where(
            core == 0, jnp.concatenate([back, other]), jnp.concatenate([other, back])
        )
        grad_down = jnp.einsum("td,tr->dr", gathered, back, preferred_element_type=f32)
        return (teacher_relu, grad_down, grad_up)

    return body


def spot(space=pltpu.VMEM):
    return pl.BlockSpec(memory_space=space)


def shape_of(shape, dtype):
    return jax.ShapeDtypeStruct(shape, dtype)


def call(kernel, outs, ins, spaces, scratch=(), mib=12, after=(), through=(), weight=1, aliases=None, out_spaces=None):
    outs = list(outs)
    out_spaces = list(out_spaces or [pltpu.VMEM] * len(outs))
    passed = list(through)
    n_in, n_out = len(ins), len(outs)

    def body(*refs):
        end = n_in + len(passed) + len(after)
        kernel(*refs[:n_in], *refs[end : end + n_out], *refs[end + n_out + len(passed) :])

    places = [pl.ANY] * len(through)
    outs += [shape_of(value.shape, value.dtype) for value in through]
    aliased = dict(aliases or {})
    aliased.update({n_in + k: n_out + k for k in range(len(passed))})
    results = pl.pallas_call(
        body,
        out_shape=tuple(outs),
        in_specs=[spot(space) for space in list(spaces) + places + [pl.ANY] * len(after)],
        out_specs=tuple(spot(space) for space in out_spaces + places),
        scratch_shapes=list(scratch),
        input_output_aliases=aliased,
        compiler_params=pltpu.CompilerParams(vmem_limit_bytes=mib * 2**20),
        cost_estimate=pl.CostEstimate(flops=weight * 4000000000 if weight == 1 else 10**10, bytes_accessed=1000, transcendentals=0),
    )(*ins, *through, *after)
    return results


def tile_of(width):
    for tile in (512, 384, 256, 128):
        if width % tile == 0:
            return tile
    return width


def held(value):
    return pltpu.with_memory_space_constraint(value, pltpu.VMEM)


def bias_part(row, bias, width, **order):
    def kernel(row_ref, bias_ref, cols_ref):
        cols_ref[...] = bias_ref[:, pl.ds(pl.multiple_of(row_ref[0] * width, 128), width)]

    return call(
        kernel,
        [shape_of((1, width), f32)],
        [row, bias.reshape(1, bias.shape[0])],
        [pltpu.SMEM, pltpu.VMEM],
        **order,
    )


def hold(*values, **order):
    def kernel(out_ref):
        out_ref[...] = jnp.zeros_like(out_ref)

    return call(kernel, [shape_of((8, 128), f32)], [], [], through=values, **order)


def joined(refs, cols=slice(None)):
    return jnp.concatenate([ref[:, cols] for ref in refs]) if len(refs) > 1 else refs[0][:, cols]


def partial_sums(row, parts, weight, width, blocks, dtype, gots=(), plus=(), cost=1, **order):
    rows = sum(part.shape[0] for part in parts)
    depth = weight.shape[0]
    tile = tile_of(width)
    per = width // tile
    tiles = len(blocks) * per
    slots = min(tiles, 3)
    extra = [value for pair in plus for value in pair]
    heights = [pair[0].shape[0] for pair in plus]
    ins = [row, *parts, *gots, *extra, weight]

    def kernel(*refs):
        row_ref, part_refs = refs[0], refs[1 : 1 + len(parts)]
        got_refs = refs[1 + len(parts) : 1 + len(parts) + len(gots)]
        weight_ref = refs[len(ins) - 1]
        outs, (buffer, sems) = refs[len(ins) : -2], refs[-2:]
        x, core = row_ref[0] // 2, row_ref[0] % 2

        def copy(j):
            distance, keep = blocks[j // per]
            whose = (x ^ distance) * 2 + (core if keep else 1 - core)
            from_cols = pl.ds(pl.multiple_of(whose * width + (j % per) * tile, 128), tile)
            return pltpu.make_async_copy(weight_ref.at[:, from_cols], buffer.at[j % slots], sems.at[j % slots])

        for j in range(slots):
            copy(j).start()
        first = 0
        for i, height in enumerate(heights):
            a_ref, b_ref = refs[len(ins) - 1 - len(extra) + 2 * i : len(ins) + 1 - len(extra) + 2 * i]
            outs[-1][first : first + height, :] = a_ref[...] + b_ref[...]
            first += height
        part = joined(part_refs)
        for j in range(tiles):
            copy(j).wait()
            cols = slice(j % per * tile, (j % per + 1) * tile)
            value = jnp.dot(part, buffer[j % slots], preferred_element_type=f32)
            if gots:
                value = value + got_refs[j // per][:, cols].astype(f32)
            outs[j // per][:, cols] = value.astype(dtype)
            if j + slots < tiles:
                copy(j + slots).start()

    sums = [shape_of((sum(heights), extra[0].shape[1]), f32)] if extra else []
    return call(
        kernel,
        [shape_of((rows, width), dtype) for _ in blocks] + sums,
        ins,
        [pltpu.SMEM] + [pltpu.VMEM] * (len(ins) - 2) + [pl.ANY],
        scratch=[pltpu.VMEM((slots, depth, tile), bf16), pltpu.SemaphoreType.DMA((slots,))],
        mib=24,
        weight=cost,
        **order,
    )


def add_all(dtype, *groups, **order):
    rows = [group[0].shape[0] for group in groups]

    def kernel(*refs):
        out_ref, at, first = refs[-1], 0, 0
        for group, size in zip(groups, rows):
            value = refs[at][...]
            for k in range(1, len(group)):
                value = value + refs[at + k][...]
            out_ref[first : first + size, :] = value.astype(dtype)
            at, first = at + len(group), first + size

    ins = [value for group in groups for value in group]
    out = shape_of((sum(rows), groups[0][0].shape[1]), dtype)
    return call(kernel, [out], ins, [pltpu.VMEM] * len(ins), **order)


def stacked(values, **order):
    def kernel(*refs):
        for k, ref in enumerate(refs[:-1]):
            refs[-1][k] = ref[...]

    out = shape_of((len(values),) + values[0].shape, values[0].dtype)
    return call(kernel, [out], values, [pltpu.VMEM] * len(values), **order)


def finish_preact(neur, bias, chunks, t, n_neur, width, before=None, **order):
    orders = [rows_of for rows_of, _, _ in chunks]
    ins = [neur, bias]
    for _, own, got in chunks:
        ins += [own] + list(got)
    counts = [len(got) for _, _, got in chunks]
    aliases = {}
    spaces = [pltpu.SMEM] + [pltpu.VMEM] * (len(ins) - 1)
    if before is not None:
        aliases = {len(ins): 0, len(ins) + 1: 1}
        ins += [before[0], before[1]]
        spaces += [pl.ANY, pltpu.VMEM]
    pieces = sum(len(rows_of) for rows_of in orders)

    def kernel(*refs):
        neur_ref, bias_ref = refs[:2]
        relu_ref, target_ref, relu, sems = refs[-4:]
        at, piece, copies = 2, 0, []
        for rows_of, count in zip(orders, counts):
            own_ref, got_refs = refs[at], refs[at + 1 : at + 1 + count]
            at += 1 + count
            for i, s in enumerate(rows_of):
                rows = pl.ds(pl.multiple_of((neur_ref[0] ^ s) * t, t), t)
                here = slice(i * t, (i + 1) * t)
                value = own_ref[here, :] + bias_ref[...]
                for got_ref in got_refs:
                    value = value + got_ref[here, :].astype(f32)
                relu[piece] = jnp.maximum(value, 0.0).astype(bf16)
                copies.append(pltpu.make_async_copy(relu.at[piece], relu_ref.at[rows, :], sems.at[piece]))
                copies[-1].start()
                target_ref[rows, :] = jax.nn.sigmoid(value)
                piece += 1
        for copy in copies:
            copy.wait()

    return call(
        kernel,
        [shape_of((n_neur * t, width), bf16), shape_of((n_neur * t, width), f32)],
        ins,
        spaces,
        scratch=[pltpu.VMEM((pieces, t, width), bf16), pltpu.SemaphoreType.DMA((pieces,))],
        aliases=aliases,
        out_spaces=[pl.ANY, pltpu.VMEM],
        **order,
    )


def hidden_sums(row, shards, down, orders, pairs, t, **order):
    rank = down.shape[1]
    listed = [s for rows_of in orders for s in rows_of]

    def kernel(row_ref, down_ref, *refs):
        keep_ref, send_ref = refs[-2:]
        sums = jnp.dot(joined(refs[: len(listed)]), down_ref[...], preferred_element_type=f32)
        value = {s: sums[i * t : (i + 1) * t, :] for i, s in enumerate(listed)}
        first = row_ref[0] % 2 == 0
        for i, (a, b) in enumerate(pairs):
            keep_ref[i * t : (i + 1) * t, :] = jnp.where(first, value[a], value[b])
            send_ref[i * t : (i + 1) * t, :] = jnp.where(first, value[b], value[a])

    out = shape_of((len(pairs) * t, rank), f32)
    ins = [row, down] + [shards[s] for s in listed]
    return call(kernel, [out, out], ins, [pltpu.SMEM] + [pltpu.VMEM] * (len(ins) - 1), **order)


def assemble_hidden(at, groups, places, lines, t, rank, **order):
    ins, layout = [at], []
    for pairs, mine, theirs in groups:
        for ours, stacks in ((True, mine), (False, theirs)):
            layout.append((pairs, ours, len(ins)))
            ins += stacks
    n_neur = places * lines

    def kernel(*refs):
        at_ref, out_ref = refs[0], refs[-1]
        core, neur = at_ref[0], at_ref[1]
        for pairs, ours, first in layout:
            which = core if ours else 1 - core
            for e in range(lines):
                for d in range(places):
                    owner = neur ^ (d * lines + e)
                    cols = pl.ds(pl.multiple_of(owner * rank, 128), rank)
                    for i, (a, b) in enumerate(pairs):
                        shard = owner ^ (a ^ (which * (a ^ b)))
                        rows = pl.ds(pl.multiple_of(shard * t, t), t)
                        out_ref[rows, cols] = refs[first + e][d, i * t : (i + 1) * t, :]

    return call(
        kernel, [shape_of((n_neur * t, n_neur * rank), bf16)], ins, [pltpu.SMEM] + [pltpu.VMEM] * (len(ins) - 1), **order
    )


def residue_and_back(at, hidden, target, up, places, lines, half_rows, rank, dtype, **order):
    ranks, width = up.shape
    tile = tile_of(width)

    def kernel(at_ref, hidden_ref, target_ref, up_ref, residue_ref, back_ref, total):
        half, neur = at_ref[0], at_ref[1]
        rows = pl.ds(pl.multiple_of(half * half_rows, half_rows), half_rows)
        for k in range(width // tile):
            cols = slice(k * tile, (k + 1) * tile)
            logits = jnp.dot(hidden_ref[rows, :], up_ref[:, cols], preferred_element_type=f32)
            residue = (loss_weight * (jax.nn.sigmoid(logits) - target_ref[rows, cols])).astype(bf16)
            residue_ref[:, cols] = residue
            term = lax.dot_general(
                residue, up_ref[:, cols], (((1,), (1,)), ((), ())), preferred_element_type=f32
            )
            total[...] = term if k == 0 else total[...] + term
        for j in range(places * lines):
            d = neur ^ j
            back_ref[(d % lines) * places + d // lines] = total[:, j * rank : (j + 1) * rank].astype(dtype)

    return call(
        kernel,
        [shape_of((half_rows, width), bf16), shape_of((places * lines, half_rows, rank), dtype)],
        [at, hidden, target, up],
        [pltpu.SMEM, pltpu.VMEM, pltpu.VMEM, pltpu.VMEM],
        scratch=[pltpu.VMEM((half_rows, ranks), f32)],
        mib=24,
        **order,
    )


def add_lines(total, gots, places, **order):
    _, half_rows, rank = total.shape

    def kernel(total_ref, *refs):
        own_ref, away_ref = refs[-2:]
        for d in range(places):
            value = total_ref[d]
            for got_ref in refs[:-2]:
                value = value + got_ref[d].astype(f32)
            if d == 0:
                own_ref[...] = value
            else:
                away_ref[d - 1] = value.astype(bf16)

    return call(
        kernel,
        [shape_of((half_rows, rank), f32), shape_of((places - 1, half_rows, rank), bf16)],
        [total, *gots],
        [pltpu.VMEM] * (1 + len(gots)),
        **order,
    )


def down_gradient(at, shards, mine, theirs, t):
    count = len(shards)
    rows, depth = count * t, shards[0].shape[1]
    half_rows, rank = mine.shape
    tile = tile_of(depth)

    def kernel(at_ref, mine_ref, theirs_ref, *refs):
        out_ref, back, placed = refs[-3:]
        core, neur = at_ref[0], at_ref[1]
        back[pl.ds(pl.multiple_of(core * half_rows, half_rows), half_rows), :] = mine_ref[...].astype(f32)
        back[pl.ds(pl.multiple_of((1 - core) * half_rows, half_rows), half_rows), :] = theirs_ref[...].astype(f32)
        for s in range(count):
            placed[s * t : (s + 1) * t, :] = back[pl.ds(pl.multiple_of((neur ^ s) * t, t), t), :]
        turned = placed[...].T.astype(bf16)
        for k in range(depth // tile):
            cols = slice(k * tile, (k + 1) * tile)
            whole = joined(refs[:count], cols)
            out_ref[cols, :] = jnp.dot(turned, whole, preferred_element_type=f32).T

    return call(
        kernel,
        [shape_of((depth, rank), f32)],
        [at, mine, theirs, *shards],
        [pltpu.SMEM] + [pltpu.VMEM] * (2 + count),
        scratch=[pltpu.VMEM((rows, rank), f32), pltpu.VMEM((rows, rank), f32)],
        mib=16,
    )[0]


def tuned_body(n_rows, n_neur, lines):
    places = n_neur // lines
    pairs_x = n_rows // 2

    def body(tokens, teacher_up, teacher_bias, predictor_down, predictor_up):
        row = lax.axis_index("rows")
        core = row % 2
        neur = lax.axis_index("neur")
        t = tokens.shape[0]
        half_rows = t * n_neur // 2
        width = teacher_up.shape[1] // n_rows
        rank = predictor_down.shape[1]
        row_at = jnp.reshape(row, (1,)).astype(jnp.int32)
        neur_at = jnp.reshape(neur, (1,)).astype(jnp.int32)
        mine_at = jnp.stack([core, neur]).astype(jnp.int32)
        other_at = jnp.stack([1 - core, neur]).astype(jnp.int32)

        def to_core(value):
            return flip(value, "rows", n_rows, 1)

        shards = {}

        orders = [
            [s for s in range(lines)],
            [s for s in range(lines, 2 * lines)] + [d * lines for d in range(2, places)],
            [s for s in range(2 * lines, n_neur) if s % lines],
        ]
        away = list(range(1, pairs_x))
        owns, arrived, got = {}, {}, {}
        (bias_cols,) = bias_part(row_at, teacher_bias, width, after=(neur_at, mine_at, other_at))
        gate = (bias_cols,)

        def sums(chunk, distances, keep, cost=1, through=(), plus=()):
            nonlocal gate
            out = partial_sums(
                row_at,
                [shards[s] for s in orders[chunk]],
                teacher_up,
                width,
                [(d, keep) for d in distances],
                f32 if keep and distances == [0] else bf16,
                gots=[got[chunk, d] for d in distances] if keep else (),
                plus=plus,
                cost=cost,
                after=gate,
                through=through,
            )
            gate = (out[0],)
            for d, part in zip(distances, out):
                if not keep:
                    got[chunk, d] = to_core(part)
                elif d == 0:
                    owns[chunk] = part
                else:
                    arrived.setdefault(chunk, []).append(flip(part, "rows", n_rows, 2 * d))
            return out[len(distances) :]

        def pin(*values):
            nonlocal gate
            token, *values = hold(*values, after=gate)
            gate = (token,)
            return values

        def finish(chunks, before=None, through=()):
            nonlocal gate
            relu, target, *passed = finish_preact(
                neur_at,
                bias_cols,
                [(orders[c], owns[c], arrived[c]) for c in chunks],
                t,
                n_neur,
                width,
                before,
                after=gate,
                through=through,
            )
            gate = (target,)
            return (relu, target), passed

        def hidden_part(chunks):
            nonlocal gate
            pairs = [(orders[c][k], orders[c][k + 1]) for c in chunks for k in range(0, len(orders[c]), 2)]
            keep, send = hidden_sums(
                row_at, shards, predictor_down, [orders[c] for c in chunks], pairs, t, after=gate
            )
            gate = (keep,)
            return keep, send, pairs

        def along_y(d):
            for e in range(1, lines):
                shards[d * lines + e] = flip(shards[d * lines], "neur", n_neur, e)

        first_cost = 10**7
        for d in range(places):
            shards[d * lines] = tokens if d == 0 else flip(tokens, "neur", n_neur, d * lines)
        along_y(0)
        sums(0, away, False, first_cost)
        sums(0, [0], False, first_cost)
        (shards[lines],) = pin(shards[lines])
        along_y(1)
        sums(0, away, True, first_cost)
        sums(0, [0], True, first_cost)
        rest = [d * lines for d in range(2, places)]
        for s, shard in zip(rest, pin(*[shards[s] for s in rest])):
            shards[s] = shard
        for d in range(2, places):
            along_y(d)
        early_keep, early_send, early_pairs = hidden_part([0, 1])
        early_got = to_core(early_send)
        done, _ = finish([0])
        sums(1, away, False)
        sums(1, [0], False)
        sums(1, away, True)
        late_keep, late_send, late_pairs = hidden_part([2])
        late_got = to_core(late_send)
        sums(1, [0], True)
        (mine,) = add_all(f32, (early_keep, early_got), (late_keep, late_got), after=gate)
        gate = (mine,)
        moved = flip(mine, "rows", n_rows, 2)
        sums(2, away, False)
        sums(2, [0], False)
        (moved,) = pin(moved)
        step = 4
        while step < n_rows:
            (mine,) = add_all(f32, (mine, moved))
            moved = flip(mine, "rows", n_rows, step)
            step *= 2
        (mine,) = add_all(bf16, (mine, moved))
        column = [mine] + [flip(mine, "neur", n_neur, d * lines) for d in range(1, places)]
        sums(2, away, True)
        column = pin(*column)
        (stack,) = stacked(column)
        stacks = [stack] + [flip(stack, "neur", n_neur, e) for e in range(1, lines)]
        others = [to_core(part) for part in stacks]
        sums(2, [0], True, through=())
        done, _ = finish([1], done)
        (teacher_relu, target), _ = finish([2], done)
        (hidden,) = assemble_hidden(
            mine_at, [(early_pairs + late_pairs, stacks, others)], places, lines, t, rank, after=gate
        )

        def half_of(at, dtype, after):
            return residue_and_back(
                at, hidden, target, predictor_up, places, lines, half_rows, rank, dtype, after=after
            )

        residue_other, send = half_of(other_at, bf16, ())
        residue_mine, kept_back = half_of(mine_at, f32, (send,))
        total = kept_back + to_core(send)
        gots = [
            flip(total[e * places : (e + 1) * places].astype(bf16), "neur", n_neur, e) for e in range(1, lines)
        ]
        swap = core == 0
        residue = jnp.concatenate(
            [jnp.where(swap, residue_mine, residue_other), jnp.where(swap, residue_other, residue_mine)]
        )
        grad_up = jnp.einsum("tr,tf->rf", hidden, residue, preferred_element_type=f32)
        back, away = add_lines(total[:places], gots, places, after=(grad_up,))
        for d in range(1, places):
            back = back + flip(away[d - 1], "neur", n_neur, d * lines)
        step = 2
        while step < n_rows:
            back = back + flip(back, "rows", n_rows, step)
            step *= 2
        back = back.astype(bf16)
        grad_down = down_gradient(mine_at, [shards[s] for s in range(n_neur)], back, to_core(back), t)
        return (teacher_relu, grad_down, grad_up)

    return body


def solution(mesh):
    in_specs = (
        P("neur", "rows"),
        P("rows", "neur"),
        P("neur"),
        P("rows", "neur"),
        P(None, ("neur", "rows")),
    )
    out_specs = (P(None, ("neur", "rows")), P("rows", "neur"), P(None, ("neur", "rows")))
    n_rows, n_neur = mesh.shape["rows"], mesh.shape["neur"]
    lines = 1
    while lines * lines * 4 <= n_neur:
        lines *= 2
    tuned = tuned_body(n_rows, n_neur, lines)
    general = general_body(n_rows, n_neur)

    def body(tokens, teacher_up, teacher_bias, predictor_down, predictor_up):
        blocks = (teacher_up.shape[1] // n_rows, predictor_down.shape[1], predictor_up.shape[1])
        fits = all(size % 128 == 0 for size in blocks) and tokens.shape[0] % 16 == 0
        small = teacher_up.size * teacher_up.dtype.itemsize <= 40 * 2**20
        chosen = tuned if fits and small else general
        return chosen(tokens, teacher_up, teacher_bias, predictor_down, predictor_up)

    return jax.shard_map(body, mesh=mesh, in_specs=in_specs, out_specs=out_specs, check_vma=False)
```

time: 322 us -> 163 us (0.51)
  waiting for transfers between devices: 178 us -> 42.2 us
  Pallas kernels: 0 us -> 82.1 us
  blocking collectives: 74.7 us -> 0 us
  matrix products: 47 us -> 1.83 us
  starting transfers between devices: 0.12 us -> 29.9 us
  between operations: 13.8 us -> 1.19 us
  other arithmetic: 3.54 us -> 0.32 us
    reduce_scatter x1 -> x0, waiting for transfers between devices: 101 us -> none  [body(): lax.psum_scatter(partial_value, 'rows', scatter_dimension=1, tiled=True)]
    pallas_call x0 -> x30, Pallas kernels: none -> 82.1 us  [call(): pl.pallas_call(body, out_shape=tuple(outs), in_specs=[spot(space) for spa...]
    all_gather x2 -> x0, waiting for transfers between devices: 76.3 us -> none  [the longest x1 65.4 us: body(): gathered = lax.all_gather(tokens, 'neur', axis=0, tiled=True)]
    psum x2 -> x0, blocking collectives: 74.7 us -> none  [the longest x1 61.2 us: body(): back_total = lax.psum(back_part, ('rows', 'neur'))]
    dot_general x6 -> x1, matrix products: 47 us -> 1.83 us  [body(): jnp.einsum('tr,tf->rf', hidden, residue, preferred_element_type=f32)]
    ppermute x0 -> x32, waiting for transfers between devices: none -> 42.2 us  [flip(): return lax.ppermute(value, axis, [(i, i ^ distance) for i in range(size)])]
    ppermute x0 -> x32, starting transfers between devices: none -> 29.9 us  [flip(): return lax.ppermute(value, axis, [(i, i ^ distance) for i in range(size)])]
    convert_element_type x1, other arithmetic: 3.54 us -> 0.02 us  [body(): back = back.astype(bf16)]
  transfers between devices with their start and end apart: 3 -> 32, of which waited for: 3 -> 13; matrix products, arithmetic and copies ran while one was open for 9% -> 1% of each run, Pallas kernels for 0% -> 40%
where the time goes in v1:
time: 163 us; the launch traced here: 162 us
  Pallas kernels  82.1 us (50%)
  waiting for transfers between devices  42.2 us (26%)
  starting transfers between devices  29.9 us (18%)
  local copies, waits for them, and re-layouts  4.48 us (3%)
  matrix products  1.83 us (1%)
    pallas_call x30, Pallas kernels, call(): pl.pallas_call(body, out_shape=tuple(outs), in_specs=[spot(space) for spa...  82.1 us
    ppermute x32, waiting for transfers between devices, flip(): return lax.ppermute(value, axis, [(i, i ^ distance) for i in range(size)])  42.2 us
    ppermute x32, starting transfers between devices, flip(): return lax.ppermute(value, axis, [(i, i ^ distance) for i in range(size)])  29.9 us
    unnamed x41, local copies, waits for them, and re-layouts  4.39 us
  transfers between devices with their start and end apart: 32, of which 13 were waited for; matrix products, arithmetic and copies ran while one was open for 1% of the time, Pallas kernels for 40%

profile of v1, /device:TPU:0, one launch (start us, length us, event | category | flops | bytes accessed | tf_op | source)
XLA Modules:
  0.0 162.0 jit_solution(12843238768393286172)
XLA Ops:
  0.6 4.1 %collective-permute-start = (bf16[64,3072]{1,0:T(8,128)(2,1)}, bf16[64,3072]{1,0:T(8,128)(2,1)}, u32[]{:S(2)}, u32[]{:S(2)}) collective-permute-start(bf16[64,3072]{1,0:T(8,128)(2,1)} %refs_3_.13), channel_id=1, source_target_pairs={{0,4},{1,5},{2,6},{3,7},{4,0},{5,1},{6,2},{7,3},{8,12},{9,13},{10,... | collective-permute-start | bytes 1179656 | tf_op jit(solution)/shard_map/ppermute | solution.py:14
  8.7 7.9 %collective-permute-done.2.refs_2_.refs_3_.refs_4_ = bf16[64,3072]{1,0:T(8,128)(2,1)S(1)} collective-permute-done((bf16[64,3072]{1,0:T(8,128)(2,1)}, bf16[64,3072]{1,0:T(8,128)(2,1)S(1)}, u32[]{:S(2)}, u32[]{:S(2)}) %collective-permute-start.2) | collective-permute-done | bytes 393248 | tf_op jit(solution)/shard_map/ppermute | solution.py:14
  16.6 4.5 %shard_map.77.refs_4_ = bf16[128,1536]{1,0:T(8,128)(2,1)S(1)} custom-call(s32[1]{0:T(128)} %bitcast.1.refs_0_, bf16[64,3072]{1,0:T(8,128)(2,1)S(1)} %copy-done.4, bf16[64,3072]{1,0:T(8,128)(2,1)S(1)} %collective-permute-done.2.refs_2_.refs_3_.refs_4_, bf16[3072,6144]{1,0:T(8,128)(2,1)} %refs_4_.7, f32[1,1536]{1,0:T(1,128)S(1)} %shard_map.76.refs_4_.refs_1_), custom_call_target="tpu_custom_call" | custom-call | flops 10000000000 | bytes 1000 | tf_op jit(solution)/shard_map/pallas_call | solution.py:173
  21.2 4.4 %shard_map.78.refs_1_ = bf16[128,1536]{1,0:T(8,128)(2,1)S(1)} custom-call(s32[1]{0:T(128)} %bitcast.1.refs_0_, bf16[64,3072]{1,0:T(8,128)(2,1)S(1)} %copy-done.4, bf16[64,3072]{1,0:T(8,128)(2,1)S(1)} %collective-permute-done.2.refs_2_.refs_3_.refs_4_, bf16[3072,6144]{1,0:T(8,128)(2,1)} %refs_4_.7, bf16[128,1536]{1,0:T(8,128)(2,1)S(1)} %shard_map.77.refs_4_), custom_call_target="tpu_custom_call" | custom-call | flops 10000000000 | bytes 1000 | tf_op jit(solution)/shard_map/pallas_call | solution.py:173
  26.2 7.3 %collective-permute-done.5.refs_0_ = bf16[64,3072]{1,0:T(8,128)(2,1)S(1)} collective-permute-done((bf16[64,3072]{1,0:T(8,128)(2,1)}, bf16[64,3072]{1,0:T(8,128)(2,1)S(1)}, u32[]{:S(2)}, u32[]{:S(2)}) %collective-permute-start.5) | collective-permute-done | bytes 393248 | tf_op jit(solution)/shard_map/ppermute | solution.py:14
  34.1 4.4 %shard_map.80.refs_5_ = bf16[128,1536]{1,0:T(8,128)(2,1)S(1)} custom-call(s32[1]{0:T(128)} %bitcast.1.refs_0_, bf16[64,3072]{1,0:T(8,128)(2,1)S(1)} %copy-done.4, bf16[64,3072]{1,0:T(8,128)(2,1)S(1)} %collective-permute-done.2.refs_2_.refs_3_.refs_4_, bf16[128,1536]{1,0:T(8,128)(2,1)S(1)} %collective-permute-done.4.refs_3_, bf16[3072,6144]{1,0:T(8,128)(2,1)} %refs_4_.7, ...), custom_call_target="tpu_custom_call" | custom-call | flops 10000000000 | bytes 1000 | tf_op jit(solution)/shard_map/pallas_call | solution.py:173
  40.1 4.4 %shard_map.81.refs_2_ = f32[128,1536]{1,0:T(8,128)S(1)} custom-call(s32[1]{0:T(128)} %bitcast.1.refs_0_, bf16[64,3072]{1,0:T(8,128)(2,1)S(1)} %copy-done.4, bf16[64,3072]{1,0:T(8,128)(2,1)S(1)} %collective-permute-done.2.refs_2_.refs_3_.refs_4_, bf16[128,1536]{1,0:T(8,128)(2,1)S(1)} %collective-permute-done.3.refs_3_, bf16[3072,6144]{1,0:T(8,128)(2,1)} %refs_4_.7, ...), custom_call_target="tpu_custom_call" | custom-call | flops 10000000000 | bytes 1000 | tf_op jit(solution)/shard_map/pallas_call | solution.py:173
  48.8 6.9 %shard_map.85.refs_6_ = bf16[256,1536]{1,0:T(8,128)(2,1)} custom-call(s32[1]{0:T(128)} %bitcast.1.refs_0_, bf16[64,3072]{1,0:T(8,128)(2,1)S(1)} %copy-done.1, bf16[64,3072]{1,0:T(8,128)(2,1)S(1)} %collective-permute-done.8.refs_5_.refs_2_.refs_6_, bf16[64,3072]{1,0:T(8,128)(2,1)} %get-tuple-element.32.refs_6_.refs_3_.refs_7_, ...), custom_call_target="tpu_custom_call" | custom-call | flops 4000000000 | bytes 1000 | tf_op jit(solution)/shard_map/pallas_call | solution.py:173
  55.7 6.9 %shard_map.86.refs_7_ = bf16[256,1536]{1,0:T(8,128)(2,1)} custom-call(s32[1]{0:T(128)} %bitcast.1.refs_0_, bf16[64,3072]{1,0:T(8,128)(2,1)S(1)} %copy-done.1, bf16[64,3072]{1,0:T(8,128)(2,1)S(1)} %collective-permute-done.8.refs_5_.refs_2_.refs_6_, bf16[64,3072]{1,0:T(8,128)(2,1)} %get-tuple-element.32.refs_6_.refs_3_.refs_7_, ...), custom_call_target="tpu_custom_call" | custom-call | flops 4000000000 | bytes 1000 | tf_op jit(solution)/shard_map/pallas_call | solution.py:173
  66.2 6.3 %shard_map.87.refs_4_ = bf16[256,1536]{1,0:T(8,128)(2,1)S(1)} custom-call(s32[1]{0:T(128)} %bitcast.1.refs_0_, bf16[64,3072]{1,0:T(8,128)(2,1)S(1)} %copy-done.2, bf16[64,3072]{1,0:T(8,128)(2,1)S(1)} %collective-permute-done.8.refs_5_.refs_2_.refs_6_, bf16[64,3072]{1,0:T(8,128)(2,1)} %get-tuple-element.32.refs_6_.refs_3_.refs_7_, ...), custom_call_target="tpu_custom_call" | custom-call | flops 4000000000 | bytes 1000 | tf_op jit(solution)/shard_map/pallas_call | solution.py:173
  75.5 7.6 %collective-permute-done.7.refs_3_.refs_2_.refs_10_ = bf16[64,3072]{1,0:T(8,128)(2,1)} collective-permute-done((bf16[64,3072]{1,0:T(8,128)(2,1)}, bf16[64,3072]{1,0:T(8,128)(2,1)}, u32[]{:S(2)}, u32[]{:S(2)}) %collective-permute-start.7) | collective-permute-done | bytes 393248 | tf_op jit(solution)/shard_map/ppermute | solution.py:14
  84.6 6.5 %shard_map.89.refs_4_.refs_2_ = f32[256,1536]{1,0:T(8,128)S(1)} custom-call(s32[1]{0:T(128)} %bitcast.1.refs_0_, bf16[64,3072]{1,0:T(8,128)(2,1)S(1)} %copy-done.2, bf16[64,3072]{1,0:T(8,128)(2,1)S(1)} %collective-permute-done.8.refs_5_.refs_2_.refs_6_, bf16[64,3072]{1,0:T(8,128)(2,1)} %get-tuple-element.32.refs_6_.refs_3_.refs_7_, ...), custom_call_target="tpu_custom_call" | custom-call | flops 4000000000 | bytes 1000 | tf_op jit(solution)/shard_map/pallas_call | solution.py:173
  91.9 5.5 %shard_map.91.refs_4_ = bf16[128,1536]{1,0:T(8,128)(2,1)S(1)} custom-call(s32[1]{0:T(128)} %bitcast.1.refs_0_, bf16[64,3072]{1,0:T(8,128)(2,1)} %collective-permute-done.6.refs_2_.refs_1_.refs_8_, bf16[64,3072]{1,0:T(8,128)(2,1)} %collective-permute-done.7.refs_3_.refs_2_.refs_10_, bf16[3072,6144]{1,0:T(8,128)(2,1)} %refs_4_.7, ...), custom_call_target="tpu_custom_call" | custom-call | flops 4000000000 | bytes 1000 | tf_op jit(solution)/shard_map/pallas_call | solution.py:173
  97.7 5.5 %shard_map.92.refs_1_ = bf16[128,1536]{1,0:T(8,128)(2,1)S(1)} custom-call(s32[1]{0:T(128)} %bitcast.1.refs_0_, bf16[64,3072]{1,0:T(8,128)(2,1)} %collective-permute-done.6.refs_2_.refs_1_.refs_8_, bf16[64,3072]{1,0:T(8,128)(2,1)} %collective-permute-done.7.refs_3_.refs_2_.refs_10_, bf16[3072,6144]{1,0:T(8,128)(2,1)} %refs_4_.7, ...), custom_call_target="tpu_custom_call" | custom-call | flops 4000000000 | bytes 1000 | tf_op jit(solution)/shard_map/pallas_call | solution.py:173
  105.2 2.9 %collective-permute-start.17 = (bf16[256,128]{1,0:T(8,128)(2,1)S(1)}, bf16[256,128]{1,0:T(8,128)(2,1)S(1)}, u32[]{:S(2)}, u32[]{:S(2)}) collective-permute-start(bf16[256,128]{1,0:T(8,128)(2,1)S(1)} %shard_map.94.refs_0_), channel_id=1, source_target_pairs={{0,4},{1,5},{2,6},{3,7},{4,0},{5,1},{6,2},{7,3},{8,12},{9,13},{10,... | collective-permute-start | bytes 196616 | tf_op jit(solution)/shard_map/ppermute | solution.py:14
  108.1 5.5 %shard_map.95.refs_4_ = bf16[128,1536]{1,0:T(8,128)(2,1)S(1)} custom-call(s32[1]{0:T(128)} %bitcast.1.refs_0_, bf16[64,3072]{1,0:T(8,128)(2,1)} %collective-permute-done.6.refs_2_.refs_1_.refs_8_, bf16[64,3072]{1,0:T(8,128)(2,1)} %collective-permute-done.7.refs_3_.refs_2_.refs_10_, bf16[128,1536]{1,0:T(8,128)(2,1)S(1)} %collective-permute-done.19.refs_3_, ...), custom_call_target="tpu_custom_call" | custom-call | flops 4000000000 | bytes 1000 | tf_op jit(solution)/shard_map/pallas_call | solution.py:173
  116.6 5.5 %shard_map.97.refs_6_.refs_2_ = f32[128,1536]{1,0:T(8,128)S(1)} custom-call(s32[1]{0:T(128)} %bitcast.1.refs_0_, bf16[64,3072]{1,0:T(8,128)(2,1)} %collective-permute-done.6.refs_2_.refs_1_.refs_8_, bf16[64,3072]{1,0:T(8,128)(2,1)} %collective-permute-done.7.refs_3_.refs_2_.refs_10_, bf16[128,1536]{1,0:T(8,128)(2,1)S(1)} %collective-permute-done.14.refs_3_, ...), custom_call_target="tpu_custom_call" | custom-call | flops 4000000000 | bytes 1000 | tf_op jit(solution)/shard_map/pallas_call | solution.py:173
  127.2 2.6 %shard_map.102 = (bf16[256,1536]{1,0:T(8,128)(2,1)S(1)}, bf16[8,256,128]{2,1,0:T(8,128)(2,1)S(1)}) custom-call(s32[2]{0:T(128)S(1)} %copy-done.11, bf16[512,1024]{1,0:T(8,128)(2,1)S(1)} %shard_map.101.refs_1_, f32[512,1536]{1,0:T(8,128)S(1)} %get-tuple-element.52.refs_5_.refs_2_, bf16[1024,1536]{1,0:T(8,128)(2,1)S(1)} %copy-done.12), custom_call_target="tpu_custom_call" | custom-call | flops 4000000000 | bytes 1000 | tf_op jit(solution)/shard_map/pallas_call | solution.py:173
  129.9 2.7 %shard_map.103 = (bf16[256,1536]{1,0:T(8,128)(2,1)S(1)}, f32[8,256,128]{2,1,0:T(8,128)S(1)}) custom-call(s32[2]{0:T(128)S(1)} %copy-done.9, bf16[512,1024]{1,0:T(8,128)(2,1)S(1)} %shard_map.101.refs_1_, f32[512,1536]{1,0:T(8,128)S(1)} %get-tuple-element.52.refs_5_.refs_2_, bf16[1024,1536]{1,0:T(8,128)(2,1)S(1)} %copy-done.12, ...), custom_call_target="tpu_custom_call" | custom-call | flops 4000000000 | bytes 1000 | tf_op jit(solution)/shard_map/pallas_call | solution.py:173
  138.3 4.8 %collective-permute-done.26.refs_1_ = bf16[4,256,128]{2,1,0:T(8,128)(2,1)S(1)} collective-permute-done((bf16[4,256,128]{2,1,0:T(8,128)(2,1)S(1)}, bf16[4,256,128]{2,1,0:T(8,128)(2,1)S(1)}, u32[]{:S(2)}, u32[]{:S(2)}) %collective-permute-start.26) | collective-permute-done | bytes 262176 | tf_op jit(solution)/shard_map/ppermute | solution.py:14
  143.2 3.6 %collective-permute-start.29 = (bf16[256,128]{1,0:T(8,128)(2,1)S(1)}, bf16[256,128]{1,0:T(8,128)(2,1)S(1)}, u32[]{:S(2)}, u32[]{:S(2)}) collective-permute-start(bf16[256,128]{1,0:T(8,128)(2,1)S(1)} %get-tuple-element.62), channel_id=1, source_target_pairs={{0,6},{1,7},{2,4},{3,5},{4,2},{5,3},{6,0},{7,1},{8,14},{9,15},{10,... | collective-permute-start | bytes 196616 | tf_op jit(solution)/shard_map/ppermute | solution.py:14
  149.4 2.6 %collective-permute-done.28 = bf16[256,128]{1,0:T(8,128)(2,1)S(1)} collective-permute-done((bf16[256,128]{1,0:T(8,128)(2,1)S(1)}, bf16[256,128]{1,0:T(8,128)(2,1)S(1)}, u32[]{:S(2)}, u32[]{:S(2)}) %collective-permute-start.28) | collective-permute-done | bytes 65568 | tf_op jit(solution)/shard_map/ppermute | solution.py:14
  153.4 4.0 %collective-permute-done.30 = f32[256,128]{1,0:T(8,128)S(1)} collective-permute-done((f32[256,128]{1,0:T(8,128)S(1)}, f32[256,128]{1,0:T(8,128)S(1)}, u32[]{:S(2)}, u32[]{:S(2)}) %collective-permute-start.30) | collective-permute-done | bytes 131104 | tf_op jit(solution)/shard_map/ppermute | solution.py:14
  158.8 3.3 %shard_map.105 = f32[3072,128]{1,0:T(8,128)} custom-call(s32[2]{0:T(128)S(1)} %copy-done.9, bf16[256,128]{1,0:T(8,128)(2,1)S(1)} %add_convert_fusion.refs_1_, bf16[256,128]{1,0:T(8,128)(2,1)S(1)} %collective-permute-done.31.refs_2_, bf16[64,3072]{1,0:T(8,128)(2,1)S(1)} %copy-done.5, bf16[64,3072]{1,0:T(8,128)(2,1)S(1)} %copy-done.7, ...), custom_call_target="tpu_custom_call" | custom-call | flops 4000000000 | bytes 1000 | tf_op jit(solution)/shard_map/pallas_call | solution.py:173
  (120 shorter events, 41.0 us)
Async XLA Ops:
  0.6 43.9 %collective-permute-start = (bf16[64,3072]{1,0:T(8,128)(2,1)}, bf16[64,3072]{1,0:T(8,128)(2,1)}, u32[]{:S(2)}, u32[]{:S(2)}) collective-permute-start(bf16[64,3072]{1,0:T(8,128)(2,1)} %refs_3_.13), channel_id=1, source_target_pairs={{0,4},{1,5},{2,6},{3,7},{4,0},{5,1},{6,2},{7,3},{8,12},{9,13},{10,... | collective-permute-start | bytes 1179656 | tf_op jit(solution)/shard_map/ppermute | solution.py:14
  4.7 39.8 %collective-permute-start.1 = (bf16[64,3072]{1,0:T(8,128)(2,1)}, bf16[64,3072]{1,0:T(8,128)(2,1)}, u32[]{:S(2)}, u32[]{:S(2)}) collective-permute-start(bf16[64,3072]{1,0:T(8,128)(2,1)} %refs_3_.13), channel_id=1, source_target_pairs={{0,6},{1,7},{2,4},{3,5},{4,2},{5,3},{6,0},{7,1},{8,14},{9,15},{10,... | collective-permute-start | bytes 1179656 | tf_op jit(solution)/shard_map/ppermute | solution.py:14
  6.1 10.5 %collective-permute-start.2 = (bf16[64,3072]{1,0:T(8,128)(2,1)}, bf16[64,3072]{1,0:T(8,128)(2,1)S(1)}, u32[]{:S(2)}, u32[]{:S(2)}) collective-permute-start(bf16[64,3072]{1,0:T(8,128)(2,1)} %refs_3_.13), channel_id=1, source_target_pairs={{0,1},{1,0},{2,3},{3,2},{4,5},{5,4},{6,7},{7,6},{8,9},{9,8},{10,11... | collective-permute-start | bytes 1179656 | tf_op jit(solution)/shard_map/ppermute | solution.py:14
  7.6 25.9 %collective-permute-start.5 = (bf16[64,3072]{1,0:T(8,128)(2,1)}, bf16[64,3072]{1,0:T(8,128)(2,1)S(1)}, u32[]{:S(2)}, u32[]{:S(2)}) collective-permute-start(bf16[64,3072]{1,0:T(8,128)(2,1)} %refs_3_.13), channel_id=1, source_target_pairs={{0,2},{1,3},{2,0},{3,1},{4,6},{5,7},{6,4},{7,5},{8,10},{9,11},{10,... | collective-permute-start | bytes 1179656 | tf_op jit(solution)/shard_map/ppermute | solution.py:14
  21.2 12.9 %collective-permute-start.4 = (bf16[128,1536]{1,0:T(8,128)(2,1)S(1)}, bf16[128,1536]{1,0:T(8,128)(2,1)S(1)}, u32[]{:S(2)}, u32[]{:S(2)}) collective-permute-start(bf16[128,1536]{1,0:T(8,128)(2,1)S(1)} %shard_map.77.refs_4_), channel_id=1, source_target_pairs={{0,8},{8,0},{16,24},{24,16},{1,9},{9,1},{17,25},{25,17},{2,10},{10... | collective-permute-start | bytes 1179656 | tf_op jit(solution)/shard_map/ppermute | solution.py:14
  25.7 14.4 %collective-permute-start.3 = (bf16[128,1536]{1,0:T(8,128)(2,1)S(1)}, bf16[128,1536]{1,0:T(8,128)(2,1)S(1)}, u32[]{:S(2)}, u32[]{:S(2)}) collective-permute-start(bf16[128,1536]{1,0:T(8,128)(2,1)S(1)} %shard_map.78.refs_1_), channel_id=1, source_target_pairs={{0,8},{8,0},{16,24},{24,16},{1,9},{9,1},{17,25},{25,17},{2,10},{10... | collective-permute-start | bytes 1179656 | tf_op jit(solution)/shard_map/ppermute | solution.py:14
  33.5 11.0 %collective-permute-start.8 = (bf16[64,3072]{1,0:T(8,128)(2,1)S(1)}, bf16[64,3072]{1,0:T(8,128)(2,1)S(1)}, u32[]{:S(2)}, u32[]{:S(2)}) collective-permute-start(bf16[64,3072]{1,0:T(8,128)(2,1)S(1)} %get-tuple-element.34.refs_4_.refs_1_.refs_5_), channel_id=1, source_target_pairs={{0,1},{1,0},{2,3},{3,2},{4,5},{5,4},{6,7},{7,6},{8,9},{9,8},{10,11... | collective-permute-start | bytes 1179656 | tf_op jit(solution)/shard_map/ppermute | solution.py:14
  38.5 9.0 %collective-permute-start.10 = (bf16[128,1536]{1,0:T(8,128)(2,1)S(1)}, bf16[128,1536]{1,0:T(8,128)(2,1)S(1)}, u32[]{:S(2)}, u32[]{:S(2)}) collective-permute-start(bf16[128,1536]{1,0:T(8,128)(2,1)S(1)} %shard_map.80.refs_5_), channel_id=1, source_target_pairs={{0,16},{8,24},{16,0},{24,8},{1,17},{9,25},{17,1},{25,9},{2,18},{10... | collective-permute-start | bytes 1179656 | tf_op jit(solution)/shard_map/ppermute | solution.py:14
  55.6 9.6 %collective-permute-start.11 = (bf16[256,1536]{1,0:T(8,128)(2,1)}, bf16[256,1536]{1,0:T(8,128)(2,1)}, u32[]{:S(2)}, u32[]{:S(2)}) collective-permute-start(bf16[256,1536]{1,0:T(8,128)(2,1)} %shard_map.85.refs_6_), channel_id=1, source_target_pairs={{0,8},{8,0},{16,24},{24,16},{1,9},{9,1},{17,25},{25,17},{2,10},{10... | collective-permute-start | bytes 2359304 | tf_op jit(solution)/shard_map/ppermute | solution.py:14
  62.6 22.0 %collective-permute-start.13 = (bf16[256,1536]{1,0:T(8,128)(2,1)}, bf16[256,1536]{1,0:T(8,128)(2,1)}, u32[]{:S(2)}, u32[]{:S(2)}) collective-permute-start(bf16[256,1536]{1,0:T(8,128)(2,1)} %shard_map.86.refs_7_), channel_id=1, source_target_pairs={{0,8},{8,0},{16,24},{24,16},{1,9},{9,1},{17,25},{25,17},{2,10},{10... | collective-permute-start | bytes 2359304 | tf_op jit(solution)/shard_map/ppermute | solution.py:14
  63.2 12.3 %collective-permute-start.6 = (bf16[64,3072]{1,0:T(8,128)(2,1)}, bf16[64,3072]{1,0:T(8,128)(2,1)}, u32[]{:S(2)}, u32[]{:S(2)}) collective-permute-start(bf16[64,3072]{1,0:T(8,128)(2,1)} %get-tuple-element.32.refs_6_.refs_3_.refs_7_), channel_id=1, source_target_pairs={{0,1},{1,0},{2,3},{3,2},{4,5},{5,4},{6,7},{7,6},{8,9},{9,8},{10,11... | collective-permute-start | bytes 1179656 | tf_op jit(solution)/shard_map/ppermute | solution.py:14
  64.7 18.3 %collective-permute-start.7 = (bf16[64,3072]{1,0:T(8,128)(2,1)}, bf16[64,3072]{1,0:T(8,128)(2,1)}, u32[]{:S(2)}, u32[]{:S(2)}) collective-permute-start(bf16[64,3072]{1,0:T(8,128)(2,1)} %get-tuple-element.33.refs_7_.refs_4_.refs_9_), channel_id=1, source_target_pairs={{0,1},{1,0},{2,3},{3,2},{4,5},{5,4},{6,7},{7,6},{8,9},{9,8},{10,11... | collective-permute-start | bytes 1179656 | tf_op jit(solution)/shard_map/ppermute | solution.py:14
  65.2 25.9 %collective-permute-start.9 = (f32[192,128]{1,0:T(8,128)}, f32[192,128]{1,0:T(8,128)S(1)}, u32[]{:S(2)}, u32[]{:S(2)}) collective-permute-start(f32[192,128]{1,0:T(8,128)} %copy-done.15), channel_id=1, source_target_pairs={{0,8},{8,0},{16,24},{24,16},{1,9},{9,1},{17,25},{25,17},{2,10},{10... | collective-permute-start | bytes 294920 | tf_op jit(solution)/shard_map/ppermute | solution.py:14
  72.6 50.2 %collective-permute-start.21 = (bf16[256,1536]{1,0:T(8,128)(2,1)S(1)}, bf16[256,1536]{1,0:T(8,128)(2,1)S(1)}, u32[]{:S(2)}, u32[]{:S(2)}) collective-permute-start(bf16[256,1536]{1,0:T(8,128)(2,1)S(1)} %shard_map.87.refs_4_), channel_id=1, source_target_pairs={{0,16},{8,24},{16,0},{24,8},{1,17},{9,25},{17,1},{25,9},{2,18},{10... | collective-permute-start | bytes 2359304 | tf_op jit(solution)/shard_map/ppermute | solution.py:14
  91.2 12.4 %collective-permute-start.15 = (f32[256,128]{1,0:T(8,128)S(1)}, f32[256,128]{1,0:T(8,128)S(1)}, u32[]{:S(2)}, u32[]{:S(2)}) collective-permute-start(f32[256,128]{1,0:T(8,128)S(1)} %shard_map.90.refs_4_.refs_0_), channel_id=1, source_target_pairs={{0,16},{8,24},{16,0},{24,8},{1,17},{9,25},{17,1},{25,9},{2,18},{10... | collective-permute-start | bytes 393224 | tf_op jit(solution)/shard_map/ppermute | solution.py:14
  97.4 10.7 %collective-permute-start.19 = (bf16[128,1536]{1,0:T(8,128)(2,1)S(1)}, bf16[128,1536]{1,0:T(8,128)(2,1)S(1)}, u32[]{:S(2)}, u32[]{:S(2)}) collective-permute-start(bf16[128,1536]{1,0:T(8,128)(2,1)S(1)} %shard_map.91.refs_4_), channel_id=1, source_target_pairs={{0,8},{8,0},{16,24},{24,16},{1,9},{9,1},{17,25},{25,17},{2,10},{10... | collective-permute-start | bytes 1179656 | tf_op jit(solution)/shard_map/ppermute | solution.py:14
  103.2 13.4 %collective-permute-start.14 = (bf16[128,1536]{1,0:T(8,128)(2,1)S(1)}, bf16[128,1536]{1,0:T(8,128)(2,1)S(1)}, u32[]{:S(2)}, u32[]{:S(2)}) collective-permute-start(bf16[128,1536]{1,0:T(8,128)(2,1)S(1)} %shard_map.92.refs_1_), channel_id=1, source_target_pairs={{0,8},{8,0},{16,24},{24,16},{1,9},{9,1},{17,25},{25,17},{2,10},{10... | collective-permute-start | bytes 1179656 | tf_op jit(solution)/shard_map/ppermute | solution.py:14
  103.6 10.1 %collective-permute-start.16 = (bf16[256,128]{1,0:T(8,128)(2,1)S(1)}, bf16[256,128]{1,0:T(8,128)(2,1)S(1)}, u32[]{:S(2)}, u32[]{:S(2)}) collective-permute-start(bf16[256,128]{1,0:T(8,128)(2,1)S(1)} %shard_map.94.refs_0_), channel_id=1, source_target_pairs={{0,2},{1,3},{2,0},{3,1},{4,6},{5,7},{6,4},{7,5},{8,10},{9,11},{10,... | collective-permute-start | bytes 196616 | tf_op jit(solution)/shard_map/ppermute | solution.py:14
  105.2 9.8 %collective-permute-start.17 = (bf16[256,128]{1,0:T(8,128)(2,1)S(1)}, bf16[256,128]{1,0:T(8,128)(2,1)S(1)}, u32[]{:S(2)}, u32[]{:S(2)}) collective-permute-start(bf16[256,128]{1,0:T(8,128)(2,1)S(1)} %shard_map.94.refs_0_), channel_id=1, source_target_pairs={{0,4},{1,5},{2,6},{3,7},{4,0},{5,1},{6,2},{7,3},{8,12},{9,13},{10,... | collective-permute-start | bytes 196616 | tf_op jit(solution)/shard_map/ppermute | solution.py:14
  108.1 6.9 %collective-permute-start.18 = (bf16[256,128]{1,0:T(8,128)(2,1)S(1)}, bf16[256,128]{1,0:T(8,128)(2,1)S(1)}, u32[]{:S(2)}, u32[]{:S(2)}) collective-permute-start(bf16[256,128]{1,0:T(8,128)(2,1)S(1)} %shard_map.94.refs_0_), channel_id=1, source_target_pairs={{0,6},{1,7},{2,4},{3,5},{4,2},{5,3},{6,0},{7,1},{8,14},{9,15},{10,... | collective-permute-start | bytes 196616 | tf_op jit(solution)/shard_map/ppermute | solution.py:14
  113.7 10.7 %collective-permute-start.20 = (bf16[128,1536]{1,0:T(8,128)(2,1)S(1)}, bf16[128,1536]{1,0:T(8,128)(2,1)S(1)}, u32[]{:S(2)}, u32[]{:S(2)}) collective-permute-start(bf16[128,1536]{1,0:T(8,128)(2,1)S(1)} %shard_map.95.refs_4_), channel_id=1, source_target_pairs={{0,16},{8,24},{16,0},{24,8},{1,17},{9,25},{17,1},{25,9},{2,18},{10... | collective-permute-start | bytes 1179656 | tf_op jit(solution)/shard_map/ppermute | solution.py:14
  115.1 7.3 %collective-permute-start.22 = (bf16[4,256,128]{2,1,0:T(8,128)(2,1)S(1)}, bf16[4,256,128]{2,1,0:T(8,128)(2,1)S(1)}, u32[]{:S(2)}, u32[]{:S(2)}) collective-permute-start(bf16[4,256,128]{2,1,0:T(8,128)(2,1)S(1)} %shard_map.100.refs_1_), channel_id=1, source_target_pairs={{0,1},{1,0},{2,3},{3,2},{4,5},{5,4},{6,7},{7,6},{8,9},{9,8},{10,11... | collective-permute-start | bytes 786440 | tf_op jit(solution)/shard_map/ppermute | solution.py:14
  116.6 8.7 %collective-permute-start.23 = (bf16[4,256,128]{2,1,0:T(8,128)(2,1)S(1)}, bf16[4,256,128]{2,1,0:T(8,128)(2,1)S(1)}, u32[]{:S(2)}, u32[]{:S(2)}) collective-permute-start(bf16[4,256,128]{2,1,0:T(8,128)(2,1)S(1)} %shard_map.100.refs_1_), channel_id=1, source_target_pairs={{0,8},{8,0},{16,24},{24,16},{1,9},{9,1},{17,25},{25,17},{2,10},{10... | collective-permute-start | bytes 786440 | tf_op jit(solution)/shard_map/ppermute | solution.py:14
  134.7 8.4 %collective-permute-start.26 = (bf16[4,256,128]{2,1,0:T(8,128)(2,1)S(1)}, bf16[4,256,128]{2,1,0:T(8,128)(2,1)S(1)}, u32[]{:S(2)}, u32[]{:S(2)}) collective-permute-start(bf16[4,256,128]{2,1,0:T(8,128)(2,1)S(1)} %slice.27), channel_id=1, source_target_pairs={{0,1},{1,0},{2,3},{3,2},{4,5},{5,4},{6,7},{7,6},{8,9},{9,8},{10,11... | collective-permute-start | bytes 786440 | tf_op jit(solution)/shard_map/ppermute | solution.py:14
  (28 other events, 182.7 us)

commit v2 on v1

--- a/solution.py
+++ b/solution.py
@@ -178,7 +178,7 @@
         scratch_shapes=list(scratch),
         input_output_aliases=aliased,
         compiler_params=pltpu.CompilerParams(vmem_limit_bytes=mib * 2**20),
-        cost_estimate=pl.CostEstimate(flops=weight * 4000000000 if weight == 1 else 10**10, bytes_accessed=1000, transcendentals=0),
+        cost_estimate=pl.CostEstimate(flops=weight * 10**6, bytes_accessed=1000, transcendentals=0),
     )(*ins, *through, *after)
     return results
 
@@ -218,56 +218,73 @@
     return jnp.concatenate([ref[:, cols] for ref in refs]) if len(refs) > 1 else refs[0][:, cols]
 
 
-def partial_sums(row, parts, weight, width, blocks, dtype, gots=(), plus=(), cost=1, **order):
+def partial_sums(row, parts, weight, width, blocks, gots=None, pieces=None, retain=False, split=1, cost=1, **order):
     rows = sum(part.shape[0] for part in parts)
     depth = weight.shape[0]
     tile = tile_of(width)
     per = width // tile
     tiles = len(blocks) * per
-    slots = min(tiles, 3)
-    extra = [value for pair in plus for value in pair]
-    heights = [pair[0].shape[0] for pair in plus]
-    ins = [row, *parts, *gots, *extra, weight]
+    slots, ahead = min(tiles, 3), min(tiles, 2)
+    gots = gots or []
+    flat = [part for listed in gots for part in listed]
+    splits = [1 if keep else split for _, keep, _ in blocks]
+    starts = [sum(splits[:k]) for k in range(len(blocks) + 1)]
+    loads = pieces is None
+    ins = [row, *parts, *flat] + ([pltpu.with_memory_space_constraint(weight, pltpu.HBM)] if loads else [held(piece) for piece in pieces])
+    n_weights = 1 if loads else len(pieces)
 
     def kernel(*refs):
         row_ref, part_refs = refs[0], refs[1 : 1 + len(parts)]
-        got_refs = refs[1 + len(parts) : 1 + len(parts) + len(gots)]
-        weight_ref = refs[len(ins) - 1]
-        outs, (buffer, sems) = refs[len(ins) : -2], refs[-2:]
+        got_refs = refs[1 + len(parts) : len(ins) - n_weights]
+        weight_refs = refs[len(ins) - n_weights : len(ins)]
+        outs = refs[len(ins) : len(ins) + starts[-1]]
+        kept = refs[len(ins) + starts[-1] : len(ins) + starts[-1] + len(blocks)] if retain else ()
         x, core = row_ref[0] // 2, row_ref[0] % 2
 
+        def cols_of(j):
+            return slice(j % per * tile, (j % per + 1) * tile)
+
+        def tile_ref(j):
+            if not loads:
+                return weight_refs[j // per].at[:, cols_of(j)]
+            return kept[j // per].at[:, cols_of(j)] if retain else refs[-2].at[j % slots]
+
         def copy(j):
-            distance, keep = blocks[j // per]
+            distance, keep, _ = blocks[j // per]
             whose = (x ^ distance) * 2 + (core if keep else 1 - core)
             from_cols = pl.ds(pl.multiple_of(whose * width + (j % per) * tile, 128), tile)
-            return pltpu.make_async_copy(weight_ref.at[:, from_cols], buffer.at[j % slots], sems.at[j % slots])
-
-        for j in range(slots):
-            copy(j).start()
-        first = 0
-        for i, height in enumerate(heights):
-            a_ref, b_ref = refs[len(ins) - 1 - len(extra) + 2 * i : len(ins) + 1 - len(extra) + 2 * i]
-            outs[-1][first : first + height, :] = a_ref[...] + b_ref[...]
-            first += height
+            return pltpu.make_async_copy(weight_refs[0].at[:, from_cols], tile_ref(j), refs[-1].at[j % slots])
+
+        if loads:
+            for j in range(ahead):
+                copy(j).start()
         part = joined(part_refs)
         for j in range(tiles):
-            copy(j).wait()
-            cols = slice(j % per * tile, (j % per + 1) * tile)
-            value = jnp.dot(part, buffer[j % slots], preferred_element_type=f32)
+            if loads:
+                copy(j).wait()
+                if j + ahead < tiles:
+                    copy(j + ahead).start()
+            value = jnp.dot(part, tile_ref(j)[...], preferred_element_type=f32)
+            b = j // per
             if gots:
-                value = value + got_refs[j // per][:, cols].astype(f32)
-            outs[j // per][:, cols] = value.astype(dtype)
-            if j + slots < tiles:
-                copy(j + slots).start()
-
-    sums = [shape_of((sum(heights), extra[0].shape[1]), f32)] if extra else []
+                count = len(gots[b])
+                value = value + joined(got_refs[b * count : (b + 1) * count], cols_of(j)).astype(f32)
+            value = value.astype(blocks[b][2])
+            height = rows // splits[b]
+            for k in range(splits[b]):
+                outs[starts[b] + k][:, cols_of(j)] = value[k * height : (k + 1) * height, :]
+
+    scratch = []
+    if loads:
+        scratch = [pltpu.VMEM((8, 128) if retain else (slots, depth, tile), bf16), pltpu.SemaphoreType.DMA((slots,))]
     return call(
         kernel,
-        [shape_of((rows, width), dtype) for _ in blocks] + sums,
+        [shape_of((rows // n, width), dtype) for n, (_, _, dtype) in zip(splits, blocks) for _ in range(n)]
+        + [pltpu.VMEM((depth, width), bf16) for _ in blocks if retain],
         ins,
-        [pltpu.SMEM] + [pltpu.VMEM] * (len(ins) - 2) + [pl.ANY],
-        scratch=[pltpu.VMEM((slots, depth, tile), bf16), pltpu.SemaphoreType.DMA((slots,))],
-        mib=24,
+        [pltpu.SMEM] + [pltpu.VMEM] * (len(ins) - 1 - n_weights) + [pl.ANY if loads else pltpu.VMEM] * n_weights,
+        scratch=scratch,
+        mib=10 if retain or not loads else 16,
         weight=cost,
         **order,
     )
@@ -281,7 +298,7 @@
         for group, size in zip(groups, rows):
             value = refs[at][...]
             for k in range(1, len(group)):
-                value = value + refs[at + k][...]
+                value = value.astype(f32) + refs[at + k][...].astype(f32)
             out_ref[first : first + size, :] = value.astype(dtype)
             at, first = at + len(group), first + size
 
@@ -290,13 +307,18 @@
     return call(kernel, [out], ins, [pltpu.VMEM] * len(ins), **order)
 
 
-def stacked(values, **order):
+def stacked(values, flat=False, **order):
+    rows, columns = values[0].shape
+
     def kernel(*refs):
-        for k, ref in enumerate(refs[:-1]):
-            refs[-1][k] = ref[...]
-
-    out = shape_of((len(values),) + values[0].shape, values[0].dtype)
-    return call(kernel, [out], values, [pltpu.VMEM] * len(values), **order)
+        for k in range(len(values)):
+            if flat:
+                refs[-1][k * rows : (k + 1) * rows, :] = refs[k][...]
+            else:
+                refs[-1][k] = refs[k][...]
+
+    shape = (len(values) * rows, columns) if flat else (len(values), rows, columns)
+    return call(kernel, [shape_of(shape, values[0].dtype)], values, [pltpu.VMEM] * len(values), **order)
 
 
 def finish_preact(neur, bias, chunks, t, n_neur, width, before=None, **order):
@@ -352,7 +374,7 @@
 
     def kernel(row_ref, down_ref, *refs):
         keep_ref, send_ref = refs[-2:]
-        sums = jnp.dot(joined(refs[: len(listed)]), down_ref[...], preferred_element_type=f32)
+        sums = jnp.dot(joined(refs[: len(shards)]), down_ref[...], preferred_element_type=f32)
         value = {s: sums[i * t : (i + 1) * t, :] for i, s in enumerate(listed)}
         first = row_ref[0] % 2 == 0
         for i, (a, b) in enumerate(pairs):
@@ -360,7 +382,7 @@
             send_ref[i * t : (i + 1) * t, :] = jnp.where(first, value[b], value[a])
 
     out = shape_of((len(pairs) * t, rank), f32)
-    ins = [row, down] + [shards[s] for s in listed]
+    ins = [row, down, *shards]
     return call(kernel, [out, out], ins, [pltpu.SMEM] + [pltpu.VMEM] * (len(ins) - 1), **order)
 
 
@@ -391,18 +413,21 @@
     )
 
 
-def residue_and_back(at, hidden, target, up, places, lines, half_rows, rank, dtype, **order):
+def residue_and_back(at, hidden, target, up, places, lines, half_rows, rank, dtype, before=None, **order):
     ranks, width = up.shape
     tile = tile_of(width)
-
-    def kernel(at_ref, hidden_ref, target_ref, up_ref, residue_ref, back_ref, total):
+    ins = [at, hidden, target, up] + ([] if before is None else [before])
+
+    def kernel(*refs):
+        at_ref, hidden_ref, target_ref, up_ref = refs[:4]
+        residue_ref, back_ref, total = refs[len(ins) :]
         half, neur = at_ref[0], at_ref[1]
         rows = pl.ds(pl.multiple_of(half * half_rows, half_rows), half_rows)
         for k in range(width // tile):
             cols = slice(k * tile, (k + 1) * tile)
             logits = jnp.dot(hidden_ref[rows, :], up_ref[:, cols], preferred_element_type=f32)
             residue = (loss_weight * (jax.nn.sigmoid(logits) - target_ref[rows, cols])).astype(bf16)
-            residue_ref[:, cols] = residue
+            residue_ref[rows, cols] = residue
             term = lax.dot_general(
                 residue, up_ref[:, cols], (((1,), (1,)), ((), ())), preferred_element_type=f32
             )
@@ -413,41 +438,48 @@
 
     return call(
         kernel,
-        [shape_of((half_rows, width), bf16), shape_of((places * lines, half_rows, rank), dtype)],
-        [at, hidden, target, up],
-        [pltpu.SMEM, pltpu.VMEM, pltpu.VMEM, pltpu.VMEM],
+        [shape_of((2 * half_rows, width), bf16), shape_of((places * lines, half_rows, rank), dtype)],
+        ins,
+        [pltpu.SMEM] + [pltpu.VMEM] * (len(ins) - 1),
         scratch=[pltpu.VMEM((half_rows, ranks), f32)],
         mib=24,
+        aliases={} if before is None else {4: 0},
         **order,
     )
 
 
-def add_lines(total, gots, places, **order):
-    _, half_rows, rank = total.shape
-
-    def kernel(total_ref, *refs):
-        own_ref, away_ref = refs[-2:]
+def add_lines(kept, got, places, lines, after=()):
+    _, half_rows, rank = kept.shape
+
+    def kernel(kept_ref, got_ref, own_ref, *away_refs):
         for d in range(places):
-            value = total_ref[d]
-            for got_ref in refs[:-2]:
+            own_ref[d] = kept_ref[d] + got_ref[d].astype(f32)
+            for e, away_ref in enumerate(away_refs):
+                k = (e + 1) * places + d
+                away_ref[d] = (kept_ref[k] + got_ref[k].astype(f32)).astype(bf16)
+
+    outs = [shape_of((places, half_rows, rank), f32)] + [shape_of((places, half_rows, rank), bf16)] * (lines - 1)
+    return call(kernel, outs, [kept, got], [pltpu.VMEM] * 2, after=after)
+
+
+def add_places(own, gots, places, after=()):
+    _, half_rows, rank = own.shape
+
+    def kernel(own_ref, *refs):
+        got_refs, outs = refs[: len(gots)], refs[len(gots) :]
+        for d in range(places):
+            value = own_ref[d]
+            for got_ref in got_refs:
                 value = value + got_ref[d].astype(f32)
-            if d == 0:
-                own_ref[...] = value
-            else:
-                away_ref[d - 1] = value.astype(bf16)
-
-    return call(
-        kernel,
-        [shape_of((half_rows, rank), f32), shape_of((places - 1, half_rows, rank), bf16)],
-        [total, *gots],
-        [pltpu.VMEM] * (1 + len(gots)),
-        **order,
-    )
-
-
-def down_gradient(at, shards, mine, theirs, t):
+            outs[d][...] = value.astype(f32 if d == 0 else bf16)
+
+    outs = [shape_of((half_rows, rank), f32)] + [shape_of((half_rows, rank), bf16)] * (places - 1)
+    return call(kernel, outs, [own, *gots], [pltpu.VMEM] * (1 + len(gots)), after=after)
+
+
+def down_gradient(at, shards, order, mine, theirs, t):
     count = len(shards)
-    rows, depth = count * t, shards[0].shape[1]
+    rows, depth = len(order) * t, shards[0].shape[1]
     half_rows, rank = mine.shape
     tile = tile_of(depth)
 
@@ -456,8 +488,8 @@
         core, neur = at_ref[0], at_ref[1]
         back[pl.ds(pl.multiple_of(core * half_rows, half_rows), half_rows), :] = mine_ref[...].astype(f32)
         back[pl.ds(pl.multiple_of((1 - core) * half_rows, half_rows), half_rows), :] = theirs_ref[...].astype(f32)
-        for s in range(count):
-            placed[s * t : (s + 1) * t, :] = back[pl.ds(pl.multiple_of((neur ^ s) * t, t), t), :]
+        for i, s in enumerate(order):
+            placed[i * t : (i + 1) * t, :] = back[pl.ds(pl.multiple_of((neur ^ s) * t, t), t), :]
         turned = placed[...].T.astype(bf16)
         for k in range(depth // tile):
             cols = slice(k * tile, (k + 1) * tile)
@@ -498,42 +530,52 @@
 
         orders = [
             [s for s in range(lines)],
-            [s for s in range(lines, 2 * lines)] + [d * lines for d in range(2, places)],
-            [s for s in range(2 * lines, n_neur) if s % lines],
+            [s for s in range(lines, 2 * lines)],
+            [d * lines for d in range(2, places)],
+            [d * lines + e for e in range(1, lines) for d in range(2, places)],
         ]
+        parts = {}
         away = list(range(1, pairs_x))
-        owns, arrived, got = {}, {}, {}
+        splits = 2
+        owns, arrived, got, mine_part, kept = {}, {}, {}, {}, {}
         (bias_cols,) = bias_part(row_at, teacher_bias, width, after=(neur_at, mine_at, other_at))
         gate = (bias_cols,)
 
-        def sums(chunk, distances, keep, cost=1, through=(), plus=()):
+        def blocks_of(chunk, distance, keep, cost=1, through=(), wait=False):
             nonlocal gate
-            out = partial_sums(
+            outs = partial_sums(
                 row_at,
-                [shards[s] for s in orders[chunk]],
+                parts[chunk],
                 teacher_up,
                 width,
-                [(d, keep) for d in distances],
-                f32 if keep and distances == [0] else bf16,
-                gots=[got[chunk, d] for d in distances] if keep else (),
-                plus=plus,
+                [(distance, keep, f32 if keep and distance == 0 else bf16)],
+                gots=[got[chunk, distance]] if keep else None,
+                pieces=[kept[distance, keep]] if chunk else None,
+                retain=chunk == 0,
+                split=splits,
                 cost=cost,
                 after=gate,
                 through=through,
             )
-            gate = (out[0],)
-            for d, part in zip(distances, out):
-                if not keep:
-                    got[chunk, d] = to_core(part)
-                elif d == 0:
-                    owns[chunk] = part
+            gate = (outs[0],)
+            if keep:
+                part, *outs = outs
+                if distance == 0:
+                    owns[chunk] = [part]
+                elif wait:
+                    outs.append(part)
                 else:
-                    arrived.setdefault(chunk, []).append(flip(part, "rows", n_rows, 2 * d))
-            return out[len(distances) :]
-
-        def pin(*values):
+                    arrived.setdefault(chunk, []).append(flip(part, "rows", n_rows, 2 * distance))
+            else:
+                got[chunk, distance] = [to_core(part) for part in outs[:splits]]
+                outs = outs[splits:]
+            if chunk == 0:
+                kept[distance, keep], *outs = outs
+            return outs
+
+        def pin(*values, cost=1):
             nonlocal gate
-            token, *values = hold(*values, after=gate)
+            token, *values = hold(*values, after=gate, weight=cost)
             gate = (token,)
             return values
 
@@ -542,7 +584,7 @@
             relu, target, *passed = finish_preact(
                 neur_at,
                 bias_cols,
-                [(orders[c], owns[c], arrived[c]) for c in chunks],
+                [(orders[c], owns[c][0], arrived[c]) for c in chunks],
                 t,
                 n_neur,
                 width,
@@ -553,93 +595,95 @@
             gate = (target,)
             return (relu, target), passed
 
-        def hidden_part(chunks):
-            nonlocal gate
-            pairs = [(orders[c][k], orders[c][k + 1]) for c in chunks for k in range(0, len(orders[c]), 2)]
-            keep, send = hidden_sums(
-                row_at, shards, predictor_down, [orders[c] for c in chunks], pairs, t, after=gate
-            )
-            gate = (keep,)
-            return keep, send, pairs
-
         def along_y(d):
             for e in range(1, lines):
                 shards[d * lines + e] = flip(shards[d * lines], "neur", n_neur, e)
 
-        first_cost = 10**7
-        for d in range(places):
-            shards[d * lines] = tokens if d == 0 else flip(tokens, "neur", n_neur, d * lines)
-        along_y(0)
-        sums(0, away, False, first_cost)
-        sums(0, [0], False, first_cost)
-        (shards[lines],) = pin(shards[lines])
-        along_y(1)
-        sums(0, away, True, first_cost)
-        sums(0, [0], True, first_cost)
-        rest = [d * lines for d in range(2, places)]
-        for s, shard in zip(rest, pin(*[shards[s] for s in rest])):
-            shards[s] = shard
-        for d in range(2, places):
-            along_y(d)
-        early_keep, early_send, early_pairs = hidden_part([0, 1])
-        early_got = to_core(early_send)
+        BIG = 10**4
+        shards = [tokens]
+        shards += [flip(tokens, "neur", n_neur, e) for e in range(1, lines)]
+        near = flip(tokens, "neur", n_neur, lines)
+        (later,) = pin(tokens)
+        far = [flip(later, "neur", n_neur, d * lines) for d in range(2, places)]
+        parts[0] = shards
+        for d in away:
+            blocks_of(0, d, False, BIG)
+        blocks_of(0, 0, False, BIG)
+        (near,) = pin(near)
+        parts[1] = [near] + [flip(near, "neur", n_neur, e) for e in range(1, lines)]
+        for d in away:
+            blocks_of(0, d, True, BIG)
+        blocks_of(0, 0, True, BIG)
+        for d in away:
+            blocks_of(1, d, False)
+        (far,) = stacked(far, True, after=gate)
+        gate = (far,)
+        parts[2] = [far]
+        parts[3] = [flip(far, "neur", n_neur, e) for e in range(1, lines)]
+        blocks_of(1, 0, False)
+        for d in away:
+            blocks_of(1, d, True)
+        for d in away:
+            blocks_of(2, d, False)
         done, _ = finish([0])
-        sums(1, away, False)
-        sums(1, [0], False)
-        sums(1, away, True)
-        late_keep, late_send, late_pairs = hidden_part([2])
-        late_got = to_core(late_send)
-        sums(1, [0], True)
-        (mine,) = add_all(f32, (early_keep, early_got), (late_keep, late_got), after=gate)
+        blocks_of(1, 0, True)
+        blocks_of(2, 0, False)
+        for d in away:
+            blocks_of(2, d, True)
+        blocks_of(2, 0, True)
+        done, _ = finish([1], done)
+        pairs = [(rows_of[k], rows_of[k + 1]) for rows_of in orders for k in range(0, len(rows_of), 2)]
+        hidden_keep, hidden_send = hidden_sums(
+            row_at, [part for c in range(4) for part in parts[c]], predictor_down, orders, pairs, t, after=gate
+        )
+        gate = (hidden_keep,)
+        hidden_got = to_core(hidden_send)
+        for d in away:
+            blocks_of(3, d, False)
+        blocks_of(3, 0, False)
+        (mine,) = add_all(f32, (hidden_keep, hidden_got), after=gate)
         gate = (mine,)
         moved = flip(mine, "rows", n_rows, 2)
-        sums(2, away, False)
-        sums(2, [0], False)
-        (moved,) = pin(moved)
+        sends = [blocks_of(3, d, True, wait=True)[-1] for d in away]
+        for d, part in zip(away, blocks_of(3, 0, True, through=sends)):
+            arrived.setdefault(3, []).append(flip(part, "rows", n_rows, 2 * d))
+        done, (moved,) = finish([2], done, [moved])
         step = 4
         while step < n_rows:
             (mine,) = add_all(f32, (mine, moved))
             moved = flip(mine, "rows", n_rows, step)
             step *= 2
-        (mine,) = add_all(bf16, (mine, moved))
+        (mine,) = add_all(bf16, (mine, moved), after=gate)
+        gate = (mine,)
         column = [mine] + [flip(mine, "neur", n_neur, d * lines) for d in range(1, places)]
-        sums(2, away, True)
-        column = pin(*column)
-        (stack,) = stacked(column)
+        (stack,) = stacked(column, after=gate)
+        gate = (stack,)
         stacks = [stack] + [flip(stack, "neur", n_neur, e) for e in range(1, lines)]
         others = [to_core(part) for part in stacks]
-        sums(2, [0], True, through=())
-        done, _ = finish([1], done)
-        (teacher_relu, target), _ = finish([2], done)
-        (hidden,) = assemble_hidden(
-            mine_at, [(early_pairs + late_pairs, stacks, others)], places, lines, t, rank, after=gate
+        (teacher_relu, target), _ = finish([3], done)
+        (hidden,) = assemble_hidden(mine_at, [(pairs, stacks, others)], places, lines, t, rank, after=gate)
+
+        half, send = residue_and_back(
+            other_at, hidden, target, predictor_up, places, lines, half_rows, rank, bf16
         )
-
-        def half_of(at, dtype, after):
-            return residue_and_back(
-                at, hidden, target, predictor_up, places, lines, half_rows, rank, dtype, after=after
-            )
-
-        residue_other, send = half_of(other_at, bf16, ())
-        residue_mine, kept_back = half_of(mine_at, f32, (send,))
-        total = kept_back + to_core(send)
-        gots = [
-            flip(total[e * places : (e + 1) * places].astype(bf16), "neur", n_neur, e) for e in range(1, lines)
-        ]
-        swap = core == 0
-        residue = jnp.concatenate(
-            [jnp.where(swap, residue_mine, residue_other), jnp.where(swap, residue_other, residue_mine)]
+        residue, kept_back = residue_and_back(
+            mine_at, hidden, target, predictor_up, places, lines, half_rows, rank, f32, half
         )
+        back, *aways = add_lines(kept_back, to_core(send), places, lines)
+        gots = [flip(value, "neur", n_neur, e + 1) for e, value in enumerate(aways)]
         grad_up = jnp.einsum("tr,tf->rf", hidden, residue, preferred_element_type=f32)
-        back, away = add_lines(total[:places], gots, places, after=(grad_up,))
-        for d in range(1, places):
-            back = back + flip(away[d - 1], "neur", n_neur, d * lines)
+        back, *aways = add_places(back, gots, places, after=(grad_up,))
+        gots = [flip(value, "neur", n_neur, (d + 1) * lines) for d, value in enumerate(aways)]
+        (back,) = add_all(f32, (back, *gots))
         step = 2
         while step < n_rows:
-            back = back + flip(back, "rows", n_rows, step)
+            other = flip(back.astype(bf16), "rows", n_rows, step)
+            back = back.astype(bf16).astype(f32) + other
             step *= 2
         back = back.astype(bf16)
-        grad_down = down_gradient(mine_at, [shards[s] for s in range(n_neur)], back, to_core(back), t)
+        grad_down = down_gradient(
+            mine_at, [part for c in range(4) for part in parts[c]], [s for c in orders for s in c], back, to_core(back), t
+        )
         return (teacher_relu, grad_down, grad_up)
 
     return body

time: 163 us -> 134 us (0.82)
  Pallas kernels: 82.1 us -> 55 us
  waiting for transfers between devices: 42.2 us -> 33.1 us
  starting transfers between devices: 29.9 us -> 36.5 us
  local copies, waits for them, and re-layouts: 4.48 us -> 6.12 us
    pallas_call x30 -> x35, Pallas kernels: 82.1 us -> 55 us  [call(): pl.pallas_call(body, out_shape=tuple(outs), in_specs=[spot(space) for spa...]
    ppermute x32 -> x41, waiting for transfers between devices: 42.2 us -> 33.1 us  [flip(): return lax.ppermute(value, axis, [(i, i ^ distance) for i in range(size)])]
    ppermute x32 -> x41, starting transfers between devices: 29.9 us -> 36.5 us  [flip(): return lax.ppermute(value, axis, [(i, i ^ distance) for i in range(size)])]
    unnamed x41 -> x34, local copies, waits for them, and re-layouts: 4.39 us -> 6.12 us
  transfers between devices with their start and end apart: 32 -> 41, of which waited for: 13 -> 10; matrix products, arithmetic and copies ran while one was open for 1% -> 3% of each run, Pallas kernels for 40% -> 36%
where the time goes in v2:
time: 134 us
  Pallas kernels  55 us (41%)
  starting transfers between devices  36.5 us (27%)
  waiting for transfers between devices  33.1 us (25%)
  local copies, waits for them, and re-layouts  6.12 us (5%)
  matrix products  1.84 us (1%)
    pallas_call x35, Pallas kernels, call(): pl.pallas_call(body, out_shape=tuple(outs), in_specs=[spot(space) for spa...  55 us
    ppermute x41, starting transfers between devices, flip(): return lax.ppermute(value, axis, [(i, i ^ distance) for i in range(size)])  36.5 us
    ppermute x41, waiting for transfers between devices, flip(): return lax.ppermute(value, axis, [(i, i ^ distance) for i in range(size)])  33.1 us
    unnamed x34, local copies, waits for them, and re-layouts  6.12 us
  transfers between devices with their start and end apart: 41, of which 10 were waited for; matrix products, arithmetic and copies ran while one was open for 3% of the time, Pallas kernels for 36%

profile of v2, /device:TPU:0, one launch (start us, length us, event | category | flops | bytes accessed | tf_op | source)
XLA Modules:
  0.0 133.8 jit_solution(5504618720184243343)
XLA Ops:
  0.6 3.0 %collective-permute-start.3 = (bf16[64,3072]{1,0:T(8,128)(2,1)}, bf16[64,3072]{1,0:T(8,128)(2,1)S(1)}, u32[]{:S(2)}, u32[]{:S(2)}) collective-permute-start(bf16[64,3072]{1,0:T(8,128)(2,1)} %refs_3_.9), channel_id=1, source_target_pairs={{0,1},{1,0},{2,3},{3,2},{4,5},{5,4},{6,7},{7,6},{8,9},{9,8},{10,11... | collective-permute-start | bytes 1179656 | tf_op jit(solution)/shard_map/ppermute | solution.py:14
  7.9 2.6 %collective-permute-start = (bf16[64,3072]{1,0:T(8,128)(2,1)}, bf16[64,3072]{1,0:T(8,128)(2,1)S(1)}, u32[]{:S(2)}, u32[]{:S(2)}) collective-permute-start(bf16[64,3072]{1,0:T(8,128)(2,1)} %get-tuple-element.52), channel_id=1, source_target_pairs={{0,4},{1,5},{2,6},{3,7},{4,0},{5,1},{6,2},{7,3},{8,12},{9,13},{10,... | collective-permute-start | bytes 1179656 | tf_op jit(solution)/shard_map/ppermute | solution.py:14
  10.7 2.3 %collective-permute-done.3.refs_2_.refs_3_.refs_4_ = bf16[64,3072]{1,0:T(8,128)(2,1)S(1)} collective-permute-done((bf16[64,3072]{1,0:T(8,128)(2,1)}, bf16[64,3072]{1,0:T(8,128)(2,1)S(1)}, u32[]{:S(2)}, u32[]{:S(2)}) %collective-permute-start.3) | collective-permute-done | bytes 393248 | tf_op jit(solution)/shard_map/ppermute | solution.py:14
  14.1 4.7 %shard_map.78 = (bf16[64,1536]{1,0:T(8,128)(2,1)S(1)}, bf16[64,1536]{1,0:T(8,128)(2,1)S(1)}, bf16[3072,1536]{1,0:T(8,128)(2,1)S(1)}) custom-call(s32[1]{0:T(128)} %bitcast.1.refs_0_, bf16[64,3072]{1,0:T(8,128)(2,1)S(1)} %copy-done.4, bf16[64,3072]{1,0:T(8,128)(2,1)S(1)} %collective-permute-done.3.refs_2_.refs_3_.refs_4_, bf16[3072,6144]{1,0:T(8,128)(2,1)} %refs_5_.3, ...), custom_call_target="tpu_custom_call" | custom-call | flops 10000000000 | bytes 1000 | tf_op jit(solution)/shard_map/pallas_call | solution.py:173
  20.4 4.7 %shard_map.79 = (bf16[64,1536]{1,0:T(8,128)(2,1)S(1)}, bf16[64,1536]{1,0:T(8,128)(2,1)S(1)}, bf16[3072,1536]{1,0:T(8,128)(2,1)S(1)}) custom-call(s32[1]{0:T(128)} %bitcast.1.refs_0_, bf16[64,3072]{1,0:T(8,128)(2,1)S(1)} %copy-done.5, bf16[64,3072]{1,0:T(8,128)(2,1)S(1)} %copy-done.7, bf16[3072,6144]{1,0:T(8,128)(2,1)} %refs_5_.3, ...), custom_call_target="tpu_custom_call" | custom-call | flops 10000000000 | bytes 1000 | tf_op jit(solution)/shard_map/pallas_call | solution.py:173
  27.4 4.6 %shard_map.81 = (bf16[128,1536]{1,0:T(8,128)(2,1)S(1)}, bf16[3072,1536]{1,0:T(8,128)(2,1)S(1)}) custom-call(s32[1]{0:T(128)} %bitcast.1.refs_0_, bf16[64,3072]{1,0:T(8,128)(2,1)S(1)} %copy-done.5, bf16[64,3072]{1,0:T(8,128)(2,1)S(1)} %copy-done.8, bf16[64,1536]{1,0:T(8,128)(2,1)S(1)} %collective-permute-done.7.refs_3_, ...), custom_call_target="tpu_custom_call" | custom-call | flops 10000000000 | bytes 1000 | tf_op jit(solution)/shard_map/pallas_call | solution.py:173
  33.7 4.6 %shard_map.82 = (f32[128,1536]{1,0:T(8,128)S(1)}, bf16[3072,1536]{1,0:T(8,128)(2,1)S(1)}) custom-call(s32[1]{0:T(128)} %bitcast.1.refs_0_, bf16[64,3072]{1,0:T(8,128)(2,1)S(1)} %copy-done.5, bf16[64,3072]{1,0:T(8,128)(2,1)S(1)} %copy-done.8, bf16[64,1536]{1,0:T(8,128)(2,1)S(1)} %collective-permute-done.5.refs_3_, ...), custom_call_target="tpu_custom_call" | custom-call | flops 10000000000 | bytes 1000 | tf_op jit(solution)/shard_map/pallas_call | solution.py:173
  38.3 2.6 %shard_map.83 = (bf16[64,1536]{1,0:T(8,128)(2,1)S(1)}, bf16[64,1536]{1,0:T(8,128)(2,1)S(1)}) custom-call(s32[1]{0:T(128)} %bitcast.1.refs_0_, bf16[64,3072]{1,0:T(8,128)(2,1)} %get-tuple-element.56.refs_1_.refs_4_.refs_5_, bf16[64,3072]{1,0:T(8,128)(2,1)S(1)} %collective-permute-done.4.refs_2_.refs_5_.refs_6_, ...), custom_call_target="tpu_custom_call" | custom-call | flops 1000000 | bytes 1000 | tf_op jit(solution)/shard_map/pallas_call | solution.py:173
  42.1 2.4 %shard_map.85 = (bf16[64,1536]{1,0:T(8,128)(2,1)S(1)}, bf16[64,1536]{1,0:T(8,128)(2,1)S(1)}) custom-call(s32[1]{0:T(128)} %bitcast.1.refs_0_, bf16[64,3072]{1,0:T(8,128)(2,1)} %get-tuple-element.56.refs_1_.refs_4_.refs_5_, bf16[64,3072]{1,0:T(8,128)(2,1)S(1)} %collective-permute-done.4.refs_2_.refs_5_.refs_6_, ...), custom_call_target="tpu_custom_call" | custom-call | flops 1000000 | bytes 1000 | tf_op jit(solution)/shard_map/pallas_call | solution.py:173
  45.1 2.4 %shard_map.86.refs_3_ = bf16[128,1536]{1,0:T(8,128)(2,1)S(1)} custom-call(s32[1]{0:T(128)} %bitcast.1.refs_0_, bf16[64,3072]{1,0:T(8,128)(2,1)} %get-tuple-element.56.refs_1_.refs_4_.refs_5_, bf16[64,3072]{1,0:T(8,128)(2,1)S(1)} %collective-permute-done.4.refs_2_.refs_5_.refs_6_, bf16[64,1536]{1,0:T(8,128)(2,1)S(1)} %collective-permute-done.13.refs_3_, ...), custom_call_target="tpu_custom_call" | custom-call | flops 1000000 | bytes 1000 | tf_op jit(solution)/shard_map/pallas_call | solution.py:173
  51.6 2.4 %shard_map.89.refs_3_.refs_2_ = f32[128,1536]{1,0:T(8,128)S(1)} custom-call(s32[1]{0:T(128)} %bitcast.1.refs_0_, bf16[64,3072]{1,0:T(8,128)(2,1)} %get-tuple-element.56.refs_1_.refs_4_.refs_5_, bf16[64,3072]{1,0:T(8,128)(2,1)S(1)} %collective-permute-done.4.refs_2_.refs_5_.refs_6_, bf16[64,1536]{1,0:T(8,128)(2,1)S(1)} %collective-permute-done.10.refs_3_, ...), custom_call_target="tpu_custom_call" | custom-call | flops 1000000 | bytes 1000 | tf_op jit(solution)/shard_map/pallas_call | solution.py:173
  61.8 2.0 %shard_map.94 = (f32[256,128]{1,0:T(8,128)S(1)}, f32[256,128]{1,0:T(8,128)S(1)}) custom-call(s32[1]{0:T(128)} %bitcast.1.refs_0_, bf16[3072,128]{1,0:T(8,128)(2,1)S(1)} %copy-done.14, bf16[64,3072]{1,0:T(8,128)(2,1)S(1)} %copy-done.5, bf16[64,3072]{1,0:T(8,128)(2,1)S(1)} %copy-done.8, bf16[64,3072]{1,0:T(8,128)(2,1)} %get-tuple-element.56.refs_1_.refs_4_.refs_5_, ...), custom_call_target="tpu_custom_call" | custom-call | flops 1000000 | bytes 1000 | tf_op jit(solution)/shard_map/pallas_call | solution.py:173
  67.9 2.0 %collective-permute-start.27 = (f32[256,128]{1,0:T(8,128)S(1)}, f32[256,128]{1,0:T(8,128)S(1)}, u32[]{:S(2)}, u32[]{:S(2)}) collective-permute-start(f32[256,128]{1,0:T(8,128)S(1)} %shard_map.97.refs_5_.refs_0_), channel_id=1, source_target_pairs={{0,16},{8,24},{16,0},{24,8},{1,17},{9,25},{17,1},{25,9},{2,18},{10... | collective-permute-start | bytes 393224 | tf_op jit(solution)/shard_map/ppermute | solution.py:14
  74.9 4.3 %collective-permute-start.28 = (bf16[256,128]{1,0:T(8,128)(2,1)S(1)}, bf16[256,128]{1,0:T(8,128)(2,1)S(1)}, u32[]{:S(2)}, u32[]{:S(2)}) collective-permute-start(bf16[256,128]{1,0:T(8,128)(2,1)S(1)} %shard_map.101.refs_0_.refs_4_), channel_id=1, source_target_pairs={{0,2},{1,3},{2,0},{3,1},{4,6},{5,7},{6,4},{7,5},{8,10},{9,11},{10,... | collective-permute-start | bytes 196616 | tf_op jit(solution)/shard_map/ppermute | solution.py:14
  81.7 5.4 %collective-permute-done.29.refs_2_ = bf16[256,128]{1,0:T(8,128)(2,1)S(1)} collective-permute-done((bf16[256,128]{1,0:T(8,128)(2,1)S(1)}, bf16[256,128]{1,0:T(8,128)(2,1)S(1)}, u32[]{:S(2)}, u32[]{:S(2)}) %collective-permute-start.29) | collective-permute-done | bytes 65568 | tf_op jit(solution)/shard_map/ppermute | solution.py:14
  90.4 3.4 %collective-permute-done.31.refs_2_ = bf16[4,256,128]{2,1,0:T(8,128)(2,1)S(1)} collective-permute-done((bf16[4,256,128]{2,1,0:T(8,128)(2,1)S(1)}, bf16[4,256,128]{2,1,0:T(8,128)(2,1)S(1)}, u32[]{:S(2)}, u32[]{:S(2)}) %collective-permute-start.31) | collective-permute-done | bytes 262176 | tf_op jit(solution)/shard_map/ppermute | solution.py:14
  93.8 4.1 %collective-permute-done.25.refs_3_ = bf16[128,1536]{1,0:T(8,128)(2,1)S(1)} collective-permute-done((bf16[128,1536]{1,0:T(8,128)(2,1)S(1)}, bf16[128,1536]{1,0:T(8,128)(2,1)S(1)}, u32[]{:S(2)}, u32[]{:S(2)}) %collective-permute-start.25) | collective-permute-done | bytes 393248 | tf_op jit(solution)/shard_map/ppermute | solution.py:14
  100.6 2.7 %shard_map.105 = (bf16[512,1536]{1,0:T(8,128)(2,1)S(1)}, bf16[8,256,128]{2,1,0:T(8,128)(2,1)S(1)}) custom-call(s32[2]{0:T(128)S(1)} %get-tuple-element.102.refs_4_.refs_0_, bf16[512,1024]{1,0:T(8,128)(2,1)S(1)} %shard_map.104.refs_1_, f32[512,1536]{1,0:T(8,128)S(1)} %get-tuple-element.90.refs_5_.refs_2_, bf16[1024,1536]{1,0:T(8,128)(2,1)S(1)} %copy-done.12), custom_call_target="tpu_custom_call" | custom-call | flops 1000000 | bytes 1000 | tf_op jit(solution)/shard_map/pallas_call | solution.py:173
  103.4 2.9 %shard_map.106 = (bf16[512,1536]{1,0:T(8,128)(2,1)S(1)}, f32[8,256,128]{2,1,0:T(8,128)S(1)}) custom-call(s32[2]{0:T(128)S(1)} %get-tuple-element.101.refs_3_.refs_0_, bf16[512,1024]{1,0:T(8,128)(2,1)S(1)} %shard_map.104.refs_1_, f32[512,1536]{1,0:T(8,128)S(1)} %get-tuple-element.90.refs_5_.refs_2_, ...), custom_call_target="tpu_custom_call", output_to_operand_aliasing={{0}: (4, {})} | custom-call | flops 1000000 | bytes 1000 | tf_op jit(solution)/shard_map/pallas_call | solution.py:173
  108.9 6.4 %collective-permute-done.35.refs_1_ = bf16[4,256,128]{2,1,0:T(8,128)(2,1)S(1)} collective-permute-done((bf16[4,256,128]{2,1,0:T(8,128)(2,1)S(1)}, bf16[4,256,128]{2,1,0:T(8,128)(2,1)S(1)}, u32[]{:S(2)}, u32[]{:S(2)}) %collective-permute-start.35) | collective-permute-done | bytes 262176 | tf_op jit(solution)/shard_map/ppermute | solution.py:14
  115.3 2.0 %collective-permute-start.36 = (bf16[256,128]{1,0:T(8,128)(2,1)S(1)}, bf16[256,128]{1,0:T(8,128)(2,1)S(1)}, u32[]{:S(2)}, u32[]{:S(2)}) collective-permute-start(bf16[256,128]{1,0:T(8,128)(2,1)S(1)} %get-tuple-element.98), channel_id=1, source_target_pairs={{0,2},{1,3},{2,0},{3,1},{4,6},{5,7},{6,4},{7,5},{8,10},{9,11},{10,... | collective-permute-start | bytes 196616 | tf_op jit(solution)/shard_map/ppermute | solution.py:14
  119.8 5.4 %collective-permute-done.37.refs_2_ = bf16[256,128]{1,0:T(8,128)(2,1)S(1)} collective-permute-done((bf16[256,128]{1,0:T(8,128)(2,1)S(1)}, bf16[256,128]{1,0:T(8,128)(2,1)S(1)}, u32[]{:S(2)}, u32[]{:S(2)}) %collective-permute-start.37) | collective-permute-done | bytes 65568 | tf_op jit(solution)/shard_map/ppermute | solution.py:14
  126.7 2.8 %collective-permute-done.39 = bf16[256,128]{1,0:T(8,128)(2,1)S(1)} collective-permute-done((bf16[256,128]{1,0:T(8,128)(2,1)S(1)}, bf16[256,128]{1,0:T(8,128)(2,1)S(1)}, u32[]{:S(2)}, u32[]{:S(2)}) %collective-permute-start.39) | collective-permute-done | bytes 65568 | tf_op jit(solution)/shard_map/ppermute | solution.py:14
  130.9 2.9 %shard_map.110 = f32[3072,128]{1,0:T(8,128)} custom-call(s32[2]{0:T(128)S(1)} %get-tuple-element.101.refs_3_.refs_0_, bf16[256,128]{1,0:T(8,128)(2,1)S(1)} %add_convert_fusion.refs_1_, bf16[256,128]{1,0:T(8,128)(2,1)S(1)} %collective-permute-done.40.refs_2_, bf16[64,3072]{1,0:T(8,128)(2,1)S(1)} %copy-done.5, bf16[64,3072]{1,0:T(8,128)(2,1)S(1)} %copy-done.9, ...), custom_call_target="tpu_custom_call" | custom-call | flops 1000000 | bytes 1000 | tf_op jit(solution)/shard_map/pallas_call | solution.py:173
  (131 shorter events, 50.0 us)
Async XLA Ops:
  0.6 12.4 %collective-permute-start.3 = (bf16[64,3072]{1,0:T(8,128)(2,1)}, bf16[64,3072]{1,0:T(8,128)(2,1)S(1)}, u32[]{:S(2)}, u32[]{:S(2)}) collective-permute-start(bf16[64,3072]{1,0:T(8,128)(2,1)} %refs_3_.9), channel_id=1, source_target_pairs={{0,1},{1,0},{2,3},{3,2},{4,5},{5,4},{6,7},{7,6},{8,9},{9,8},{10,11... | collective-permute-start | bytes 1179656 | tf_op jit(solution)/shard_map/ppermute | solution.py:14
  3.7 21.4 %collective-permute-start.2 = (bf16[64,3072]{1,0:T(8,128)(2,1)}, bf16[64,3072]{1,0:T(8,128)(2,1)}, u32[]{:S(2)}, u32[]{:S(2)}) collective-permute-start(bf16[64,3072]{1,0:T(8,128)(2,1)} %refs_3_.9), channel_id=1, source_target_pairs={{0,2},{1,3},{2,0},{3,1},{4,6},{5,7},{6,4},{7,5},{8,10},{9,11},{10,... | collective-permute-start | bytes 1179656 | tf_op jit(solution)/shard_map/ppermute | solution.py:14
  7.9 33.0 %collective-permute-start = (bf16[64,3072]{1,0:T(8,128)(2,1)}, bf16[64,3072]{1,0:T(8,128)(2,1)S(1)}, u32[]{:S(2)}, u32[]{:S(2)}) collective-permute-start(bf16[64,3072]{1,0:T(8,128)(2,1)} %get-tuple-element.52), channel_id=1, source_target_pairs={{0,4},{1,5},{2,6},{3,7},{4,0},{5,1},{6,2},{7,3},{8,12},{9,13},{10,... | collective-permute-start | bytes 1179656 | tf_op jit(solution)/shard_map/ppermute | solution.py:14
  10.4 30.5 %collective-permute-start.1 = (bf16[64,3072]{1,0:T(8,128)(2,1)}, bf16[64,3072]{1,0:T(8,128)(2,1)S(1)}, u32[]{:S(2)}, u32[]{:S(2)}) collective-permute-start(bf16[64,3072]{1,0:T(8,128)(2,1)} %get-tuple-element.52), channel_id=1, source_target_pairs={{0,6},{1,7},{2,4},{3,5},{4,2},{5,3},{6,0},{7,1},{8,14},{9,15},{10,... | collective-permute-start | bytes 1179656 | tf_op jit(solution)/shard_map/ppermute | solution.py:14
  18.8 6.4 %collective-permute-start.7 = (bf16[64,1536]{1,0:T(8,128)(2,1)S(1)}, bf16[64,1536]{1,0:T(8,128)(2,1)S(1)}, u32[]{:S(2)}, u32[]{:S(2)}) collective-permute-start(bf16[64,1536]{1,0:T(8,128)(2,1)S(1)} %get-tuple-element.54.refs_4_), channel_id=1, source_target_pairs={{0,8},{8,0},{16,24},{24,16},{1,9},{9,1},{17,25},{25,17},{2,10},{10... | collective-permute-start | bytes 589832 | tf_op jit(solution)/shard_map/ppermute | solution.py:14
  18.9 6.8 %collective-permute-start.8 = (bf16[64,1536]{1,0:T(8,128)(2,1)S(1)}, bf16[64,1536]{1,0:T(8,128)(2,1)S(1)}, u32[]{:S(2)}, u32[]{:S(2)}) collective-permute-start(bf16[64,1536]{1,0:T(8,128)(2,1)S(1)} %get-tuple-element.59), channel_id=1, source_target_pairs={{0,8},{8,0},{16,24},{24,16},{1,9},{9,1},{17,25},{25,17},{2,10},{10... | collective-permute-start | bytes 589832 | tf_op jit(solution)/shard_map/ppermute | solution.py:14
  25.1 7.0 %collective-permute-start.5 = (bf16[64,1536]{1,0:T(8,128)(2,1)S(1)}, bf16[64,1536]{1,0:T(8,128)(2,1)S(1)}, u32[]{:S(2)}, u32[]{:S(2)}) collective-permute-start(bf16[64,1536]{1,0:T(8,128)(2,1)S(1)} %get-tuple-element.55.refs_1_), channel_id=1, source_target_pairs={{0,8},{8,0},{16,24},{24,16},{1,9},{9,1},{17,25},{25,17},{2,10},{10... | collective-permute-start | bytes 589832 | tf_op jit(solution)/shard_map/ppermute | solution.py:14
  25.3 8.4 %collective-permute-start.6 = (bf16[64,1536]{1,0:T(8,128)(2,1)S(1)}, bf16[64,1536]{1,0:T(8,128)(2,1)S(1)}, u32[]{:S(2)}, u32[]{:S(2)}) collective-permute-start(bf16[64,1536]{1,0:T(8,128)(2,1)S(1)} %get-tuple-element.58), channel_id=1, source_target_pairs={{0,8},{8,0},{16,24},{24,16},{1,9},{9,1},{17,25},{25,17},{2,10},{10... | collective-permute-start | bytes 589832 | tf_op jit(solution)/shard_map/ppermute | solution.py:14
  25.7 12.6 %collective-permute-start.4 = (bf16[64,3072]{1,0:T(8,128)(2,1)}, bf16[64,3072]{1,0:T(8,128)(2,1)S(1)}, u32[]{:S(2)}, u32[]{:S(2)}) collective-permute-start(bf16[64,3072]{1,0:T(8,128)(2,1)} %get-tuple-element.56.refs_1_.refs_4_.refs_5_), channel_id=1, source_target_pairs={{0,1},{1,0},{2,3},{3,2},{4,5},{5,4},{6,7},{7,6},{8,9},{9,8},{10,11... | collective-permute-start | bytes 1179656 | tf_op jit(solution)/shard_map/ppermute | solution.py:14
  32.1 17.0 %collective-permute-start.12 = (bf16[128,1536]{1,0:T(8,128)(2,1)S(1)}, bf16[128,1536]{1,0:T(8,128)(2,1)S(1)}, u32[]{:S(2)}, u32[]{:S(2)}) collective-permute-start(bf16[128,1536]{1,0:T(8,128)(2,1)S(1)} %get-tuple-element.61.refs_6_), channel_id=1, source_target_pairs={{0,16},{8,24},{16,0},{24,8},{1,17},{9,25},{17,1},{25,9},{2,18},{10... | collective-permute-start | bytes 1179656 | tf_op jit(solution)/shard_map/ppermute | solution.py:14
  41.0 20.4 %collective-permute-start.9 = (bf16[128,3072]{1,0:T(8,128)(2,1)S(1)}, bf16[128,3072]{1,0:T(8,128)(2,1)S(1)}, u32[]{:S(2)}, u32[]{:S(2)}) collective-permute-start(bf16[128,3072]{1,0:T(8,128)(2,1)S(1)} %shard_map.84.refs_4_.refs_1_.refs_6_.refs_7_), channel_id=1, source_target_pairs={{0,1},{1,0},{2,3},{3,2},{4,5},{5,4},{6,7},{7,6},{8,9},{9,8},{10,11... | collective-permute-start | bytes 2359304 | tf_op jit(solution)/shard_map/ppermute | solution.py:14
  44.6 7.0 %collective-permute-start.11 = (bf16[64,1536]{1,0:T(8,128)(2,1)S(1)}, bf16[64,1536]{1,0:T(8,128)(2,1)S(1)}, u32[]{:S(2)}, u32[]{:S(2)}) collective-permute-start(bf16[64,1536]{1,0:T(8,128)(2,1)S(1)} %get-tuple-element.66), channel_id=1, source_target_pairs={{0,8},{8,0},{16,24},{24,16},{1,9},{9,1},{17,25},{25,17},{2,10},{10... | collective-permute-start | bytes 589832 | tf_op jit(solution)/shard_map/ppermute | solution.py:14
  48.9 7.1 %collective-permute-start.18 = (bf16[64,1536]{1,0:T(8,128)(2,1)S(1)}, bf16[64,1536]{1,0:T(8,128)(2,1)S(1)}, u32[]{:S(2)}, u32[]{:S(2)}) collective-permute-start(bf16[64,1536]{1,0:T(8,128)(2,1)S(1)} %get-tuple-element.70.refs_4_), channel_id=1, source_target_pairs={{0,8},{8,0},{16,24},{24,16},{1,9},{9,1},{17,25},{25,17},{2,10},{10... | collective-permute-start | bytes 589832 | tf_op jit(solution)/shard_map/ppermute | solution.py:14
  49.1 11.5 %collective-permute-start.15 = (bf16[128,1536]{1,0:T(8,128)(2,1)S(1)}, bf16[128,1536]{1,0:T(8,128)(2,1)S(1)}, u32[]{:S(2)}, u32[]{:S(2)}) collective-permute-start(bf16[128,1536]{1,0:T(8,128)(2,1)S(1)} %shard_map.86.refs_3_), channel_id=1, source_target_pairs={{0,16},{8,24},{16,0},{24,8},{1,17},{9,25},{17,1},{25,9},{2,18},{10... | collective-permute-start | bytes 1179656 | tf_op jit(solution)/shard_map/ppermute | solution.py:14
  57.6 15.2 %collective-permute-start.26 = (bf16[128,1536]{1,0:T(8,128)(2,1)S(1)}, bf16[128,1536]{1,0:T(8,128)(2,1)S(1)}, u32[]{:S(2)}, u32[]{:S(2)}) collective-permute-start(bf16[128,1536]{1,0:T(8,128)(2,1)S(1)} %shard_map.91.refs_5_), channel_id=1, source_target_pairs={{0,16},{8,24},{16,0},{24,8},{1,17},{9,25},{17,1},{25,9},{2,18},{10... | collective-permute-start | bytes 1179656 | tf_op jit(solution)/shard_map/ppermute | solution.py:14
  74.9 6.8 %collective-permute-start.28 = (bf16[256,128]{1,0:T(8,128)(2,1)S(1)}, bf16[256,128]{1,0:T(8,128)(2,1)S(1)}, u32[]{:S(2)}, u32[]{:S(2)}) collective-permute-start(bf16[256,128]{1,0:T(8,128)(2,1)S(1)} %shard_map.101.refs_0_.refs_4_), channel_id=1, source_target_pairs={{0,2},{1,3},{2,0},{3,1},{4,6},{5,7},{6,4},{7,5},{8,10},{9,11},{10,... | collective-permute-start | bytes 196616 | tf_op jit(solution)/shard_map/ppermute | solution.py:14
  79.3 7.9 %collective-permute-start.29 = (bf16[256,128]{1,0:T(8,128)(2,1)S(1)}, bf16[256,128]{1,0:T(8,128)(2,1)S(1)}, u32[]{:S(2)}, u32[]{:S(2)}) collective-permute-start(bf16[256,128]{1,0:T(8,128)(2,1)S(1)} %shard_map.101.refs_0_.refs_4_), channel_id=1, source_target_pairs={{0,4},{1,5},{2,6},{3,7},{4,0},{5,1},{6,2},{7,3},{8,12},{9,13},{10,... | collective-permute-start | bytes 196616 | tf_op jit(solution)/shard_map/ppermute | solution.py:14
  80.3 6.8 %collective-permute-start.30 = (bf16[256,128]{1,0:T(8,128)(2,1)S(1)}, bf16[256,128]{1,0:T(8,128)(2,1)S(1)}, u32[]{:S(2)}, u32[]{:S(2)}) collective-permute-start(bf16[256,128]{1,0:T(8,128)(2,1)S(1)} %shard_map.101.refs_0_.refs_4_), channel_id=1, source_target_pairs={{0,6},{1,7},{2,4},{3,5},{4,2},{5,3},{6,0},{7,1},{8,14},{9,15},{10,... | collective-permute-start | bytes 196616 | tf_op jit(solution)/shard_map/ppermute | solution.py:14
  87.2 6.6 %collective-permute-start.31 = (bf16[4,256,128]{2,1,0:T(8,128)(2,1)S(1)}, bf16[4,256,128]{2,1,0:T(8,128)(2,1)S(1)}, u32[]{:S(2)}, u32[]{:S(2)}) collective-permute-start(bf16[4,256,128]{2,1,0:T(8,128)(2,1)S(1)} %shard_map.102.refs_6_.refs_1_), channel_id=1, source_target_pairs={{0,1},{1,0},{2,3},{3,2},{4,5},{5,4},{6,7},{7,6},{8,9},{9,8},{10,11... | collective-permute-start | bytes 786440 | tf_op jit(solution)/shard_map/ppermute | solution.py:14
  88.8 9.1 %collective-permute-start.25 = (bf16[128,1536]{1,0:T(8,128)(2,1)S(1)}, bf16[128,1536]{1,0:T(8,128)(2,1)S(1)}, u32[]{:S(2)}, u32[]{:S(2)}) collective-permute-start(bf16[128,1536]{1,0:T(8,128)(2,1)S(1)} %get-tuple-element.84), channel_id=1, source_target_pairs={{0,16},{8,24},{16,0},{24,8},{1,17},{9,25},{17,1},{25,9},{2,18},{10... | collective-permute-start | bytes 1179656 | tf_op jit(solution)/shard_map/ppermute | solution.py:14
  90.4 8.4 %collective-permute-start.32 = (bf16[4,256,128]{2,1,0:T(8,128)(2,1)S(1)}, bf16[4,256,128]{2,1,0:T(8,128)(2,1)S(1)}, u32[]{:S(2)}, u32[]{:S(2)}) collective-permute-start(bf16[4,256,128]{2,1,0:T(8,128)(2,1)S(1)} %shard_map.102.refs_6_.refs_1_), channel_id=1, source_target_pairs={{0,8},{8,0},{16,24},{24,16},{1,9},{9,1},{17,25},{25,17},{2,10},{10... | collective-permute-start | bytes 786440 | tf_op jit(solution)/shard_map/ppermute | solution.py:14
  106.5 8.8 %collective-permute-start.35 = (bf16[4,256,128]{2,1,0:T(8,128)(2,1)S(1)}, bf16[4,256,128]{2,1,0:T(8,128)(2,1)S(1)}, u32[]{:S(2)}, u32[]{:S(2)}) collective-permute-start(bf16[4,256,128]{2,1,0:T(8,128)(2,1)S(1)} %get-tuple-element.95), channel_id=1, source_target_pairs={{0,1},{1,0},{2,3},{3,2},{4,5},{5,4},{6,7},{7,6},{8,9},{9,8},{10,11... | collective-permute-start | bytes 786440 | tf_op jit(solution)/shard_map/ppermute | solution.py:14
  117.3 7.8 %collective-permute-start.37 = (bf16[256,128]{1,0:T(8,128)(2,1)S(1)}, bf16[256,128]{1,0:T(8,128)(2,1)S(1)}, u32[]{:S(2)}, u32[]{:S(2)}) collective-permute-start(bf16[256,128]{1,0:T(8,128)(2,1)S(1)} %get-tuple-element.99), channel_id=1, source_target_pairs={{0,4},{1,5},{2,6},{3,7},{4,0},{5,1},{6,2},{7,3},{8,12},{9,13},{10,... | collective-permute-start | bytes 196616 | tf_op jit(solution)/shard_map/ppermute | solution.py:14
  118.2 6.9 %collective-permute-start.38 = (bf16[256,128]{1,0:T(8,128)(2,1)S(1)}, bf16[256,128]{1,0:T(8,128)(2,1)S(1)}, u32[]{:S(2)}, u32[]{:S(2)}) collective-permute-start(bf16[256,128]{1,0:T(8,128)(2,1)S(1)} %get-tuple-element.100), channel_id=1, source_target_pairs={{0,6},{1,7},{2,4},{3,5},{4,2},{5,3},{6,0},{7,1},{8,14},{9,15},{10,... | collective-permute-start | bytes 196616 | tf_op jit(solution)/shard_map/ppermute | solution.py:14
  (33 other events, 212.4 us)

commit v3 on v2

--- a/solution.py
+++ b/solution.py
@@ -156,7 +156,7 @@
     return jax.ShapeDtypeStruct(shape, dtype)
 
 
-def call(kernel, outs, ins, spaces, scratch=(), mib=12, after=(), through=(), weight=1, aliases=None, out_spaces=None):
+def call(kernel, outs, ins, spaces, scratch=(), mib=12, after=(), through=(), weight=10**4, aliases=None, out_spaces=None):
     outs = list(outs)
     out_spaces = list(out_spaces or [pltpu.VMEM] * len(outs))
     passed = list(through)
@@ -218,19 +218,20 @@
     return jnp.concatenate([ref[:, cols] for ref in refs]) if len(refs) > 1 else refs[0][:, cols]
 
 
-def partial_sums(row, parts, weight, width, blocks, gots=None, pieces=None, retain=False, split=1, cost=1, **order):
+def partial_sums(row, parts, weight, width, blocks, gots=None, pieces=None, retain=False, split=1, cost=10**4, **order):
     rows = sum(part.shape[0] for part in parts)
     depth = weight.shape[0]
     tile = tile_of(width)
     per = width // tile
     tiles = len(blocks) * per
     slots, ahead = min(tiles, 3), min(tiles, 2)
+    cuts = 4 if depth % 64 == 0 else 1
     gots = gots or []
     flat = [part for listed in gots for part in listed]
     splits = [1 if keep else split for _, keep, _ in blocks]
     starts = [sum(splits[:k]) for k in range(len(blocks) + 1)]
     loads = pieces is None
-    ins = [row, *parts, *flat] + ([pltpu.with_memory_space_constraint(weight, pltpu.HBM)] if loads else [held(piece) for piece in pieces])
+    ins = [row, *[held(part) for part in parts], *flat] + ([pltpu.with_memory_space_constraint(weight, pltpu.HBM)] if loads else [held(piece) for piece in pieces])
     n_weights = 1 if loads else len(pieces)
 
     def kernel(*refs):
@@ -253,17 +254,27 @@
             distance, keep, _ = blocks[j // per]
             whose = (x ^ distance) * 2 + (core if keep else 1 - core)
             from_cols = pl.ds(pl.multiple_of(whose * width + (j % per) * tile, 128), tile)
-            return pltpu.make_async_copy(weight_refs[0].at[:, from_cols], tile_ref(j), refs[-1].at[j % slots])
+            return [
+                pltpu.make_async_copy(
+                    weight_refs[0].at[pl.ds(k * depth // cuts, depth // cuts), from_cols],
+                    tile_ref(j).at[pl.ds(k * depth // cuts, depth // cuts), :],
+                    refs[-1].at[j % slots, k],
+                )
+                for k in range(cuts)
+            ]
 
         if loads:
             for j in range(ahead):
-                copy(j).start()
+                for piece in copy(j):
+                    piece.start()
         part = joined(part_refs)
         for j in range(tiles):
             if loads:
-                copy(j).wait()
                 if j + ahead < tiles:
-                    copy(j + ahead).start()
+                    for piece in copy(j + ahead):
+                        piece.start()
+                for piece in copy(j):
+                    piece.wait()
             value = jnp.dot(part, tile_ref(j)[...], preferred_element_type=f32)
             b = j // per
             if gots:
@@ -276,7 +287,7 @@
 
     scratch = []
     if loads:
-        scratch = [pltpu.VMEM((8, 128) if retain else (slots, depth, tile), bf16), pltpu.SemaphoreType.DMA((slots,))]
+        scratch = [pltpu.VMEM((8, 128) if retain else (slots, depth, tile), bf16), pltpu.SemaphoreType.DMA((slots, cuts))]
     return call(
         kernel,
         [shape_of((rows // n, width), dtype) for n, (_, _, dtype) in zip(splits, blocks) for _ in range(n)]
@@ -321,12 +332,13 @@
     return call(kernel, [shape_of(shape, values[0].dtype)], values, [pltpu.VMEM] * len(values), **order)
 
 
-def finish_preact(neur, bias, chunks, t, n_neur, width, before=None, **order):
+def finish_preact(neur, bias, chunks, t, n_neur, width, before=None, beside=(), **order):
     orders = [rows_of for rows_of, _, _ in chunks]
     ins = [neur, bias]
     for _, own, got in chunks:
         ins += [own] + list(got)
     counts = [len(got) for _, _, got in chunks]
+    ins += [held(value) for value in beside]
     aliases = {}
     spaces = [pltpu.SMEM] + [pltpu.VMEM] * (len(ins) - 1)
     if before is not None:
@@ -499,7 +511,7 @@
     return call(
         kernel,
         [shape_of((depth, rank), f32)],
-        [at, mine, theirs, *shards],
+        [at, mine, theirs, *[held(shard) for shard in shards]],
         [pltpu.SMEM] + [pltpu.VMEM] * (2 + count),
         scratch=[pltpu.VMEM((rows, rank), f32), pltpu.VMEM((rows, rank), f32)],
         mib=16,
@@ -536,12 +548,12 @@
         ]
         parts = {}
         away = list(range(1, pairs_x))
-        splits = 2
+        splits = 1
         owns, arrived, got, mine_part, kept = {}, {}, {}, {}, {}
         (bias_cols,) = bias_part(row_at, teacher_bias, width, after=(neur_at, mine_at, other_at))
         gate = (bias_cols,)
 
-        def blocks_of(chunk, distance, keep, cost=1, through=(), wait=False):
+        def blocks_of(chunk, distance, keep, cost=10**4, through=(), wait=False):
             nonlocal gate
             outs = partial_sums(
                 row_at,
@@ -573,13 +585,13 @@
                 kept[distance, keep], *outs = outs
             return outs
 
-        def pin(*values, cost=1):
+        def pin(*values, cost=10**4):
             nonlocal gate
             token, *values = hold(*values, after=gate, weight=cost)
             gate = (token,)
             return values
 
-        def finish(chunks, before=None, through=()):
+        def finish(chunks, before=None, through=(), beside=()):
             nonlocal gate
             relu, target, *passed = finish_preact(
                 neur_at,
@@ -589,6 +601,7 @@
                 n_neur,
                 width,
                 before,
+                beside,
                 after=gate,
                 through=through,
             )
@@ -603,8 +616,7 @@
         shards = [tokens]
         shards += [flip(tokens, "neur", n_neur, e) for e in range(1, lines)]
         near = flip(tokens, "neur", n_neur, lines)
-        (later,) = pin(tokens)
-        far = [flip(later, "neur", n_neur, d * lines) for d in range(2, places)]
+        far = [flip(tokens, "neur", n_neur, d * lines) for d in range(2, places)]
         parts[0] = shards
         for d in away:
             blocks_of(0, d, False, BIG)
@@ -631,13 +643,13 @@
         for d in away:
             blocks_of(2, d, True)
         blocks_of(2, 0, True)
-        done, _ = finish([1], done)
         pairs = [(rows_of[k], rows_of[k + 1]) for rows_of in orders for k in range(0, len(rows_of), 2)]
         hidden_keep, hidden_send = hidden_sums(
             row_at, [part for c in range(4) for part in parts[c]], predictor_down, orders, pairs, t, after=gate
         )
         gate = (hidden_keep,)
         hidden_got = to_core(hidden_send)
+        done, _ = finish([1], done)
         for d in away:
             blocks_of(3, d, False)
         blocks_of(3, 0, False)
@@ -647,7 +659,7 @@
         sends = [blocks_of(3, d, True, wait=True)[-1] for d in away]
         for d, part in zip(away, blocks_of(3, 0, True, through=sends)):
             arrived.setdefault(3, []).append(flip(part, "rows", n_rows, 2 * d))
-        done, (moved,) = finish([2], done, [moved])
+        (moved,) = pin(moved)
         step = 4
         while step < n_rows:
             (mine,) = add_all(f32, (mine, moved))
@@ -656,11 +668,12 @@
         (mine,) = add_all(bf16, (mine, moved), after=gate)
         gate = (mine,)
         column = [mine] + [flip(mine, "neur", n_neur, d * lines) for d in range(1, places)]
+        done, _ = finish([2], done)
         (stack,) = stacked(column, after=gate)
         gate = (stack,)
         stacks = [stack] + [flip(stack, "neur", n_neur, e) for e in range(1, lines)]
         others = [to_core(part) for part in stacks]
-        (teacher_relu, target), _ = finish([3], done)
+        (teacher_relu, target), _ = finish([3], done, beside=[predictor_up])
         (hidden,) = assemble_hidden(mine_at, [(pairs, stacks, others)], places, lines, t, rank, after=gate)
 
         half, send = residue_and_back(

time: 134 us -> 123 us (0.918)
  waiting for transfers between devices: 33.1 us -> 39.5 us
  starting transfers between devices: 36.5 us -> 30.2 us
  Pallas kernels: 55 us -> 48.8 us
  local copies, waits for them, and re-layouts: 6.12 us -> 1.28 us
    ppermute x41 -> x33, waiting for transfers between devices: 33.1 us -> 39.5 us  [flip(): return lax.ppermute(value, axis, [(i, i ^ distance) for i in range(size)])]
    ppermute x41 -> x33, starting transfers between devices: 36.5 us -> 30.2 us  [flip(): return lax.ppermute(value, axis, [(i, i ^ distance) for i in range(size)])]
    pallas_call x35, Pallas kernels: 55 us -> 48.8 us  [call(): pl.pallas_call(body, out_shape=tuple(outs), in_specs=[spot(space) for spa...]
    unnamed x34 -> x37, local copies, waits for them, and re-layouts: 6.12 us -> 1.28 us
  transfers between devices with their start and end apart: 41 -> 33, of which waited for: 10 -> 13; matrix products, arithmetic and copies ran while one was open for 3% -> 2% of each run, Pallas kernels for 36% -> 35%
where the time goes in v3:
time: 123 us
  Pallas kernels  48.8 us (40%)
  waiting for transfers between devices  39.5 us (32%)
  starting transfers between devices  30.2 us (25%)
  matrix products  1.84 us (1%)
  local copies, waits for them, and re-layouts  1.28 us (1%)
    pallas_call x35, Pallas kernels, call(): pl.pallas_call(body, out_shape=tuple(outs), in_specs=[spot(space) for spa...  48.8 us
    ppermute x33, waiting for transfers between devices, flip(): return lax.ppermute(value, axis, [(i, i ^ distance) for i in range(size)])  39.5 us
    ppermute x33, starting transfers between devices, flip(): return lax.ppermute(value, axis, [(i, i ^ distance) for i in range(size)])  30.2 us
  transfers between devices with their start and end apart: 33, of which 13 were waited for; matrix products, arithmetic and copies ran while one was open for 2% of the time, Pallas kernels for 35%

profile of v3, /device:TPU:0, one launch (start us, length us, event | category | flops | bytes accessed | tf_op | source)
XLA Modules:
  0.0 122.8 jit_solution(11031393711060409522)
XLA Ops:
  0.6 3.0 %collective-permute-start.3 = (bf16[64,3072]{1,0:T(8,128)(2,1)}, bf16[64,3072]{1,0:T(8,128)(2,1)S(1)}, u32[]{:S(2)}, u32[]{:S(2)}) collective-permute-start(bf16[64,3072]{1,0:T(8,128)(2,1)} %refs_3_.9), channel_id=1, source_target_pairs={{0,1},{1,0},{2,3},{3,2},{4,5},{5,4},{6,7},{7,6},{8,9},{9,8},{10,11... | collective-permute-start | bytes 1179656 | tf_op jit(solution)/shard_map/ppermute | solution.py:14
  3.7 1.6 %collective-permute-start.2 = (bf16[64,3072]{1,0:T(8,128)(2,1)}, bf16[64,3072]{1,0:T(8,128)(2,1)S(1)}, u32[]{:S(2)}, u32[]{:S(2)}) collective-permute-start(bf16[64,3072]{1,0:T(8,128)(2,1)} %refs_3_.9), channel_id=1, source_target_pairs={{0,2},{1,3},{2,0},{3,1},{4,6},{5,7},{6,4},{7,5},{8,10},{9,11},{10,... | collective-permute-start | bytes 1179656 | tf_op jit(solution)/shard_map/ppermute | solution.py:14
  5.2 2.5 %collective-permute-start.1 = (bf16[64,3072]{1,0:T(8,128)(2,1)}, bf16[64,3072]{1,0:T(8,128)(2,1)S(1)}, u32[]{:S(2)}, u32[]{:S(2)}) collective-permute-start(bf16[64,3072]{1,0:T(8,128)(2,1)} %refs_3_.9), channel_id=1, source_target_pairs={{0,6},{1,7},{2,4},{3,5},{4,2},{5,3},{6,0},{7,1},{8,14},{9,15},{10,... | collective-permute-start | bytes 1179656 | tf_op jit(solution)/shard_map/ppermute | solution.py:14
  8.7 4.3 %collective-permute-done.3.refs_2_.refs_3_.refs_4_ = bf16[64,3072]{1,0:T(8,128)(2,1)S(1)} collective-permute-done((bf16[64,3072]{1,0:T(8,128)(2,1)}, bf16[64,3072]{1,0:T(8,128)(2,1)S(1)}, u32[]{:S(2)}, u32[]{:S(2)}) %collective-permute-start.3) | collective-permute-done | bytes 393248 | tf_op jit(solution)/shard_map/ppermute | solution.py:14
  13.0 4.5 %shard_map.77 = (bf16[128,1536]{1,0:T(8,128)(2,1)S(1)}, bf16[3072,1536]{1,0:T(8,128)(2,1)S(1)}) custom-call(s32[1]{0:T(128)} %bitcast.1.refs_0_, bf16[64,3072]{1,0:T(8,128)(2,1)S(1)} %copy-done, bf16[64,3072]{1,0:T(8,128)(2,1)S(1)} %collective-permute-done.3.refs_2_.refs_3_.refs_4_, bf16[3072,6144]{1,0:T(8,128)(2,1)} %refs_4_.4, ...), custom_call_target="tpu_custom_call" | custom-call | flops 10000000000 | bytes 1000 | tf_op jit(solution)/shard_map/pallas_call | solution.py:173
  17.5 4.5 %shard_map.78 = (bf16[128,1536]{1,0:T(8,128)(2,1)S(1)}, bf16[3072,1536]{1,0:T(8,128)(2,1)S(1)}) custom-call(s32[1]{0:T(128)} %bitcast.1.refs_0_, bf16[64,3072]{1,0:T(8,128)(2,1)S(1)} %copy-done, bf16[64,3072]{1,0:T(8,128)(2,1)S(1)} %collective-permute-done.3.refs_2_.refs_3_.refs_4_, bf16[3072,6144]{1,0:T(8,128)(2,1)} %refs_4_.4, ...), custom_call_target="tpu_custom_call" | custom-call | flops 10000000000 | bytes 1000 | tf_op jit(solution)/shard_map/pallas_call | solution.py:173
  22.6 1.7 %collective-permute-start.4 = (bf16[64,3072]{1,0:T(8,128)(2,1)S(1)}, bf16[64,3072]{1,0:T(8,128)(2,1)S(1)}, u32[]{:S(2)}, u32[]{:S(2)}) collective-permute-start(bf16[64,3072]{1,0:T(8,128)(2,1)S(1)} %get-tuple-element.39.refs_1_.refs_4_.refs_5_), channel_id=1, source_target_pairs={{0,1},{1,0},{2,3},{3,2},{4,5},{5,4},{6,7},{7,6},{8,9},{9,8},{10,11... | collective-permute-start | bytes 1179656 | tf_op jit(solution)/shard_map/ppermute | solution.py:14
  24.3 4.5 %shard_map.80 = (bf16[128,1536]{1,0:T(8,128)(2,1)S(1)}, bf16[3072,1536]{1,0:T(8,128)(2,1)S(1)}) custom-call(s32[1]{0:T(128)} %bitcast.1.refs_0_, bf16[64,3072]{1,0:T(8,128)(2,1)S(1)} %copy-done, bf16[64,3072]{1,0:T(8,128)(2,1)S(1)} %collective-permute-done.3.refs_2_.refs_3_.refs_4_, bf16[128,1536]{1,0:T(8,128)(2,1)S(1)} %collective-permute-done.6.refs_3_, ...), custom_call_target="tpu_custom_call" | custom-call | flops 10000000000 | bytes 1000 | tf_op jit(solution)/shard_map/pallas_call | solution.py:173
  30.4 4.5 %shard_map.81 = (f32[128,1536]{1,0:T(8,128)S(1)}, bf16[3072,1536]{1,0:T(8,128)(2,1)S(1)}) custom-call(s32[1]{0:T(128)} %bitcast.1.refs_0_, bf16[64,3072]{1,0:T(8,128)(2,1)S(1)} %copy-done, bf16[64,3072]{1,0:T(8,128)(2,1)S(1)} %collective-permute-done.3.refs_2_.refs_3_.refs_4_, bf16[128,1536]{1,0:T(8,128)(2,1)S(1)} %collective-permute-done.5.refs_3_, ...), custom_call_target="tpu_custom_call" | custom-call | flops 10000000000 | bytes 1000 | tf_op jit(solution)/shard_map/pallas_call | solution.py:173
  36.4 5.5 %collective-permute-done.refs_0_ = bf16[64,3072]{1,0:T(8,128)(2,1)S(1)} collective-permute-done((bf16[64,3072]{1,0:T(8,128)(2,1)}, bf16[64,3072]{1,0:T(8,128)(2,1)S(1)}, u32[]{:S(2)}, u32[]{:S(2)}) %collective-permute-start) | collective-permute-done | bytes 393248 | tf_op jit(solution)/shard_map/ppermute | solution.py:14
  51.2 1.6 %shard_map.89.refs_4_ = bf16[128,1536]{1,0:T(8,128)(2,1)S(1)} custom-call(s32[1]{0:T(128)} %bitcast.1.refs_0_, bf16[128,3072]{1,0:T(8,128)(2,1)S(1)} %shard_map.83.refs_4_.refs_1_.refs_6_.refs_7_, bf16[3072,1536]{1,0:T(8,128)(2,1)S(1)} %get-tuple-element.44.refs_3_.refs_2_, f32[128,1536]{1,0:T(8,128)S(1)} %shard_map.88.refs_3_.refs_2_), custom_call_target="tpu_custom_call" | custom-call | flops 10000000000 | bytes 1000 | tf_op jit(solution)/shard_map/pallas_call | solution.py:173
  56.7 3.5 %collective-permute-done.7.refs_7_.refs_1_.refs_8_ = bf16[128,3072]{1,0:T(8,128)(2,1)S(1)} collective-permute-done((bf16[128,3072]{1,0:T(8,128)(2,1)S(1)}, bf16[128,3072]{1,0:T(8,128)(2,1)S(1)}, u32[]{:S(2)}, u32[]{:S(2)}) %collective-permute-start.7) | collective-permute-done | bytes 786464 | tf_op jit(solution)/shard_map/ppermute | solution.py:14
  71.8 2.4 %collective-permute-start.22 = (bf16[256,128]{1,0:T(8,128)(2,1)S(1)}, bf16[256,128]{1,0:T(8,128)(2,1)S(1)}, u32[]{:S(2)}, u32[]{:S(2)}) collective-permute-start(bf16[256,128]{1,0:T(8,128)(2,1)S(1)} %shard_map.100.refs_6_.refs_0_), channel_id=1, source_target_pairs={{0,6},{1,7},{2,4},{3,5},{4,2},{5,3},{6,0},{7,1},{8,14},{9,15},{10,... | collective-permute-start | bytes 196616 | tf_op jit(solution)/shard_map/ppermute | solution.py:14
  74.2 2.1 %collective-permute-start.20 = (bf16[256,128]{1,0:T(8,128)(2,1)S(1)}, bf16[256,128]{1,0:T(8,128)(2,1)S(1)}, u32[]{:S(2)}, u32[]{:S(2)}) collective-permute-start(bf16[256,128]{1,0:T(8,128)(2,1)S(1)} %shard_map.100.refs_6_.refs_0_), channel_id=1, source_target_pairs={{0,2},{1,3},{2,0},{3,1},{4,6},{5,7},{6,4},{7,5},{8,10},{9,11},{10,... | collective-permute-start | bytes 196616 | tf_op jit(solution)/shard_map/ppermute | solution.py:14
  80.7 7.6 %collective-permute-done.23.refs_2_ = bf16[4,256,128]{2,1,0:T(8,128)(2,1)S(1)} collective-permute-done((bf16[4,256,128]{2,1,0:T(8,128)(2,1)S(1)}, bf16[4,256,128]{2,1,0:T(8,128)(2,1)S(1)}, u32[]{:S(2)}, u32[]{:S(2)}) %collective-permute-start.23) | collective-permute-done | bytes 262176 | tf_op jit(solution)/shard_map/ppermute | solution.py:14
  90.7 2.7 %shard_map.105 = (bf16[512,1536]{1,0:T(8,128)(2,1)S(1)}, bf16[8,256,128]{2,1,0:T(8,128)(2,1)S(1)}) custom-call(s32[2]{0:T(128)S(1)} %copy-done.5, bf16[512,1024]{1,0:T(8,128)(2,1)S(1)} %shard_map.104.refs_1_, f32[512,1536]{1,0:T(8,128)S(1)} %get-tuple-element.60.refs_5_.refs_2_, bf16[1024,1536]{1,0:T(8,128)(2,1)S(1)} %copy-done.6), custom_call_target="tpu_custom_call" | custom-call | flops 10000000000 | bytes 1000 | tf_op jit(solution)/shard_map/pallas_call | solution.py:173
  93.7 3.0 %shard_map.106 = (bf16[512,1536]{1,0:T(8,128)(2,1)S(1)}, f32[8,256,128]{2,1,0:T(8,128)S(1)}) custom-call(s32[2]{0:T(128)S(1)} %copy-done.3, bf16[512,1024]{1,0:T(8,128)(2,1)S(1)} %shard_map.104.refs_1_, f32[512,1536]{1,0:T(8,128)S(1)} %get-tuple-element.60.refs_5_.refs_2_, bf16[1024,1536]{1,0:T(8,128)(2,1)S(1)} %copy-done.6, ...), custom_call_target="tpu_custom_call", output_to_operand_aliasing={{0}: (4, {})} | custom-call | flops 10000000000 | bytes 1000 | tf_op jit(solution)/shard_map/pallas_call | solution.py:173
  97.4 1.8 %fusion.refs_2_ = f32[1024,1536]{1,0:T(8,128)S(1)} fusion(bf16[512,1024]{1,0:T(8,128)(2,1)S(1)} %shard_map.104.refs_1_, bf16[512,1536]{1,0:T(8,128)(2,1)S(1)} %get-tuple-element.66), kind=kOutput, calls=%fused_computation.3 | convolution fusion | flops 1610612736 | bytes 8912896 | tf_op jit(solution)/shard_map/tr,tf->rf/dot_general | solution.py:687
  99.2 6.2 %collective-permute-done.27.refs_1_ = bf16[4,256,128]{2,1,0:T(8,128)(2,1)S(1)} collective-permute-done((bf16[4,256,128]{2,1,0:T(8,128)(2,1)S(1)}, bf16[4,256,128]{2,1,0:T(8,128)(2,1)S(1)}, u32[]{:S(2)}, u32[]{:S(2)}) %collective-permute-start.27) | collective-permute-done | bytes 262176 | tf_op jit(solution)/shard_map/ppermute | solution.py:14
  105.6 2.9 %collective-permute-start.29 = (bf16[256,128]{1,0:T(8,128)(2,1)S(1)}, bf16[256,128]{1,0:T(8,128)(2,1)S(1)}, u32[]{:S(2)}, u32[]{:S(2)}) collective-permute-start(bf16[256,128]{1,0:T(8,128)(2,1)S(1)} %get-tuple-element.69), channel_id=1, source_target_pairs={{0,4},{1,5},{2,6},{3,7},{4,0},{5,1},{6,2},{7,3},{8,12},{9,13},{10,... | collective-permute-start | bytes 196616 | tf_op jit(solution)/shard_map/ppermute | solution.py:14
  110.1 3.2 %collective-permute-done.29.refs_2_ = bf16[256,128]{1,0:T(8,128)(2,1)S(1)} collective-permute-done((bf16[256,128]{1,0:T(8,128)(2,1)S(1)}, bf16[256,128]{1,0:T(8,128)(2,1)S(1)}, u32[]{:S(2)}, u32[]{:S(2)}) %collective-permute-start.29) | collective-permute-done | bytes 65568 | tf_op jit(solution)/shard_map/ppermute | solution.py:14
  114.6 1.6 %collective-permute-start.31 = (bf16[256,128]{1,0:T(8,128)(2,1)S(1)}, bf16[256,128]{1,0:T(8,128)(2,1)S(1)}, u32[]{:S(2)}, u32[]{:S(2)}) collective-permute-start(bf16[256,128]{1,0:T(8,128)(2,1)S(1)} %convert_element_type.13), channel_id=1, source_target_pairs={{0,16},{8,24},{16,0},{24,8},{1,17},{9,25},{17,1},{25,9},{2,18},{10... | collective-permute-start | bytes 196616 | tf_op jit(solution)/shard_map/ppermute | solution.py:14
  116.2 2.8 %collective-permute-done.31 = bf16[256,128]{1,0:T(8,128)(2,1)S(1)} collective-permute-done((bf16[256,128]{1,0:T(8,128)(2,1)S(1)}, bf16[256,128]{1,0:T(8,128)(2,1)S(1)}, u32[]{:S(2)}, u32[]{:S(2)}) %collective-permute-start.31) | collective-permute-done | bytes 65568 | tf_op jit(solution)/shard_map/ppermute | solution.py:14
  120.3 2.5 %shard_map.110 = f32[3072,128]{1,0:T(8,128)} custom-call(s32[2]{0:T(128)S(1)} %copy-done.3, bf16[256,128]{1,0:T(8,128)(2,1)S(1)} %add_convert_fusion.refs_1_, bf16[256,128]{1,0:T(8,128)(2,1)S(1)} %collective-permute-done.32.refs_2_, bf16[64,3072]{1,0:T(8,128)(2,1)S(1)} %copy-done.1, bf16[64,3072]{1,0:T(8,128)(2,1)S(1)} %collective-permute-done.3.refs_2_.refs_3_.refs_4_, ...), custom_call_target="tpu_custom_call" | custom-call | flops 10000000000 | bytes 1000 | tf_op jit(solution)/shard_map/pallas_call | solution.py:173
  (118 shorter events, 41.4 us)
Async XLA Ops:
  0.6 12.4 %collective-permute-start.3 = (bf16[64,3072]{1,0:T(8,128)(2,1)}, bf16[64,3072]{1,0:T(8,128)(2,1)S(1)}, u32[]{:S(2)}, u32[]{:S(2)}) collective-permute-start(bf16[64,3072]{1,0:T(8,128)(2,1)} %refs_3_.9), channel_id=1, source_target_pairs={{0,1},{1,0},{2,3},{3,2},{4,5},{5,4},{6,7},{7,6},{8,9},{9,8},{10,11... | collective-permute-start | bytes 1179656 | tf_op jit(solution)/shard_map/ppermute | solution.py:14
  3.7 18.9 %collective-permute-start.2 = (bf16[64,3072]{1,0:T(8,128)(2,1)}, bf16[64,3072]{1,0:T(8,128)(2,1)S(1)}, u32[]{:S(2)}, u32[]{:S(2)}) collective-permute-start(bf16[64,3072]{1,0:T(8,128)(2,1)} %refs_3_.9), channel_id=1, source_target_pairs={{0,2},{1,3},{2,0},{3,1},{4,6},{5,7},{6,4},{7,5},{8,10},{9,11},{10,... | collective-permute-start | bytes 1179656 | tf_op jit(solution)/shard_map/ppermute | solution.py:14
  5.2 31.1 %collective-permute-start.1 = (bf16[64,3072]{1,0:T(8,128)(2,1)}, bf16[64,3072]{1,0:T(8,128)(2,1)S(1)}, u32[]{:S(2)}, u32[]{:S(2)}) collective-permute-start(bf16[64,3072]{1,0:T(8,128)(2,1)} %refs_3_.9), channel_id=1, source_target_pairs={{0,6},{1,7},{2,4},{3,5},{4,2},{5,3},{6,0},{7,1},{8,14},{9,15},{10,... | collective-permute-start | bytes 1179656 | tf_op jit(solution)/shard_map/ppermute | solution.py:14
  7.7 34.2 %collective-permute-start = (bf16[64,3072]{1,0:T(8,128)(2,1)}, bf16[64,3072]{1,0:T(8,128)(2,1)S(1)}, u32[]{:S(2)}, u32[]{:S(2)}) collective-permute-start(bf16[64,3072]{1,0:T(8,128)(2,1)} %refs_3_.9), channel_id=1, source_target_pairs={{0,4},{1,5},{2,6},{3,7},{4,0},{5,1},{6,2},{7,3},{8,12},{9,13},{10,... | collective-permute-start | bytes 1179656 | tf_op jit(solution)/shard_map/ppermute | solution.py:14
  17.5 6.9 %collective-permute-start.6 = (bf16[128,1536]{1,0:T(8,128)(2,1)S(1)}, bf16[128,1536]{1,0:T(8,128)(2,1)S(1)}, u32[]{:S(2)}, u32[]{:S(2)}) collective-permute-start(bf16[128,1536]{1,0:T(8,128)(2,1)S(1)} %get-tuple-element.37.refs_4_), channel_id=1, source_target_pairs={{0,8},{8,0},{16,24},{24,16},{1,9},{9,1},{17,25},{25,17},{2,10},{10... | collective-permute-start | bytes 1179656 | tf_op jit(solution)/shard_map/ppermute | solution.py:14
  22.0 8.3 %collective-permute-start.5 = (bf16[128,1536]{1,0:T(8,128)(2,1)S(1)}, bf16[128,1536]{1,0:T(8,128)(2,1)S(1)}, u32[]{:S(2)}, u32[]{:S(2)}) collective-permute-start(bf16[128,1536]{1,0:T(8,128)(2,1)S(1)} %get-tuple-element.38.refs_1_), channel_id=1, source_target_pairs={{0,8},{8,0},{16,24},{24,16},{1,9},{9,1},{17,25},{25,17},{2,10},{10... | collective-permute-start | bytes 1179656 | tf_op jit(solution)/shard_map/ppermute | solution.py:14
  22.6 12.3 %collective-permute-start.4 = (bf16[64,3072]{1,0:T(8,128)(2,1)S(1)}, bf16[64,3072]{1,0:T(8,128)(2,1)S(1)}, u32[]{:S(2)}, u32[]{:S(2)}) collective-permute-start(bf16[64,3072]{1,0:T(8,128)(2,1)S(1)} %get-tuple-element.39.refs_1_.refs_4_.refs_5_), channel_id=1, source_target_pairs={{0,1},{1,0},{2,3},{3,2},{4,5},{5,4},{6,7},{7,6},{8,9},{9,8},{10,11... | collective-permute-start | bytes 1179656 | tf_op jit(solution)/shard_map/ppermute | solution.py:14
  28.8 19.8 %collective-permute-start.9 = (bf16[128,1536]{1,0:T(8,128)(2,1)S(1)}, bf16[128,1536]{1,0:T(8,128)(2,1)S(1)}, u32[]{:S(2)}, u32[]{:S(2)}) collective-permute-start(bf16[128,1536]{1,0:T(8,128)(2,1)S(1)} %get-tuple-element.42.refs_5_), channel_id=1, source_target_pairs={{0,16},{8,24},{16,0},{24,8},{1,17},{9,25},{17,1},{25,9},{2,18},{10... | collective-permute-start | bytes 1179656 | tf_op jit(solution)/shard_map/ppermute | solution.py:14
  36.3 7.7 %collective-permute-start.10 = (bf16[128,1536]{1,0:T(8,128)(2,1)S(1)}, bf16[128,1536]{1,0:T(8,128)(2,1)S(1)}, u32[]{:S(2)}, u32[]{:S(2)}) collective-permute-start(bf16[128,1536]{1,0:T(8,128)(2,1)S(1)} %shard_map.82.refs_2_), channel_id=1, source_target_pairs={{0,8},{8,0},{16,24},{24,16},{1,9},{9,1},{17,25},{25,17},{2,10},{10... | collective-permute-start | bytes 1179656 | tf_op jit(solution)/shard_map/ppermute | solution.py:14
  42.0 18.2 %collective-permute-start.7 = (bf16[128,3072]{1,0:T(8,128)(2,1)S(1)}, bf16[128,3072]{1,0:T(8,128)(2,1)S(1)}, u32[]{:S(2)}, u32[]{:S(2)}) collective-permute-start(bf16[128,3072]{1,0:T(8,128)(2,1)S(1)} %shard_map.83.refs_4_.refs_1_.refs_6_.refs_7_), channel_id=1, source_target_pairs={{0,1},{1,0},{2,3},{3,2},{4,5},{5,4},{6,7},{7,6},{8,9},{9,8},{10,11... | collective-permute-start | bytes 2359304 | tf_op jit(solution)/shard_map/ppermute | solution.py:14
  44.0 5.6 %collective-permute-start.8 = (bf16[128,1536]{1,0:T(8,128)(2,1)S(1)}, bf16[128,1536]{1,0:T(8,128)(2,1)S(1)}, u32[]{:S(2)}, u32[]{:S(2)}) collective-permute-start(bf16[128,1536]{1,0:T(8,128)(2,1)S(1)} %shard_map.84.refs_5_), channel_id=1, source_target_pairs={{0,8},{8,0},{16,24},{24,16},{1,9},{9,1},{17,25},{25,17},{2,10},{10... | collective-permute-start | bytes 1179656 | tf_op jit(solution)/shard_map/ppermute | solution.py:14
  46.9 14.3 %collective-permute-start.11 = (bf16[128,1536]{1,0:T(8,128)(2,1)S(1)}, bf16[128,1536]{1,0:T(8,128)(2,1)S(1)}, u32[]{:S(2)}, u32[]{:S(2)}) collective-permute-start(bf16[128,1536]{1,0:T(8,128)(2,1)S(1)} %shard_map.85.refs_3_), channel_id=1, source_target_pairs={{0,16},{8,24},{16,0},{24,8},{1,17},{9,25},{17,1},{25,9},{2,18},{10... | collective-permute-start | bytes 1179656 | tf_op jit(solution)/shard_map/ppermute | solution.py:14
  48.4 4.7 %collective-permute-start.13 = (bf16[128,1536]{1,0:T(8,128)(2,1)S(1)}, bf16[128,1536]{1,0:T(8,128)(2,1)S(1)}, u32[]{:S(2)}, u32[]{:S(2)}) collective-permute-start(bf16[128,1536]{1,0:T(8,128)(2,1)S(1)} %shard_map.86.refs_4_), channel_id=1, source_target_pairs={{0,8},{8,0},{16,24},{24,16},{1,9},{9,1},{17,25},{25,17},{2,10},{10... | collective-permute-start | bytes 1179656 | tf_op jit(solution)/shard_map/ppermute | solution.py:14
  54.6 23.1 %collective-permute-start.18 = (bf16[128,1536]{1,0:T(8,128)(2,1)S(1)}, bf16[128,1536]{1,0:T(8,128)(2,1)S(1)}, u32[]{:S(2)}, u32[]{:S(2)}) collective-permute-start(bf16[128,1536]{1,0:T(8,128)(2,1)S(1)} %shard_map.90.refs_4_), channel_id=1, source_target_pairs={{0,16},{8,24},{16,0},{24,8},{1,17},{9,25},{17,1},{25,9},{2,18},{10... | collective-permute-start | bytes 1179656 | tf_op jit(solution)/shard_map/ppermute | solution.py:14
  65.8 5.9 %collective-permute-start.19 = (f32[256,128]{1,0:T(8,128)S(1)}, f32[256,128]{1,0:T(8,128)S(1)}, u32[]{:S(2)}, u32[]{:S(2)}) collective-permute-start(f32[256,128]{1,0:T(8,128)S(1)} %shard_map.96.refs_4_.refs_0_), channel_id=1, source_target_pairs={{0,16},{8,24},{16,0},{24,8},{1,17},{9,25},{17,1},{25,9},{2,18},{10... | collective-permute-start | bytes 393224 | tf_op jit(solution)/shard_map/ppermute | solution.py:14
  71.8 6.8 %collective-permute-start.22 = (bf16[256,128]{1,0:T(8,128)(2,1)S(1)}, bf16[256,128]{1,0:T(8,128)(2,1)S(1)}, u32[]{:S(2)}, u32[]{:S(2)}) collective-permute-start(bf16[256,128]{1,0:T(8,128)(2,1)S(1)} %shard_map.100.refs_6_.refs_0_), channel_id=1, source_target_pairs={{0,6},{1,7},{2,4},{3,5},{4,2},{5,3},{6,0},{7,1},{8,14},{9,15},{10,... | collective-permute-start | bytes 196616 | tf_op jit(solution)/shard_map/ppermute | solution.py:14
  74.2 6.0 %collective-permute-start.21 = (bf16[256,128]{1,0:T(8,128)(2,1)S(1)}, bf16[256,128]{1,0:T(8,128)(2,1)S(1)}, u32[]{:S(2)}, u32[]{:S(2)}) collective-permute-start(bf16[256,128]{1,0:T(8,128)(2,1)S(1)} %shard_map.100.refs_6_.refs_0_), channel_id=1, source_target_pairs={{0,4},{1,5},{2,6},{3,7},{4,0},{5,1},{6,2},{7,3},{8,12},{9,13},{10,... | collective-permute-start | bytes 196616 | tf_op jit(solution)/shard_map/ppermute | solution.py:14
  74.2 6.0 %collective-permute-start.20 = (bf16[256,128]{1,0:T(8,128)(2,1)S(1)}, bf16[256,128]{1,0:T(8,128)(2,1)S(1)}, u32[]{:S(2)}, u32[]{:S(2)}) collective-permute-start(bf16[256,128]{1,0:T(8,128)(2,1)S(1)} %shard_map.100.refs_6_.refs_0_), channel_id=1, source_target_pairs={{0,2},{1,3},{2,0},{3,1},{4,6},{5,7},{6,4},{7,5},{8,10},{9,11},{10,... | collective-permute-start | bytes 196616 | tf_op jit(solution)/shard_map/ppermute | solution.py:14
  76.2 12.1 %collective-permute-start.17 = (bf16[128,1536]{1,0:T(8,128)(2,1)S(1)}, bf16[128,1536]{1,0:T(8,128)(2,1)S(1)}, u32[]{:S(2)}, u32[]{:S(2)}) collective-permute-start(bf16[128,1536]{1,0:T(8,128)(2,1)S(1)} %get-tuple-element.53), channel_id=1, source_target_pairs={{0,16},{8,24},{16,0},{24,8},{1,17},{9,25},{17,1},{25,9},{2,18},{10... | collective-permute-start | bytes 1179656 | tf_op jit(solution)/shard_map/ppermute | solution.py:14
  80.2 8.2 %collective-permute-start.23 = (bf16[4,256,128]{2,1,0:T(8,128)(2,1)S(1)}, bf16[4,256,128]{2,1,0:T(8,128)(2,1)S(1)}, u32[]{:S(2)}, u32[]{:S(2)}) collective-permute-start(bf16[4,256,128]{2,1,0:T(8,128)(2,1)S(1)} %shard_map.102.refs_7_.refs_1_), channel_id=1, source_target_pairs={{0,1},{1,0},{2,3},{3,2},{4,5},{5,4},{6,7},{7,6},{8,9},{9,8},{10,11... | collective-permute-start | bytes 786440 | tf_op jit(solution)/shard_map/ppermute | solution.py:14
  80.7 8.5 %collective-permute-start.24 = (bf16[4,256,128]{2,1,0:T(8,128)(2,1)S(1)}, bf16[4,256,128]{2,1,0:T(8,128)(2,1)S(1)}, u32[]{:S(2)}, u32[]{:S(2)}) collective-permute-start(bf16[4,256,128]{2,1,0:T(8,128)(2,1)S(1)} %shard_map.102.refs_7_.refs_1_), channel_id=1, source_target_pairs={{0,8},{8,0},{16,24},{24,16},{1,9},{9,1},{17,25},{25,17},{2,10},{10... | collective-permute-start | bytes 786440 | tf_op jit(solution)/shard_map/ppermute | solution.py:14
  96.8 8.6 %collective-permute-start.27 = (bf16[4,256,128]{2,1,0:T(8,128)(2,1)S(1)}, bf16[4,256,128]{2,1,0:T(8,128)(2,1)S(1)}, u32[]{:S(2)}, u32[]{:S(2)}) collective-permute-start(bf16[4,256,128]{2,1,0:T(8,128)(2,1)S(1)} %get-tuple-element.65), channel_id=1, source_target_pairs={{0,1},{1,0},{2,3},{3,2},{4,5},{5,4},{6,7},{7,6},{8,9},{9,8},{10,11... | collective-permute-start | bytes 786440 | tf_op jit(solution)/shard_map/ppermute | solution.py:14
  105.6 7.7 %collective-permute-start.29 = (bf16[256,128]{1,0:T(8,128)(2,1)S(1)}, bf16[256,128]{1,0:T(8,128)(2,1)S(1)}, u32[]{:S(2)}, u32[]{:S(2)}) collective-permute-start(bf16[256,128]{1,0:T(8,128)(2,1)S(1)} %get-tuple-element.69), channel_id=1, source_target_pairs={{0,4},{1,5},{2,6},{3,7},{4,0},{5,1},{6,2},{7,3},{8,12},{9,13},{10,... | collective-permute-start | bytes 196616 | tf_op jit(solution)/shard_map/ppermute | solution.py:14
  108.4 6.2 %collective-permute-start.30 = (bf16[256,128]{1,0:T(8,128)(2,1)S(1)}, bf16[256,128]{1,0:T(8,128)(2,1)S(1)}, u32[]{:S(2)}, u32[]{:S(2)}) collective-permute-start(bf16[256,128]{1,0:T(8,128)(2,1)S(1)} %get-tuple-element.70), channel_id=1, source_target_pairs={{0,6},{1,7},{2,4},{3,5},{4,2},{5,3},{6,0},{7,1},{8,14},{9,15},{10,... | collective-permute-start | bytes 196616 | tf_op jit(solution)/shard_map/ppermute | solution.py:14
  (27 other events, 132.2 us)

commit v4 on v3

--- a/solution.py
+++ b/solution.py
@@ -87,6 +87,7 @@
             step *= 2
         mine = mine.astype(bf16)
         column = [mine] + [flip(mine, "neur", n_neur, d * lines) for d in range(1, places)]
+        own_lines = [flip(mine, "neur", n_neur, e) for e in range(1, lines)]
         stack = jnp.stack(column)
         stacks = [stack] + [flip(stack, "neur", n_neur, e) for e in range(1, lines)]
         blocks = [stacks[d % lines][d // lines] for d in range(n_neur)]
@@ -418,7 +419,11 @@
                     for i, (a, b) in enumerate(pairs):
                         shard = owner ^ (a ^ (which * (a ^ b)))
                         rows = pl.ds(pl.multiple_of(shard * t, t), t)
-                        out_ref[rows, cols] = refs[first + e][d, i * t : (i + 1) * t, :]
+                        here = slice(i * t, (i + 1) * t)
+                        if d == 0:
+                            out_ref[rows, cols] = refs[first + 2 * e][here, :]
+                        else:
+                            out_ref[rows, cols] = refs[first + 2 * e + 1][d - 1, here, :]
 
     return call(
         kernel, [shape_of((n_neur * t, n_neur * rank), bf16)], ins, [pltpu.SMEM] + [pltpu.VMEM] * (len(ins) - 1), **order
@@ -496,24 +501,35 @@
     tile = tile_of(depth)
 
     def kernel(at_ref, mine_ref, theirs_ref, *refs):
-        out_ref, back, placed = refs[-3:]
+        out_ref, back, placed, result, sems = refs[-5:]
         core, neur = at_ref[0], at_ref[1]
         back[pl.ds(pl.multiple_of(core * half_rows, half_rows), half_rows), :] = mine_ref[...].astype(f32)
         back[pl.ds(pl.multiple_of((1 - core) * half_rows, half_rows), half_rows), :] = theirs_ref[...].astype(f32)
         for i, s in enumerate(order):
             placed[i * t : (i + 1) * t, :] = back[pl.ds(pl.multiple_of((neur ^ s) * t, t), t), :]
         turned = placed[...].T.astype(bf16)
+        copies = []
         for k in range(depth // tile):
             cols = slice(k * tile, (k + 1) * tile)
             whole = joined(refs[:count], cols)
-            out_ref[cols, :] = jnp.dot(turned, whole, preferred_element_type=f32).T
+            result[cols, :] = jnp.dot(turned, whole, preferred_element_type=f32).T
+            copies.append(pltpu.make_async_copy(result.at[cols, :], out_ref.at[cols, :], sems.at[k]))
+            copies[-1].start()
+        for copy in copies:
+            copy.wait()
 
     return call(
         kernel,
         [shape_of((depth, rank), f32)],
         [at, mine, theirs, *[held(shard) for shard in shards]],
         [pltpu.SMEM] + [pltpu.VMEM] * (2 + count),
-        scratch=[pltpu.VMEM((rows, rank), f32), pltpu.VMEM((rows, rank), f32)],
+        scratch=[
+            pltpu.VMEM((rows, rank), f32),
+            pltpu.VMEM((rows, rank), f32),
+            pltpu.VMEM((depth, rank), f32),
+            pltpu.SemaphoreType.DMA((depth // tile,)),
+        ],
+        out_spaces=[pl.ANY],
         mib=16,
     )[0]
 
@@ -668,10 +684,13 @@
         (mine,) = add_all(bf16, (mine, moved), after=gate)
         gate = (mine,)
         column = [mine] + [flip(mine, "neur", n_neur, d * lines) for d in range(1, places)]
+        own_lines = [flip(mine, "neur", n_neur, e) for e in range(1, lines)]
         done, _ = finish([2], done)
-        (stack,) = stacked(column, after=gate)
+        (stack,) = stacked(column[1:], after=gate)
         gate = (stack,)
-        stacks = [stack] + [flip(stack, "neur", n_neur, e) for e in range(1, lines)]
+        stacks = [mine, stack]
+        for e in range(1, lines):
+            stacks += [own_lines[e - 1], flip(stack, "neur", n_neur, e)]
         others = [to_core(part) for part in stacks]
         (teacher_relu, target), _ = finish([3], done, beside=[predictor_up])
         (hidden,) = assemble_hidden(mine_at, [(pairs, stacks, others)], places, lines, t, rank, after=gate)

time: 123 us -> 123 us (level)
  waiting for transfers between devices: 39.5 us -> 36.6 us
  starting transfers between devices: 30.2 us -> 32.9 us
    ppermute x33 -> x36, waiting for transfers between devices: 39.5 us -> 36.6 us  [flip(): return lax.ppermute(value, axis, [(i, i ^ distance) for i in range(size)])]
    ppermute x33 -> x36, starting transfers between devices: 30.2 us -> 32.9 us  [flip(): return lax.ppermute(value, axis, [(i, i ^ distance) for i in range(size)])]
  transfers between devices with their start and end apart: 33 -> 36, of which waited for: 13 -> 12; matrix products, arithmetic and copies ran while one was open for 2% -> 2% of each run, Pallas kernels for 35% -> 35%
where the time goes in v4:
time: 123 us
  Pallas kernels  48.5 us (39%)
  waiting for transfers between devices  36.6 us (30%)
  starting transfers between devices  32.9 us (27%)
  matrix products  1.84 us (1%)
  between operations  1.31 us (1%)
  local copies, waits for them, and re-layouts  1.28 us (1%)
    pallas_call x35, Pallas kernels, call(): pl.pallas_call(body, out_shape=tuple(outs), in_specs=[spot(space) for spa...  48.5 us
    ppermute x36, waiting for transfers between devices, flip(): return lax.ppermute(value, axis, [(i, i ^ distance) for i in range(size)])  36.6 us
    ppermute x36, starting transfers between devices, flip(): return lax.ppermute(value, axis, [(i, i ^ distance) for i in range(size)])  32.9 us
  transfers between devices with their start and end apart: 36, of which 12 were waited for; matrix products, arithmetic and copies ran while one was open for 2% of the time, Pallas kernels for 35%

profile of v4, /device:TPU:0, one launch (start us, length us, event | category | flops | bytes accessed | tf_op | source)
XLA Modules:
  0.0 122.6 jit_solution(11402755425064666273)
XLA Ops:
  0.6 3.0 %collective-permute-start.3 = (bf16[64,3072]{1,0:T(8,128)(2,1)}, bf16[64,3072]{1,0:T(8,128)(2,1)S(1)}, u32[]{:S(2)}, u32[]{:S(2)}) collective-permute-start(bf16[64,3072]{1,0:T(8,128)(2,1)} %refs_3_.9), channel_id=1, source_target_pairs={{0,1},{1,0},{2,3},{3,2},{4,5},{5,4},{6,7},{7,6},{8,9},{9,8},{10,11... | collective-permute-start | bytes 1179656 | tf_op jit(solution)/shard_map/ppermute | solution.py:14
  3.7 1.6 %collective-permute-start.2 = (bf16[64,3072]{1,0:T(8,128)(2,1)}, bf16[64,3072]{1,0:T(8,128)(2,1)S(1)}, u32[]{:S(2)}, u32[]{:S(2)}) collective-permute-start(bf16[64,3072]{1,0:T(8,128)(2,1)} %refs_3_.9), channel_id=1, source_target_pairs={{0,2},{1,3},{2,0},{3,1},{4,6},{5,7},{6,4},{7,5},{8,10},{9,11},{10,... | collective-permute-start | bytes 1179656 | tf_op jit(solution)/shard_map/ppermute | solution.py:14
  5.2 2.5 %collective-permute-start.1 = (bf16[64,3072]{1,0:T(8,128)(2,1)}, bf16[64,3072]{1,0:T(8,128)(2,1)S(1)}, u32[]{:S(2)}, u32[]{:S(2)}) collective-permute-start(bf16[64,3072]{1,0:T(8,128)(2,1)} %refs_3_.9), channel_id=1, source_target_pairs={{0,6},{1,7},{2,4},{3,5},{4,2},{5,3},{6,0},{7,1},{8,14},{9,15},{10,... | collective-permute-start | bytes 1179656 | tf_op jit(solution)/shard_map/ppermute | solution.py:14
  8.7 4.3 %collective-permute-done.3.refs_2_.refs_3_.refs_4_ = bf16[64,3072]{1,0:T(8,128)(2,1)S(1)} collective-permute-done((bf16[64,3072]{1,0:T(8,128)(2,1)}, bf16[64,3072]{1,0:T(8,128)(2,1)S(1)}, u32[]{:S(2)}, u32[]{:S(2)}) %collective-permute-start.3) | collective-permute-done | bytes 393248 | tf_op jit(solution)/shard_map/ppermute | solution.py:14
  13.0 4.5 %shard_map.77 = (bf16[128,1536]{1,0:T(8,128)(2,1)S(1)}, bf16[3072,1536]{1,0:T(8,128)(2,1)S(1)}) custom-call(s32[1]{0:T(128)} %bitcast.1.refs_0_, bf16[64,3072]{1,0:T(8,128)(2,1)S(1)} %copy-done, bf16[64,3072]{1,0:T(8,128)(2,1)S(1)} %collective-permute-done.3.refs_2_.refs_3_.refs_4_, bf16[3072,6144]{1,0:T(8,128)(2,1)} %refs_4_.4, ...), custom_call_target="tpu_custom_call" | custom-call | flops 10000000000 | bytes 1000 | tf_op jit(solution)/shard_map/pallas_call | solution.py:174
  17.5 4.5 %shard_map.78 = (bf16[128,1536]{1,0:T(8,128)(2,1)S(1)}, bf16[3072,1536]{1,0:T(8,128)(2,1)S(1)}) custom-call(s32[1]{0:T(128)} %bitcast.1.refs_0_, bf16[64,3072]{1,0:T(8,128)(2,1)S(1)} %copy-done, bf16[64,3072]{1,0:T(8,128)(2,1)S(1)} %collective-permute-done.3.refs_2_.refs_3_.refs_4_, bf16[3072,6144]{1,0:T(8,128)(2,1)} %refs_4_.4, ...), custom_call_target="tpu_custom_call" | custom-call | flops 10000000000 | bytes 1000 | tf_op jit(solution)/shard_map/pallas_call | solution.py:174
  22.6 1.7 %collective-permute-start.4 = (bf16[64,3072]{1,0:T(8,128)(2,1)S(1)}, bf16[64,3072]{1,0:T(8,128)(2,1)S(1)}, u32[]{:S(2)}, u32[]{:S(2)}) collective-permute-start(bf16[64,3072]{1,0:T(8,128)(2,1)S(1)} %get-tuple-element.39.refs_1_.refs_4_.refs_5_), channel_id=1, source_target_pairs={{0,1},{1,0},{2,3},{3,2},{4,5},{5,4},{6,7},{7,6},{8,9},{9,8},{10,11... | collective-permute-start | bytes 1179656 | tf_op jit(solution)/shard_map/ppermute | solution.py:14
  24.3 4.5 %shard_map.80 = (bf16[128,1536]{1,0:T(8,128)(2,1)S(1)}, bf16[3072,1536]{1,0:T(8,128)(2,1)S(1)}) custom-call(s32[1]{0:T(128)} %bitcast.1.refs_0_, bf16[64,3072]{1,0:T(8,128)(2,1)S(1)} %copy-done, bf16[64,3072]{1,0:T(8,128)(2,1)S(1)} %collective-permute-done.3.refs_2_.refs_3_.refs_4_, bf16[128,1536]{1,0:T(8,128)(2,1)S(1)} %collective-permute-done.6.refs_3_, ...), custom_call_target="tpu_custom_call" | custom-call | flops 10000000000 | bytes 1000 | tf_op jit(solution)/shard_map/pallas_call | solution.py:174
  30.4 4.5 %shard_map.81 = (f32[128,1536]{1,0:T(8,128)S(1)}, bf16[3072,1536]{1,0:T(8,128)(2,1)S(1)}) custom-call(s32[1]{0:T(128)} %bitcast.1.refs_0_, bf16[64,3072]{1,0:T(8,128)(2,1)S(1)} %copy-done, bf16[64,3072]{1,0:T(8,128)(2,1)S(1)} %collective-permute-done.3.refs_2_.refs_3_.refs_4_, bf16[128,1536]{1,0:T(8,128)(2,1)S(1)} %collective-permute-done.5.refs_3_, ...), custom_call_target="tpu_custom_call" | custom-call | flops 10000000000 | bytes 1000 | tf_op jit(solution)/shard_map/pallas_call | solution.py:174
  36.4 5.5 %collective-permute-done.refs_0_ = bf16[64,3072]{1,0:T(8,128)(2,1)S(1)} collective-permute-done((bf16[64,3072]{1,0:T(8,128)(2,1)}, bf16[64,3072]{1,0:T(8,128)(2,1)S(1)}, u32[]{:S(2)}, u32[]{:S(2)}) %collective-permute-start) | collective-permute-done | bytes 393248 | tf_op jit(solution)/shard_map/ppermute | solution.py:14
  51.2 1.6 %shard_map.89.refs_4_ = bf16[128,1536]{1,0:T(8,128)(2,1)S(1)} custom-call(s32[1]{0:T(128)} %bitcast.1.refs_0_, bf16[128,3072]{1,0:T(8,128)(2,1)S(1)} %shard_map.83.refs_4_.refs_1_.refs_6_.refs_7_, bf16[3072,1536]{1,0:T(8,128)(2,1)S(1)} %get-tuple-element.44.refs_3_.refs_2_, f32[128,1536]{1,0:T(8,128)S(1)} %shard_map.88.refs_3_.refs_2_), custom_call_target="tpu_custom_call" | custom-call | flops 10000000000 | bytes 1000 | tf_op jit(solution)/shard_map/pallas_call | solution.py:174
  56.7 3.5 %collective-permute-done.7.refs_7_.refs_1_.refs_8_ = bf16[128,3072]{1,0:T(8,128)(2,1)S(1)} collective-permute-done((bf16[128,3072]{1,0:T(8,128)(2,1)S(1)}, bf16[128,3072]{1,0:T(8,128)(2,1)S(1)}, u32[]{:S(2)}, u32[]{:S(2)}) %collective-permute-start.7) | collective-permute-done | bytes 786464 | tf_op jit(solution)/shard_map/ppermute | solution.py:14
  71.8 2.4 %collective-permute-start.22 = (bf16[256,128]{1,0:T(8,128)(2,1)S(1)}, bf16[256,128]{1,0:T(8,128)(2,1)S(1)}, u32[]{:S(2)}, u32[]{:S(2)}) collective-permute-start(bf16[256,128]{1,0:T(8,128)(2,1)S(1)} %shard_map.100.refs_6_.refs_1_), channel_id=1, source_target_pairs={{0,6},{1,7},{2,4},{3,5},{4,2},{5,3},{6,0},{7,1},{8,14},{9,15},{10,... | collective-permute-start | bytes 196616 | tf_op jit(solution)/shard_map/ppermute | solution.py:14
  74.2 2.1 %collective-permute-start.20 = (bf16[256,128]{1,0:T(8,128)(2,1)S(1)}, bf16[256,128]{1,0:T(8,128)(2,1)S(1)}, u32[]{:S(2)}, u32[]{:S(2)}) collective-permute-start(bf16[256,128]{1,0:T(8,128)(2,1)S(1)} %shard_map.100.refs_6_.refs_1_), channel_id=1, source_target_pairs={{0,2},{1,3},{2,0},{3,1},{4,6},{5,7},{6,4},{7,5},{8,10},{9,11},{10,... | collective-permute-start | bytes 196616 | tf_op jit(solution)/shard_map/ppermute | solution.py:14
  82.8 5.6 %collective-permute-done.23.refs_3_ = bf16[256,128]{1,0:T(8,128)(2,1)S(1)} collective-permute-done((bf16[256,128]{1,0:T(8,128)(2,1)S(1)}, bf16[256,128]{1,0:T(8,128)(2,1)S(1)}, u32[]{:S(2)}, u32[]{:S(2)}) %collective-permute-start.23) | collective-permute-done | bytes 65568 | tf_op jit(solution)/shard_map/ppermute | solution.py:14
  90.8 2.7 %shard_map.105 = (bf16[512,1536]{1,0:T(8,128)(2,1)S(1)}, bf16[8,256,128]{2,1,0:T(8,128)(2,1)S(1)}) custom-call(s32[2]{0:T(128)S(1)} %copy-done.5, bf16[512,1024]{1,0:T(8,128)(2,1)S(1)} %shard_map.104.refs_1_, f32[512,1536]{1,0:T(8,128)S(1)} %get-tuple-element.60.refs_9_.refs_2_, bf16[1024,1536]{1,0:T(8,128)(2,1)S(1)} %copy-done.6), custom_call_target="tpu_custom_call" | custom-call | flops 10000000000 | bytes 1000 | tf_op jit(solution)/shard_map/pallas_call | solution.py:174
  94.0 3.0 %shard_map.106 = (bf16[512,1536]{1,0:T(8,128)(2,1)S(1)}, f32[8,256,128]{2,1,0:T(8,128)S(1)}) custom-call(s32[2]{0:T(128)S(1)} %copy-done.3, bf16[512,1024]{1,0:T(8,128)(2,1)S(1)} %shard_map.104.refs_1_, f32[512,1536]{1,0:T(8,128)S(1)} %get-tuple-element.60.refs_9_.refs_2_, bf16[1024,1536]{1,0:T(8,128)(2,1)S(1)} %copy-done.6, ...), custom_call_target="tpu_custom_call", output_to_operand_aliasing={{0}: (4, {})} | custom-call | flops 10000000000 | bytes 1000 | tf_op jit(solution)/shard_map/pallas_call | solution.py:174
  97.6 1.8 %fusion.refs_2_ = f32[1024,1536]{1,0:T(8,128)S(1)} fusion(bf16[512,1024]{1,0:T(8,128)(2,1)S(1)} %shard_map.104.refs_1_, bf16[512,1536]{1,0:T(8,128)(2,1)S(1)} %get-tuple-element.66), kind=kOutput, calls=%fused_computation.3 | convolution fusion | flops 1610612736 | bytes 8912896 | tf_op jit(solution)/shard_map/tr,tf->rf/dot_general | solution.py:706
  99.5 6.0 %collective-permute-done.30.refs_1_ = bf16[4,256,128]{2,1,0:T(8,128)(2,1)S(1)} collective-permute-done((bf16[4,256,128]{2,1,0:T(8,128)(2,1)S(1)}, bf16[4,256,128]{2,1,0:T(8,128)(2,1)S(1)}, u32[]{:S(2)}, u32[]{:S(2)}) %collective-permute-start.30) | collective-permute-done | bytes 262176 | tf_op jit(solution)/shard_map/ppermute | solution.py:14
  105.6 2.9 %collective-permute-start.32 = (bf16[256,128]{1,0:T(8,128)(2,1)S(1)}, bf16[256,128]{1,0:T(8,128)(2,1)S(1)}, u32[]{:S(2)}, u32[]{:S(2)}) collective-permute-start(bf16[256,128]{1,0:T(8,128)(2,1)S(1)} %get-tuple-element.69), channel_id=1, source_target_pairs={{0,4},{1,5},{2,6},{3,7},{4,0},{5,1},{6,2},{7,3},{8,12},{9,13},{10,... | collective-permute-start | bytes 196616 | tf_op jit(solution)/shard_map/ppermute | solution.py:14
  110.0 3.1 %collective-permute-done.32.refs_2_ = bf16[256,128]{1,0:T(8,128)(2,1)S(1)} collective-permute-done((bf16[256,128]{1,0:T(8,128)(2,1)S(1)}, bf16[256,128]{1,0:T(8,128)(2,1)S(1)}, u32[]{:S(2)}, u32[]{:S(2)}) %collective-permute-start.32) | collective-permute-done | bytes 65568 | tf_op jit(solution)/shard_map/ppermute | solution.py:14
  114.6 1.6 %collective-permute-start.34 = (bf16[256,128]{1,0:T(8,128)(2,1)S(1)}, bf16[256,128]{1,0:T(8,128)(2,1)S(1)}, u32[]{:S(2)}, u32[]{:S(2)}) collective-permute-start(bf16[256,128]{1,0:T(8,128)(2,1)S(1)} %convert_element_type.13), channel_id=1, source_target_pairs={{0,16},{8,24},{16,0},{24,8},{1,17},{9,25},{17,1},{25,9},{2,18},{10... | collective-permute-start | bytes 196616 | tf_op jit(solution)/shard_map/ppermute | solution.py:14
  116.2 2.8 %collective-permute-done.34 = bf16[256,128]{1,0:T(8,128)(2,1)S(1)} collective-permute-done((bf16[256,128]{1,0:T(8,128)(2,1)S(1)}, bf16[256,128]{1,0:T(8,128)(2,1)S(1)}, u32[]{:S(2)}, u32[]{:S(2)}) %collective-permute-start.34) | collective-permute-done | bytes 65568 | tf_op jit(solution)/shard_map/ppermute | solution.py:14
  120.3 2.2 %shard_map.110 = f32[3072,128]{1,0:T(8,128)} custom-call(s32[2]{0:T(128)S(1)} %copy-done.3, bf16[256,128]{1,0:T(8,128)(2,1)S(1)} %add_convert_fusion.refs_1_, bf16[256,128]{1,0:T(8,128)(2,1)S(1)} %collective-permute-done.35.refs_2_, bf16[64,3072]{1,0:T(8,128)(2,1)S(1)} %copy-done.1, bf16[64,3072]{1,0:T(8,128)(2,1)S(1)} %collective-permute-done.3.refs_2_.refs_3_.refs_4_, ...), custom_call_target="tpu_custom_call" | custom-call | flops 10000000000 | bytes 1000 | tf_op jit(solution)/shard_map/pallas_call | solution.py:174
  (124 shorter events, 43.6 us)
Async XLA Ops:
  0.6 12.4 %collective-permute-start.3 = (bf16[64,3072]{1,0:T(8,128)(2,1)}, bf16[64,3072]{1,0:T(8,128)(2,1)S(1)}, u32[]{:S(2)}, u32[]{:S(2)}) collective-permute-start(bf16[64,3072]{1,0:T(8,128)(2,1)} %refs_3_.9), channel_id=1, source_target_pairs={{0,1},{1,0},{2,3},{3,2},{4,5},{5,4},{6,7},{7,6},{8,9},{9,8},{10,11... | collective-permute-start | bytes 1179656 | tf_op jit(solution)/shard_map/ppermute | solution.py:14
  3.7 18.9 %collective-permute-start.2 = (bf16[64,3072]{1,0:T(8,128)(2,1)}, bf16[64,3072]{1,0:T(8,128)(2,1)S(1)}, u32[]{:S(2)}, u32[]{:S(2)}) collective-permute-start(bf16[64,3072]{1,0:T(8,128)(2,1)} %refs_3_.9), channel_id=1, source_target_pairs={{0,2},{1,3},{2,0},{3,1},{4,6},{5,7},{6,4},{7,5},{8,10},{9,11},{10,... | collective-permute-start | bytes 1179656 | tf_op jit(solution)/shard_map/ppermute | solution.py:14
  5.2 31.1 %collective-permute-start.1 = (bf16[64,3072]{1,0:T(8,128)(2,1)}, bf16[64,3072]{1,0:T(8,128)(2,1)S(1)}, u32[]{:S(2)}, u32[]{:S(2)}) collective-permute-start(bf16[64,3072]{1,0:T(8,128)(2,1)} %refs_3_.9), channel_id=1, source_target_pairs={{0,6},{1,7},{2,4},{3,5},{4,2},{5,3},{6,0},{7,1},{8,14},{9,15},{10,... | collective-permute-start | bytes 1179656 | tf_op jit(solution)/shard_map/ppermute | solution.py:14
  7.7 34.2 %collective-permute-start = (bf16[64,3072]{1,0:T(8,128)(2,1)}, bf16[64,3072]{1,0:T(8,128)(2,1)S(1)}, u32[]{:S(2)}, u32[]{:S(2)}) collective-permute-start(bf16[64,3072]{1,0:T(8,128)(2,1)} %refs_3_.9), channel_id=1, source_target_pairs={{0,4},{1,5},{2,6},{3,7},{4,0},{5,1},{6,2},{7,3},{8,12},{9,13},{10,... | collective-permute-start | bytes 1179656 | tf_op jit(solution)/shard_map/ppermute | solution.py:14
  17.5 6.9 %collective-permute-start.6 = (bf16[128,1536]{1,0:T(8,128)(2,1)S(1)}, bf16[128,1536]{1,0:T(8,128)(2,1)S(1)}, u32[]{:S(2)}, u32[]{:S(2)}) collective-permute-start(bf16[128,1536]{1,0:T(8,128)(2,1)S(1)} %get-tuple-element.37.refs_4_), channel_id=1, source_target_pairs={{0,8},{8,0},{16,24},{24,16},{1,9},{9,1},{17,25},{25,17},{2,10},{10... | collective-permute-start | bytes 1179656 | tf_op jit(solution)/shard_map/ppermute | solution.py:14
  22.0 8.3 %collective-permute-start.5 = (bf16[128,1536]{1,0:T(8,128)(2,1)S(1)}, bf16[128,1536]{1,0:T(8,128)(2,1)S(1)}, u32[]{:S(2)}, u32[]{:S(2)}) collective-permute-start(bf16[128,1536]{1,0:T(8,128)(2,1)S(1)} %get-tuple-element.38.refs_1_), channel_id=1, source_target_pairs={{0,8},{8,0},{16,24},{24,16},{1,9},{9,1},{17,25},{25,17},{2,10},{10... | collective-permute-start | bytes 1179656 | tf_op jit(solution)/shard_map/ppermute | solution.py:14
  22.6 12.3 %collective-permute-start.4 = (bf16[64,3072]{1,0:T(8,128)(2,1)S(1)}, bf16[64,3072]{1,0:T(8,128)(2,1)S(1)}, u32[]{:S(2)}, u32[]{:S(2)}) collective-permute-start(bf16[64,3072]{1,0:T(8,128)(2,1)S(1)} %get-tuple-element.39.refs_1_.refs_4_.refs_5_), channel_id=1, source_target_pairs={{0,1},{1,0},{2,3},{3,2},{4,5},{5,4},{6,7},{7,6},{8,9},{9,8},{10,11... | collective-permute-start | bytes 1179656 | tf_op jit(solution)/shard_map/ppermute | solution.py:14
  28.8 19.8 %collective-permute-start.9 = (bf16[128,1536]{1,0:T(8,128)(2,1)S(1)}, bf16[128,1536]{1,0:T(8,128)(2,1)S(1)}, u32[]{:S(2)}, u32[]{:S(2)}) collective-permute-start(bf16[128,1536]{1,0:T(8,128)(2,1)S(1)} %get-tuple-element.42.refs_5_), channel_id=1, source_target_pairs={{0,16},{8,24},{16,0},{24,8},{1,17},{9,25},{17,1},{25,9},{2,18},{10... | collective-permute-start | bytes 1179656 | tf_op jit(solution)/shard_map/ppermute | solution.py:14
  36.3 7.7 %collective-permute-start.10 = (bf16[128,1536]{1,0:T(8,128)(2,1)S(1)}, bf16[128,1536]{1,0:T(8,128)(2,1)S(1)}, u32[]{:S(2)}, u32[]{:S(2)}) collective-permute-start(bf16[128,1536]{1,0:T(8,128)(2,1)S(1)} %shard_map.82.refs_2_), channel_id=1, source_target_pairs={{0,8},{8,0},{16,24},{24,16},{1,9},{9,1},{17,25},{25,17},{2,10},{10... | collective-permute-start | bytes 1179656 | tf_op jit(solution)/shard_map/ppermute | solution.py:14
  42.0 18.2 %collective-permute-start.7 = (bf16[128,3072]{1,0:T(8,128)(2,1)S(1)}, bf16[128,3072]{1,0:T(8,128)(2,1)S(1)}, u32[]{:S(2)}, u32[]{:S(2)}) collective-permute-start(bf16[128,3072]{1,0:T(8,128)(2,1)S(1)} %shard_map.83.refs_4_.refs_1_.refs_6_.refs_7_), channel_id=1, source_target_pairs={{0,1},{1,0},{2,3},{3,2},{4,5},{5,4},{6,7},{7,6},{8,9},{9,8},{10,11... | collective-permute-start | bytes 2359304 | tf_op jit(solution)/shard_map/ppermute | solution.py:14
  46.9 14.3 %collective-permute-start.11 = (bf16[128,1536]{1,0:T(8,128)(2,1)S(1)}, bf16[128,1536]{1,0:T(8,128)(2,1)S(1)}, u32[]{:S(2)}, u32[]{:S(2)}) collective-permute-start(bf16[128,1536]{1,0:T(8,128)(2,1)S(1)} %shard_map.85.refs_3_), channel_id=1, source_target_pairs={{0,16},{8,24},{16,0},{24,8},{1,17},{9,25},{17,1},{25,9},{2,18},{10... | collective-permute-start | bytes 1179656 | tf_op jit(solution)/shard_map/ppermute | solution.py:14
  54.6 23.1 %collective-permute-start.18 = (bf16[128,1536]{1,0:T(8,128)(2,1)S(1)}, bf16[128,1536]{1,0:T(8,128)(2,1)S(1)}, u32[]{:S(2)}, u32[]{:S(2)}) collective-permute-start(bf16[128,1536]{1,0:T(8,128)(2,1)S(1)} %shard_map.90.refs_4_), channel_id=1, source_target_pairs={{0,16},{8,24},{16,0},{24,8},{1,17},{9,25},{17,1},{25,9},{2,18},{10... | collective-permute-start | bytes 1179656 | tf_op jit(solution)/shard_map/ppermute | solution.py:14
  65.8 5.9 %collective-permute-start.19 = (f32[256,128]{1,0:T(8,128)S(1)}, f32[256,128]{1,0:T(8,128)S(1)}, u32[]{:S(2)}, u32[]{:S(2)}) collective-permute-start(f32[256,128]{1,0:T(8,128)S(1)} %shard_map.96.refs_4_.refs_0_), channel_id=1, source_target_pairs={{0,16},{8,24},{16,0},{24,8},{1,17},{9,25},{17,1},{25,9},{2,18},{10... | collective-permute-start | bytes 393224 | tf_op jit(solution)/shard_map/ppermute | solution.py:14
  71.8 6.8 %collective-permute-start.22 = (bf16[256,128]{1,0:T(8,128)(2,1)S(1)}, bf16[256,128]{1,0:T(8,128)(2,1)S(1)}, u32[]{:S(2)}, u32[]{:S(2)}) collective-permute-start(bf16[256,128]{1,0:T(8,128)(2,1)S(1)} %shard_map.100.refs_6_.refs_1_), channel_id=1, source_target_pairs={{0,6},{1,7},{2,4},{3,5},{4,2},{5,3},{6,0},{7,1},{8,14},{9,15},{10,... | collective-permute-start | bytes 196616 | tf_op jit(solution)/shard_map/ppermute | solution.py:14
  74.2 6.0 %collective-permute-start.21 = (bf16[256,128]{1,0:T(8,128)(2,1)S(1)}, bf16[256,128]{1,0:T(8,128)(2,1)S(1)}, u32[]{:S(2)}, u32[]{:S(2)}) collective-permute-start(bf16[256,128]{1,0:T(8,128)(2,1)S(1)} %shard_map.100.refs_6_.refs_1_), channel_id=1, source_target_pairs={{0,4},{1,5},{2,6},{3,7},{4,0},{5,1},{6,2},{7,3},{8,12},{9,13},{10,... | collective-permute-start | bytes 196616 | tf_op jit(solution)/shard_map/ppermute | solution.py:14
  74.2 6.0 %collective-permute-start.20 = (bf16[256,128]{1,0:T(8,128)(2,1)S(1)}, bf16[256,128]{1,0:T(8,128)(2,1)S(1)}, u32[]{:S(2)}, u32[]{:S(2)}) collective-permute-start(bf16[256,128]{1,0:T(8,128)(2,1)S(1)} %shard_map.100.refs_6_.refs_1_), channel_id=1, source_target_pairs={{0,2},{1,3},{2,0},{3,1},{4,6},{5,7},{6,4},{7,5},{8,10},{9,11},{10,... | collective-permute-start | bytes 196616 | tf_op jit(solution)/shard_map/ppermute | solution.py:14
  76.2 12.7 %collective-permute-start.17 = (bf16[128,1536]{1,0:T(8,128)(2,1)S(1)}, bf16[128,1536]{1,0:T(8,128)(2,1)S(1)}, u32[]{:S(2)}, u32[]{:S(2)}) collective-permute-start(bf16[128,1536]{1,0:T(8,128)(2,1)S(1)} %get-tuple-element.53), channel_id=1, source_target_pairs={{0,16},{8,24},{16,0},{24,8},{1,17},{9,25},{17,1},{25,9},{2,18},{10... | collective-permute-start | bytes 1179656 | tf_op jit(solution)/shard_map/ppermute | solution.py:14
  80.2 8.2 %collective-permute-start.24 = (bf16[3,256,128]{2,1,0:T(8,128)(2,1)S(1)}, bf16[3,256,128]{2,1,0:T(8,128)(2,1)S(1)}, u32[]{:S(2)}, u32[]{:S(2)}) collective-permute-start(bf16[3,256,128]{2,1,0:T(8,128)(2,1)S(1)} %shard_map.102.refs_7_.refs_2_), channel_id=1, source_target_pairs={{0,1},{1,0},{2,3},{3,2},{4,5},{5,4},{6,7},{7,6},{8,9},{9,8},{10,11... | collective-permute-start | bytes 589832 | tf_op jit(solution)/shard_map/ppermute | solution.py:14
  80.7 7.6 %collective-permute-start.23 = (bf16[256,128]{1,0:T(8,128)(2,1)S(1)}, bf16[256,128]{1,0:T(8,128)(2,1)S(1)}, u32[]{:S(2)}, u32[]{:S(2)}) collective-permute-start(bf16[256,128]{1,0:T(8,128)(2,1)S(1)} %shard_map.100.refs_6_.refs_1_), channel_id=1, source_target_pairs={{0,1},{1,0},{2,3},{3,2},{4,5},{5,4},{6,7},{7,6},{8,9},{9,8},{10,11... | collective-permute-start | bytes 196616 | tf_op jit(solution)/shard_map/ppermute | solution.py:14
  82.3 7.5 %collective-permute-start.25 = (bf16[256,128]{1,0:T(8,128)(2,1)S(1)}, bf16[256,128]{1,0:T(8,128)(2,1)S(1)}, u32[]{:S(2)}, u32[]{:S(2)}) collective-permute-start(bf16[256,128]{1,0:T(8,128)(2,1)S(1)} %shard_map.100.refs_6_.refs_1_), channel_id=1, source_target_pairs={{0,8},{8,0},{16,24},{24,16},{1,9},{9,1},{17,25},{25,17},{2,10},{10... | collective-permute-start | bytes 196616 | tf_op jit(solution)/shard_map/ppermute | solution.py:14
  82.3 7.5 %collective-permute-start.26 = (bf16[3,256,128]{2,1,0:T(8,128)(2,1)S(1)}, bf16[3,256,128]{2,1,0:T(8,128)(2,1)S(1)}, u32[]{:S(2)}, u32[]{:S(2)}) collective-permute-start(bf16[3,256,128]{2,1,0:T(8,128)(2,1)S(1)} %shard_map.102.refs_7_.refs_2_), channel_id=1, source_target_pairs={{0,8},{8,0},{16,24},{24,16},{1,9},{9,1},{17,25},{25,17},{2,10},{10... | collective-permute-start | bytes 589832 | tf_op jit(solution)/shard_map/ppermute | solution.py:14
  97.1 8.4 %collective-permute-start.30 = (bf16[4,256,128]{2,1,0:T(8,128)(2,1)S(1)}, bf16[4,256,128]{2,1,0:T(8,128)(2,1)S(1)}, u32[]{:S(2)}, u32[]{:S(2)}) collective-permute-start(bf16[4,256,128]{2,1,0:T(8,128)(2,1)S(1)} %get-tuple-element.65), channel_id=1, source_target_pairs={{0,1},{1,0},{2,3},{3,2},{4,5},{5,4},{6,7},{7,6},{8,9},{9,8},{10,11... | collective-permute-start | bytes 786440 | tf_op jit(solution)/shard_map/ppermute | solution.py:14
  105.6 7.5 %collective-permute-start.32 = (bf16[256,128]{1,0:T(8,128)(2,1)S(1)}, bf16[256,128]{1,0:T(8,128)(2,1)S(1)}, u32[]{:S(2)}, u32[]{:S(2)}) collective-permute-start(bf16[256,128]{1,0:T(8,128)(2,1)S(1)} %get-tuple-element.69), channel_id=1, source_target_pairs={{0,4},{1,5},{2,6},{3,7},{4,0},{5,1},{6,2},{7,3},{8,12},{9,13},{10,... | collective-permute-start | bytes 196616 | tf_op jit(solution)/shard_map/ppermute | solution.py:14
  108.5 6.1 %collective-permute-start.33 = (bf16[256,128]{1,0:T(8,128)(2,1)S(1)}, bf16[256,128]{1,0:T(8,128)(2,1)S(1)}, u32[]{:S(2)}, u32[]{:S(2)}) collective-permute-start(bf16[256,128]{1,0:T(8,128)(2,1)S(1)} %get-tuple-element.70), channel_id=1, source_target_pairs={{0,6},{1,7},{2,4},{3,5},{4,2},{5,3},{6,0},{7,1},{8,14},{9,15},{10,... | collective-permute-start | bytes 196616 | tf_op jit(solution)/shard_map/ppermute | solution.py:14
  (30 other events, 144.0 us)
